TPU v7x, 32 devices: a whole 2x2x4 slice. The times are simulated.
32 devices in a mesh: dp: 2 (over core), seq: 16 (over z, y, x).
Axes of the slice: x: 2, y: 2, z: 4, core: 2. Of those that a mesh axis runs over, the one named last changes fastest.
Arguments:
- queries: bfloat16 [2, 2048, 1024], P('dp', 'seq'), may hold values from -5 to 5
- keys: bfloat16 [2, 2048, 1024], P('dp', 'seq'), may hold values from -5 to 5
- values: bfloat16 [2, 2048, 1024], P('dp', 'seq'), may hold values from -6 to 6
- out_grad: bfloat16 [2, 2048, 1024], P('dp', 'seq'), may hold values from -6 to 6
- out_weight: bfloat16 [1024, 1024], P('dp'), may hold values from -0.1875 to 0.1875
- band_width: int32 [4], replicated, may hold values from 1 to 4, as said below
- col_reach: int32 [4], replicated, may hold values from 2 to 4, as said below
Outputs:
- query_grad: bfloat16 [2, 2048, 1024], P('dp', 'seq')
- key_grad: bfloat16 [2, 2048, 1024], P('dp', 'seq')
- value_grad: bfloat16 [2, 2048, 1024], P('dp', 'seq')
- weight_grad: bfloat16 [1024, 1024], P('dp')
Inputs may be any that keep to these rules, and one draw needn't show every extreme that they name: `band_width`: some band head has width exactly 4. `col_reach`: some strided head reaches all 4 rows.
All inputs are finite; a program needn't handle non-finite values.
Results may differ from a plain program's by a relative error of at most 0.019.
Values may be sent and summed in bfloat16 or wider, within the bound.
No kernel may reach another device: no remote copies, remote signals or barrier semaphores. Data moves between devices by JAX's collectives and lax.ppermute only.
A program may use at most 64 MiB of HBM per device.

v0:
```python
import jax
import jax.numpy as jnp
from jax import lax
from jax.sharding import PartitionSpec as P

HD = 128
HB = 4
HS = 4
IMW = 512
BLK = 128
WMAX = 4


def from_behind(value, axis, steps):
    count = lax.axis_size(axis)
    leading, last = (max(0, -steps), min(count, count - steps))
    return lax.ppermute(value, axis, [(source, source + steps) for source in range(leading, last)])


def attend(query_g, key_g, value_g, grad_g, allowed):
    scale = query_g.shape[-1] ** (-0.5)
    scores = jnp.einsum("gqd,gkd->gqk", query_g, key_g, preferred_element_type=jnp.float32) * scale
    scores = jnp.where(allowed, scores, -1e30)
    peak = jnp.max(scores, axis=-1, keepdims=True)
    raised = jnp.where(allowed, jnp.exp(scores - peak), 0.0)
    probs = raised / jnp.sum(raised, axis=-1, keepdims=True)
    probs_low = probs.astype(jnp.bfloat16)
    output = jnp.einsum(
        "gqk,gkd->gqd", probs_low, value_g, preferred_element_type=jnp.float32
    ).astype(jnp.bfloat16)
    delta = jnp.sum(grad_g.astype(jnp.float32) * output.astype(jnp.float32), axis=-1, keepdims=True)
    dprobs = jnp.einsum("gqd,gkd->gqk", grad_g, value_g, preferred_element_type=jnp.float32)
    dscores = (probs * (dprobs - delta)).astype(jnp.bfloat16)
    d_query = jnp.einsum("gqk,gkd->gqd", dscores, key_g, preferred_element_type=jnp.float32) * scale
    d_key = jnp.einsum("gqk,gqd->gkd", dscores, query_g, preferred_element_type=jnp.float32) * scale
    d_value = jnp.einsum("gqk,gqd->gkd", probs_low, grad_g, preferred_element_type=jnp.float32)
    return (output, d_query, d_key, d_value)


def band_mask(q_pos, k_pos, width):
    lower = (q_pos // BLK)[None, :, None] - width[:, None, None]
    causal = k_pos[None, None, :] <= q_pos[None, :, None]
    inside = k_pos[None, None, :] >= 0
    return causal & inside & ((k_pos // BLK)[None, None, :] >= lower)


def column_mask(count, reach):
    row_q = jnp.arange(count, dtype=jnp.int32)[None, :, None]
    row_k = jnp.arange(count, dtype=jnp.int32)[None, None, :]
    return (row_k <= row_q) & (row_q - row_k < reach[:, None, None])


def column_local(field, reach, devices):
    per_dev = IMW // devices
    count = field.shape[1] // per_dev
    grid = (
        field.reshape(4, count, per_dev, HS, HD)
        .transpose(0, 2, 3, 1, 4)
        .reshape(4, per_dev * HS, count, HD)
    )
    allowed = jnp.tile(column_mask(count, reach), (per_dev, 1, 1))
    output, d_query, d_key, d_value = attend(grid[0], grid[1], grid[2], grid[3], allowed)
    stacked = jnp.stack(
        [
            output,
            d_query.astype(jnp.bfloat16),
            d_key.astype(jnp.bfloat16),
            d_value.astype(jnp.bfloat16),
        ]
    )
    stacked = stacked.reshape(4, per_dev, HS, count, HD).transpose(0, 3, 1, 2, 4)
    return stacked.reshape(4, count * per_dev, 1, HS, HD)


def heads_first(field, count):
    return field.reshape(count, HB, HD).transpose(1, 0, 2)


def rows_first(field, count):
    return field.transpose(1, 0, 2).reshape(count, HB * HD)


def body(queries, keys, values, out_grad, out_weight, band_width, col_reach):
    query_all = queries[0]
    key_all = keys[0]
    value_all = values[0]
    grad_out = out_grad[0]
    rows = query_all.shape[0]
    devices = lax.axis_size("seq")
    place = lax.axis_index("seq")
    band_dim = HB * HD
    att_grad = jnp.einsum(
        "to,ao->ta",
        grad_out,
        lax.all_gather(out_weight, "dp", axis=0, tiled=True),
        preferred_element_type=jnp.float32,
    ).astype(jnp.bfloat16)
    strided = jnp.stack(
        [
            query_all[:, band_dim:],
            key_all[:, band_dim:],
            value_all[:, band_dim:],
            att_grad[:, band_dim:],
        ]
    )
    strided = strided.reshape(4, rows // devices, devices, HS, HD)
    column_major = lax.all_to_all(strided, "seq", split_axis=2, concat_axis=1, tiled=True)
    column_result = column_local(column_major, col_reach, devices)
    row_major = lax.all_to_all(
        column_result, "seq", split_axis=1, concat_axis=2, tiled=True
    ).reshape(4, rows, HS * HD)
    kv_own = (key_all[:, :band_dim], value_all[:, :band_dim])
    reach_dev = -(-(WMAX * BLK) // rows)
    earlier = []
    for hop in range(reach_dev, 0, -1):
        earlier.append(from_behind((kv_own[0], kv_own[1]), "seq", hop))
    key_window = jnp.concatenate([pair[0] for pair in earlier] + [kv_own[0]], 0)
    value_window = jnp.concatenate([pair[1] for pair in earlier] + [kv_own[1]], 0)
    width_all = (reach_dev + 1) * rows
    q_pos = place * rows + jnp.arange(rows, dtype=jnp.int32)
    k_pos = (place - reach_dev) * rows + jnp.arange(width_all, dtype=jnp.int32)
    allowed = band_mask(q_pos, k_pos, band_width)
    band_query = heads_first(query_all[:, :band_dim], rows)
    band_grad = heads_first(att_grad[:, :band_dim], rows)
    band_out, band_dq, band_dk, band_dv = attend(
        band_query,
        heads_first(key_window, width_all),
        heads_first(value_window, width_all),
        band_grad,
        allowed,
    )
    key_rows = rows_first(band_dk, width_all)
    value_rows = rows_first(band_dv, width_all)
    key_total = key_rows[reach_dev * rows :]
    value_total = value_rows[reach_dev * rows :]
    for hop in range(1, reach_dev + 1):
        slot = (reach_dev - hop) * rows
        returned = (
            from_behind(key_rows[slot : slot + rows].astype(jnp.bfloat16), "seq", -hop).astype(
                jnp.float32
            ),
            from_behind(value_rows[slot : slot + rows].astype(jnp.bfloat16), "seq", -hop).astype(
                jnp.float32
            ),
        )
        key_total = key_total + returned[0]
        value_total = value_total + returned[1]
    attn_out = jnp.concatenate([rows_first(band_out, rows), row_major[0]], 1)
    query_grad = jnp.concatenate([rows_first(band_dq, rows).astype(jnp.bfloat16), row_major[1]], 1)
    key_grad = jnp.concatenate([key_total.astype(jnp.bfloat16), row_major[2]], 1)
    value_grad = jnp.concatenate([value_total.astype(jnp.bfloat16), row_major[3]], 1)
    shared = lax.psum_scatter(
        jnp.einsum("ta,to->ao", attn_out, grad_out, preferred_element_type=jnp.float32).astype(
            jnp.bfloat16
        ),
        "dp",
        scatter_dimension=0,
        tiled=True,
    ).astype(jnp.float32)
    weight_grad = lax.psum(shared, "seq")
    return (query_grad[None], key_grad[None], value_grad[None], weight_grad.astype(jnp.bfloat16))


def solution(mesh):
    return jax.shard_map(
        body,
        mesh=mesh,
        in_specs=(
            P("dp", "seq", None),
            P("dp", "seq", None),
            P("dp", "seq", None),
            P("dp", "seq", None),
            P("dp", None),
            P(),
            P(),
        ),
        out_specs=(P("dp", "seq", None), P("dp", "seq", None), P("dp", "seq", None), P("dp", None)),
        check_vma=False,
    )
```

profile of v0, /device:TPU:0, one launch (start us, length us, event | category | flops | bytes accessed | tf_op | source)
XLA Modules:
  0.0 235.7 jit_solution(11305797614252872399)
XLA Ops:
  7.2 0.7 all-gather.2.cloned.1.call-update
  7.9 1.1 copy.301
  9.1 4.8 %collective-permute-start.3 = (bf16[128,512]{0,1:T(8,128)(2,1)S(1)}, bf16[128,512]{0,1:T(8,128)(2,1)S(1)}, u32[]{:S(2)}, u32[]{:S(2)}) collective-permute-start(bf16[128,512]{0,1:T(8,128)(2,1)S(1)} %slice.136), channel_id=1, source_target_pairs={{0,1},{1,2},{2,3},{3,4},{4,5},{5,6},{6,7},{7,8},{8,9},{9,10},{10,1... | collective-permute-start | bytes 393224 | tf_op jit(solution)/shard_map/ppermute | solution.py:17
  13.9 3.4 %collective-permute-start.2 = (bf16[128,512]{0,1:T(8,128)(2,1)S(1)}, bf16[128,512]{0,1:T(8,128)(2,1)S(1)}, u32[]{:S(2)}, u32[]{:S(2)}) collective-permute-start(bf16[128,512]{0,1:T(8,128)(2,1)S(1)} %slice.136), channel_id=1, source_target_pairs={{0,2},{1,3},{2,4},{3,5},{4,6},{5,7},{6,8},{7,9},{8,10},{9,11},{10,... | collective-permute-start | bytes 393224 | tf_op jit(solution)/shard_map/ppermute | solution.py:17
  17.4 4.4 %collective-permute-start.1 = (bf16[128,512]{0,1:T(8,128)(2,1)S(1)}, bf16[128,512]{0,1:T(8,128)(2,1)S(1)}, u32[]{:S(2)}, u32[]{:S(2)}) collective-permute-start(bf16[128,512]{0,1:T(8,128)(2,1)S(1)} %slice.136), channel_id=1, source_target_pairs={{0,3},{1,4},{2,5},{3,6},{4,7},{5,8},{6,9},{7,10},{8,11},{9,12},{10... | collective-permute-start | bytes 393224 | tf_op jit(solution)/shard_map/ppermute | solution.py:17
  21.9 3.5 %collective-permute-start.5 = (bf16[128,512]{0,1:T(8,128)(2,1)S(1)}, bf16[128,512]{0,1:T(8,128)(2,1)S(1)}, u32[]{:S(2)}, u32[]{:S(2)}) collective-permute-start(bf16[128,512]{0,1:T(8,128)(2,1)S(1)} %slice.139), channel_id=1, source_target_pairs={{0,3},{1,4},{2,5},{3,6},{4,7},{5,8},{6,9},{7,10},{8,11},{9,12},{10... | collective-permute-start | bytes 393224 | tf_op jit(solution)/shard_map/ppermute | solution.py:17
  25.4 3.5 %collective-permute-start.4 = (bf16[128,512]{0,1:T(8,128)(2,1)S(1)}, bf16[128,512]{0,1:T(8,128)(2,1)S(1)}, u32[]{:S(2)}, u32[]{:S(2)}) collective-permute-start(bf16[128,512]{0,1:T(8,128)(2,1)S(1)} %slice.139), channel_id=1, source_target_pairs={{0,4},{1,5},{2,6},{3,7},{4,8},{5,9},{6,10},{7,11},{8,12},{9,13},{1... | collective-permute-start | bytes 393224 | tf_op jit(solution)/shard_map/ppermute | solution.py:17
  29.3 2.1 collective-permute-done.4
  31.4 3.4 %collective-permute-start.6 = (bf16[128,512]{0,1:T(8,128)(2,1)S(1)}, bf16[128,512]{0,1:T(8,128)(2,1)S(1)}, u32[]{:S(2)}, u32[]{:S(2)}) collective-permute-start(bf16[128,512]{0,1:T(8,128)(2,1)S(1)} %slice.139), channel_id=1, source_target_pairs={{0,2},{1,3},{2,4},{3,5},{4,6},{5,7},{6,8},{7,9},{8,10},{9,11},{10,... | collective-permute-start | bytes 393224 | tf_op jit(solution)/shard_map/ppermute | solution.py:17
  34.9 2.7 %collective-permute-start.7 = (bf16[128,512]{0,1:T(8,128)(2,1)S(1)}, bf16[128,512]{0,1:T(8,128)(2,1)S(1)}, u32[]{:S(2)}, u32[]{:S(2)}) collective-permute-start(bf16[128,512]{0,1:T(8,128)(2,1)S(1)} %slice.139), channel_id=1, source_target_pairs={{0,1},{1,2},{2,3},{3,4},{4,5},{5,6},{6,7},{7,8},{8,9},{9,10},{10,1... | collective-permute-start | bytes 393224 | tf_op jit(solution)/shard_map/ppermute | solution.py:17
  37.6 6.0 %collective-permute-start = (bf16[128,512]{0,1:T(8,128)(2,1)S(1)}, bf16[128,512]{0,1:T(8,128)(2,1)S(1)}, u32[]{:S(2)}, u32[]{:S(2)}) collective-permute-start(bf16[128,512]{0,1:T(8,128)(2,1)S(1)} %slice.136), channel_id=1, source_target_pairs={{0,4},{1,5},{2,6},{3,7},{4,8},{5,9},{6,10},{7,11},{8,12},{9,13},{1... | collective-permute-start | bytes 393224 | tf_op jit(solution)/shard_map/ppermute | solution.py:17
  43.8 2.4 collective-permute-done
  46.7 2.4 %convolution_convert_fusion.1 = bf16[128,1024]{1,0:T(8,128)(2,1)S(1)} fusion(bf16[1024,1024]{1,0:T(8,128)(2,1)} %all-gather.2.cloned.1.call-done, bf16[1,128,1024]{2,1,0:T(8,128)(2,1)S(1)} %copy-done), kind=kOutput, calls=%fused_computation.16 | convolution fusion | flops 268566528 | bytes 2621440 | tf_op jit(solution)/shard_map/to,ao->ta/dot_general | solution.py:92
  49.2 0.5 pad_maximum_fusion
  49.7 1.0 copy.317
  50.7 6.0 %all-to-all-start = ((bf16[4,8,16,4,128]{4,3,1,0,2:T(4,128)(2,1)}), bf16[4,8,16,4,128]{4,3,1,0,2:T(4,128)(2,1)S(1)}, u32[]{:S(2)}, u32[]{:S(2)}) async-start(bf16[4,8,16,4,128]{4,3,1,0,2:T(4,128)(2,1)} %copy.317), calls=%async_computation | async-start | bytes 1048576 | tf_op jit(solution)/shard_map/all_to_all | solution.py:107
  56.9 0.2 tile.10
  57.3 10.4 %all-to-all-done = bf16[4,8,16,4,128]{4,3,1,0,2:T(4,128)(2,1)S(1)} async-done(((bf16[4,8,16,4,128]{4,3,1,0,2:T(4,128)(2,1)}), bf16[4,8,16,4,128]{4,3,1,0,2:T(4,128)(2,1)S(1)}, u32[]{:S(2)}, u32[]{:S(2)}) %all-to-all-start) | async-done | bytes 524320 | tf_op jit(solution)/shard_map/all_to_all | solution.py:107
  68.2 0.3 fusion.68
  68.8 0.3 convolution_convert_fusion.2
  69.1 0.4 multiply_reduce_fusion
  69.6 0.3 fusion.69
  70.3 0.4 fusion.10
  70.6 0.3 fusion.11
  71.2 1.2 copy.334
  72.4 4.0 %all-to-all-start.1 = ((bf16[4,128,1,4,128]{4,3,0,2,1:T(4,128)(2,1)}), bf16[4,128,1,4,128]{4,3,0,2,1:T(4,128)(2,1)S(1)}, u32[]{:S(2)}, u32[]{:S(2)}) async-start(bf16[4,128,1,4,128]{4,3,0,2,1:T(4,128)(2,1)} %copy.334), calls=%async_computation.1 | async-start | bytes 1048576 | tf_op jit(solution)/shard_map/all_to_all | solution.py:109
  76.6 0.2 compare_and_fusion.1
  76.8 0.3 copy.302
  77.1 2.0 fusion.61
  79.2 1.8 multiply_reduce_fusion.1
  81.1 6.3 %all-to-all-done.1 = bf16[4,128,1,4,128]{4,3,0,2,1:T(4,128)(2,1)S(1)} async-done(((bf16[4,128,1,4,128]{4,3,0,2,1:T(4,128)(2,1)}), bf16[4,128,1,4,128]{4,3,0,2,1:T(4,128)(2,1)S(1)}, u32[]{:S(2)}, u32[]{:S(2)}) %all-to-all-start.1) | async-done | bytes 524320 | tf_op jit(solution)/shard_map/all_to_all | solution.py:109
  87.5 0.7 fusion.57
  88.5 2.0 convolution_convert_fusion
  90.6 0.2 all-reduce.2.cloned.1.call-start
  90.8 0.3 copy.307
  91.2 1.7 fusion.9
  92.8 0.3 fusion.12
  93.3 2.8 %fusion.67 = (bf16[640,4,128]{0,2,1:T(8,128)(2,1)S(1)}, f32[640,4,128]{0,2,1:T(8,128)}) fusion(bf16[16,4,8,128]{3,2,1,0:T(8,128)(2,1)S(1)} %get-tuple-element.44, f32[4,128,640]{1,2,0:T(8,128)} %get-tuple-element.57, f32[4,128]{1,0:T(4,128)S(1)} %get-tuple-element.56), kind=kOutput, calls=%fused_computation.112 | convolution fusion | flops 84869120 | bytes 3409920 | tf_op jit(solution)/shard_map/gqk,gqd->gkd/dot_general | solution.py:36
  96.2 0.8 copy.350
  97.0 0.8 copy.354
  97.8 0.8 copy.353
  98.5 0.8 copy.352
  99.3 1.3 collective-permute-start.13
  100.6 1.3 collective-permute-start.14
  101.9 1.3 collective-permute-start.15
  103.2 1.3 collective-permute-start.12
  104.5 1.0 slice.155
  105.6 0.3 fusion.66
  106.2 0.8 copy.345
  107.0 0.8 copy.344
  107.7 0.8 copy.343
  108.5 1.3 collective-permute-start.9
  110.0 1.4 collective-permute-start.10
  111.4 1.3 collective-permute-start.11
  112.7 1.3 collective-permute-start.8
  114.0 1.2 add_convert_fusion
  115.2 1.7 collective-permute-done.9
  116.9 3.6 %collective-permute-done.10 = bf16[128,512]{0,1:T(8,128)(2,1)S(1)} collective-permute-done((bf16[128,512]{0,1:T(8,128)(2,1)}, bf16[128,512]{0,1:T(8,128)(2,1)S(1)}, u32[]{:S(2)}, u32[]{:S(2)}) %collective-permute-start.10) | collective-permute-done | bytes 131104 | tf_op jit(solution)/shard_map/ppermute | solution.py:17
  120.5 7.0 %collective-permute-done.11 = bf16[128,512]{0,1:T(8,128)(2,1)S(1)} collective-permute-done((bf16[128,512]{0,1:T(8,128)(2,1)}, bf16[128,512]{0,1:T(8,128)(2,1)S(1)}, u32[]{:S(2)}, u32[]{:S(2)}) %collective-permute-start.11) | collective-permute-done | bytes 131104 | tf_op jit(solution)/shard_map/ppermute | solution.py:17
  128.2 0.9 copy.359
  129.0 0.7 maximum_bitcast_fusion
  129.8 0.7 maximum_bitcast_fusion.2
  130.5 96.5 %all-reduce.2.cloned.1.call-done = bf16[512,1024]{1,0:T(8,128)(2,1)} async-done(((bf16[512,1024]{1,0:T(8,128)(2,1)}), bf16[512,1024]{1,0:T(8,128)(2,1)}) %all-reduce.2.cloned.1.call-update) | async-done | bytes 1048592 | tf_op jit(solution)/shard_map/psum | solution.py:160
  226.9 2.3 copy.414
  (103 shorter events, 5.0 us)
Async XLA Ops:
  7.2 39.5 %copy-start = (bf16[1,128,1024]{2,1,0:T(8,128)(2,1)S(1)}, bf16[1,128,1024]{2,1,0:T(8,128)(2,1)}, u32[]{:S(2)}) copy-start(bf16[1,128,1024]{2,1,0:T(8,128)(2,1)} %param.10) | copy-start | bytes 786436
  7.2 14.6 %copy-start.3 = (bf16[1,128,1024]{2,1,0:T(8,128)(2,1)S(1)}, bf16[1,128,1024]{2,1,0:T(8,128)(2,1)}, u32[]{:S(2)}) copy-start(bf16[1,128,1024]{2,1,0:T(8,128)(2,1)} %param.9) | copy-start | bytes 786436
  7.2 21.7 %copy-start.4 = (bf16[1,128,1024]{2,1,0:T(8,128)(2,1)S(1)}, bf16[1,128,1024]{2,1,0:T(8,128)(2,1)}, u32[]{:S(2)}) copy-start(bf16[1,128,1024]{2,1,0:T(8,128)(2,1)} %param.7) | copy-start | bytes 786436
  7.2 39.5 %all-gather.2.cloned.1.call-start = ((), (), s32[]{:S(2)}) async-start(), calls=%async_computation.3 | async-start | bytes 3145728 | tf_op jit(solution)/shard_map/all_gather | solution.py:95
  9.1 37.3 %collective-permute-start.3 = (bf16[128,512]{0,1:T(8,128)(2,1)S(1)}, bf16[128,512]{0,1:T(8,128)(2,1)S(1)}, u32[]{:S(2)}, u32[]{:S(2)}) collective-permute-start(bf16[128,512]{0,1:T(8,128)(2,1)S(1)} %slice.136), channel_id=1, source_target_pairs={{0,1},{1,2},{2,3},{3,4},{4,5},{5,6},{6,7},{7,8},{8,9},{9,10},{10,1... | collective-permute-start | bytes 393224 | tf_op jit(solution)/shard_map/ppermute | solution.py:17
  13.9 32.4 %collective-permute-start.2 = (bf16[128,512]{0,1:T(8,128)(2,1)S(1)}, bf16[128,512]{0,1:T(8,128)(2,1)S(1)}, u32[]{:S(2)}, u32[]{:S(2)}) collective-permute-start(bf16[128,512]{0,1:T(8,128)(2,1)S(1)} %slice.136), channel_id=1, source_target_pairs={{0,2},{1,3},{2,4},{3,5},{4,6},{5,7},{6,8},{7,9},{8,10},{9,11},{10,... | collective-permute-start | bytes 393224 | tf_op jit(solution)/shard_map/ppermute | solution.py:17
  17.4 28.8 %collective-permute-start.1 = (bf16[128,512]{0,1:T(8,128)(2,1)S(1)}, bf16[128,512]{0,1:T(8,128)(2,1)S(1)}, u32[]{:S(2)}, u32[]{:S(2)}) collective-permute-start(bf16[128,512]{0,1:T(8,128)(2,1)S(1)} %slice.136), channel_id=1, source_target_pairs={{0,3},{1,4},{2,5},{3,6},{4,7},{5,8},{6,9},{7,10},{8,11},{9,12},{10... | collective-permute-start | bytes 393224 | tf_op jit(solution)/shard_map/ppermute | solution.py:17
  21.9 12.9 %collective-permute-start.5 = (bf16[128,512]{0,1:T(8,128)(2,1)S(1)}, bf16[128,512]{0,1:T(8,128)(2,1)S(1)}, u32[]{:S(2)}, u32[]{:S(2)}) collective-permute-start(bf16[128,512]{0,1:T(8,128)(2,1)S(1)} %slice.139), channel_id=1, source_target_pairs={{0,3},{1,4},{2,5},{3,6},{4,7},{5,8},{6,9},{7,10},{8,11},{9,12},{10... | collective-permute-start | bytes 393224 | tf_op jit(solution)/shard_map/ppermute | solution.py:17
  25.4 6.0 %collective-permute-start.4 = (bf16[128,512]{0,1:T(8,128)(2,1)S(1)}, bf16[128,512]{0,1:T(8,128)(2,1)S(1)}, u32[]{:S(2)}, u32[]{:S(2)}) collective-permute-start(bf16[128,512]{0,1:T(8,128)(2,1)S(1)} %slice.139), channel_id=1, source_target_pairs={{0,4},{1,5},{2,6},{3,7},{4,8},{5,9},{6,10},{7,11},{8,12},{9,13},{1... | collective-permute-start | bytes 393224 | tf_op jit(solution)/shard_map/ppermute | solution.py:17
  31.4 6.2 %collective-permute-start.6 = (bf16[128,512]{0,1:T(8,128)(2,1)S(1)}, bf16[128,512]{0,1:T(8,128)(2,1)S(1)}, u32[]{:S(2)}, u32[]{:S(2)}) collective-permute-start(bf16[128,512]{0,1:T(8,128)(2,1)S(1)} %slice.139), channel_id=1, source_target_pairs={{0,2},{1,3},{2,4},{3,5},{4,6},{5,7},{6,8},{7,9},{8,10},{9,11},{10,... | collective-permute-start | bytes 393224 | tf_op jit(solution)/shard_map/ppermute | solution.py:17
  34.9 8.8 %collective-permute-start.7 = (bf16[128,512]{0,1:T(8,128)(2,1)S(1)}, bf16[128,512]{0,1:T(8,128)(2,1)S(1)}, u32[]{:S(2)}, u32[]{:S(2)}) collective-permute-start(bf16[128,512]{0,1:T(8,128)(2,1)S(1)} %slice.139), channel_id=1, source_target_pairs={{0,1},{1,2},{2,3},{3,4},{4,5},{5,6},{6,7},{7,8},{8,9},{9,10},{10,1... | collective-permute-start | bytes 393224 | tf_op jit(solution)/shard_map/ppermute | solution.py:17
  37.6 8.5 %collective-permute-start = (bf16[128,512]{0,1:T(8,128)(2,1)S(1)}, bf16[128,512]{0,1:T(8,128)(2,1)S(1)}, u32[]{:S(2)}, u32[]{:S(2)}) collective-permute-start(bf16[128,512]{0,1:T(8,128)(2,1)S(1)} %slice.136), channel_id=1, source_target_pairs={{0,4},{1,5},{2,6},{3,7},{4,8},{5,9},{6,10},{7,11},{8,12},{9,13},{1... | collective-permute-start | bytes 393224 | tf_op jit(solution)/shard_map/ppermute | solution.py:17
  49.7 7.1 %copy-start.5 = (s32[4]{0:T(128)S(1)}, s32[4]{0:T(128)}, u32[]{:S(2)}) copy-start(s32[4]{0:T(128)} %param.13) | copy-start | bytes 52
  50.7 17.0 %all-to-all-start = ((bf16[4,8,16,4,128]{4,3,1,0,2:T(4,128)(2,1)}), bf16[4,8,16,4,128]{4,3,1,0,2:T(4,128)(2,1)S(1)}, u32[]{:S(2)}, u32[]{:S(2)}) async-start(bf16[4,8,16,4,128]{4,3,1,0,2:T(4,128)(2,1)} %copy.317), calls=%async_computation | async-start | bytes 1048576 | tf_op jit(solution)/shard_map/all_to_all | solution.py:107
  71.2 5.3 %copy-start.6 = (s32[4]{0:T(128)S(1)}, s32[4]{0:T(128)}, u32[]{:S(2)}) copy-start(s32[4]{0:T(128)} %param.12) | copy-start | bytes 52
  72.4 15.0 %all-to-all-start.1 = ((bf16[4,128,1,4,128]{4,3,0,2,1:T(4,128)(2,1)}), bf16[4,128,1,4,128]{4,3,0,2,1:T(4,128)(2,1)S(1)}, u32[]{:S(2)}, u32[]{:S(2)}) async-start(bf16[4,128,1,4,128]{4,3,0,2,1:T(4,128)(2,1)} %copy.334), calls=%async_computation.1 | async-start | bytes 1048576 | tf_op jit(solution)/shard_map/all_to_all | solution.py:109
  76.4 29.5 %reduce-scatter.2.cloned.1.call-start = ((), (), s32[]{:S(2)}) async-start(), calls=%async_computation.4 | async-start | bytes 3145728 | tf_op jit(solution)/shard_map/reduce_scatter | solution.py:152
  90.6 136.3 %all-reduce.2.cloned.1.call-start = ((), (), s32[]{:S(2)}) async-start(), calls=%async_computation.5 | async-start | bytes 2097152 | tf_op jit(solution)/shard_map/psum | solution.py:160
  99.3 10.7 %collective-permute-start.13 = (bf16[128,512]{1,0:T(8,128)(2,1)}, bf16[128,512]{1,0:T(8,128)(2,1)}, u32[]{:S(2)}, u32[]{:S(2)}) collective-permute-start(bf16[128,512]{1,0:T(8,128)(2,1)} %copy.352), channel_id=1, source_target_pairs={{2,0},{3,1},{4,2},{5,3},{6,4},{7,5},{8,6},{9,7},{10,8},{11,9},{12,... | collective-permute-start | bytes 393224 | tf_op jit(solution)/shard_map/ppermute | solution.py:17
  100.6 10.8 %collective-permute-start.14 = (bf16[128,512]{1,0:T(8,128)(2,1)}, bf16[128,512]{1,0:T(8,128)(2,1)}, u32[]{:S(2)}, u32[]{:S(2)}) collective-permute-start(bf16[128,512]{1,0:T(8,128)(2,1)} %copy.353), channel_id=1, source_target_pairs={{3,0},{4,1},{5,2},{6,3},{7,4},{8,5},{9,6},{10,7},{11,8},{12,9},{13... | collective-permute-start | bytes 393224 | tf_op jit(solution)/shard_map/ppermute | solution.py:17
  101.9 10.8 %collective-permute-start.15 = (bf16[128,512]{1,0:T(8,128)(2,1)}, bf16[128,512]{1,0:T(8,128)(2,1)}, u32[]{:S(2)}, u32[]{:S(2)}) collective-permute-start(bf16[128,512]{1,0:T(8,128)(2,1)} %copy.354), channel_id=1, source_target_pairs={{4,0},{5,1},{6,2},{7,3},{8,4},{9,5},{10,6},{11,7},{12,8},{13,9},{1... | collective-permute-start | bytes 393224 | tf_op jit(solution)/shard_map/ppermute | solution.py:17
  103.2 10.8 %collective-permute-start.12 = (bf16[128,512]{1,0:T(8,128)(2,1)}, bf16[128,512]{1,0:T(8,128)(2,1)}, u32[]{:S(2)}, u32[]{:S(2)}) collective-permute-start(bf16[128,512]{1,0:T(8,128)(2,1)} %copy.350), channel_id=1, source_target_pairs={{1,0},{2,1},{3,2},{4,3},{5,4},{6,5},{7,6},{8,7},{9,8},{10,9},{11,1... | collective-permute-start | bytes 393224 | tf_op jit(solution)/shard_map/ppermute | solution.py:17
  108.5 8.4 %collective-permute-start.9 = (bf16[128,512]{0,1:T(8,128)(2,1)}, bf16[128,512]{0,1:T(8,128)(2,1)S(1)}, u32[]{:S(2)}, u32[]{:S(2)}) collective-permute-start(bf16[128,512]{0,1:T(8,128)(2,1)} %bitcast.40), channel_id=1, source_target_pairs={{2,0},{3,1},{4,2},{5,3},{6,4},{7,5},{8,6},{9,7},{10,8},{11,9},{12,... | collective-permute-start | bytes 393224 | tf_op jit(solution)/shard_map/ppermute | solution.py:17
  109.8 17.8 %copy-start.2 = (bf16[1,8,16,1,4,128]{5,1,2,4,0,3:T(8,128)(2,1)S(1)}, bf16[1,8,16,1,4,128]{5,1,2,4,0,3:T(8,128)(2,1)}, u32[]{:S(2)}) copy-start(bf16[1,8,16,1,4,128]{5,1,2,4,0,3:T(8,128)(2,1)} %get-tuple-element.37) | copy-start | bytes 393220
  109.9 17.8 %copy-start.1 = (bf16[1,8,16,1,4,128]{5,1,2,4,0,3:T(8,128)(2,1)S(1)}, bf16[1,8,16,1,4,128]{5,1,2,4,0,3:T(8,128)(2,1)}, u32[]{:S(2)}) copy-start(bf16[1,8,16,1,4,128]{5,1,2,4,0,3:T(8,128)(2,1)} %get-tuple-element.38) | copy-start | bytes 393220
  110.0 10.5 %collective-permute-start.10 = (bf16[128,512]{0,1:T(8,128)(2,1)}, bf16[128,512]{0,1:T(8,128)(2,1)S(1)}, u32[]{:S(2)}, u32[]{:S(2)}) collective-permute-start(bf16[128,512]{0,1:T(8,128)(2,1)} %bitcast.41), channel_id=1, source_target_pairs={{3,0},{4,1},{5,2},{6,3},{7,4},{8,5},{9,6},{10,7},{11,8},{12,9},{13... | collective-permute-start | bytes 393224 | tf_op jit(solution)/shard_map/ppermute | solution.py:17
  111.4 16.1 %collective-permute-start.11 = (bf16[128,512]{0,1:T(8,128)(2,1)}, bf16[128,512]{0,1:T(8,128)(2,1)S(1)}, u32[]{:S(2)}, u32[]{:S(2)}) collective-permute-start(bf16[128,512]{0,1:T(8,128)(2,1)} %bitcast.42), channel_id=1, source_target_pairs={{4,0},{5,1},{6,2},{7,3},{8,4},{9,5},{10,6},{11,7},{12,8},{13,9},{1... | collective-permute-start | bytes 393224 | tf_op jit(solution)/shard_map/ppermute | solution.py:17
  112.7 14.8 %collective-permute-start.8 = (bf16[128,512]{0,1:T(8,128)(2,1)S(1)}, bf16[128,512]{0,1:T(8,128)(2,1)S(1)}, u32[]{:S(2)}, u32[]{:S(2)}) collective-permute-start(bf16[128,512]{0,1:T(8,128)(2,1)S(1)} %bitcast.209), channel_id=1, source_target_pairs={{1,0},{2,1},{3,2},{4,3},{5,4},{6,5},{7,6},{8,7},{9,8},{10,9},{11,1... | collective-permute-start | bytes 393224 | tf_op jit(solution)/shard_map/ppermute | solution.py:17
Sparse Core Ops, SparseCore 0:
  9.6 13.2 all-gather.1
  90.7 8.0 reduce-scatter.1
  106.1 120.7 all-reduce.1
where the time goes:
time: 237 us; the launch traced here: 236 us
  waiting for transfers between devices  131 us (55%)
  starting transfers between devices  52.5 us (22%)
  local copies, waits for them, and re-layouts  18.8 us (8%)
  matrix products  15.3 us (6%)
  between operations  14.7 us (6%)
  other arithmetic  3.82 us (2%)
    psum x1, waiting for transfers between devices, body(): weight_grad = lax.psum(shared, 'seq')  96.5 us
    ppermute x16, starting transfers between devices, from_behind(): lax.ppermute(value, axis, [(source, source + steps) for source in range(l...  42.1 us
    ppermute x16, waiting for transfers between devices, from_behind(): lax.ppermute(value, axis, [(source, source + steps) for source in range(l...  16.8 us
    all_to_all x1, waiting for transfers between devices, body(): lax.all_to_all(strided, 'seq', split_axis=2, concat_axis=1, tiled=True)  10.4 us
    all_to_all x1, waiting for transfers between devices, body(): lax.all_to_all(column_result, 'seq', split_axis=1, concat_axis=2, tiled=T...  6.28 us
    all_to_all x1, starting transfers between devices, body(): lax.all_to_all(strided, 'seq', split_axis=2, concat_axis=1, tiled=True)  6.02 us
    unnamed x32, local copies, waits for them, and re-layouts  4.96 us
  transfers between devices with their start and end apart: 21, of which 8 were waited for; matrix products, arithmetic and copies ran while one was open for 10% of the time, Pallas kernels for 0%

commit v1 on v0

v1 whole, which is shorter than its diff:
```python
import functools

import jax
import jax.numpy as jnp
from jax import lax
from jax.experimental import pallas as pl
from jax.experimental.pallas import tpu as pltpu
from jax.sharding import PartitionSpec as P

HD = 128
HB = 4
HS = 4
IMW = 512
BLK = 128
WMAX = 4

BF = jnp.bfloat16
F32 = jnp.float32
MIB = 1 << 20


def nn(a, b):
    return lax.dot_general(a, b, (((1,), (0,)), ((), ())), preferred_element_type=F32)


def nt(a, b):
    return lax.dot_general(a, b, (((1,), (1,)), ((), ())), preferred_element_type=F32)


def tn(a, b):
    return lax.dot_general(a, b, (((0,), (0,)), ((), ())), preferred_element_type=F32)


def rows_at(start, size):
    return pl.ds(pl.multiple_of(start, size), size)


def shaped(shape, dtype=BF):
    return jax.ShapeDtypeStruct(shape, dtype)


def call(kernel, outs, args, smem=0, scratch=(), mib=16, name=None):
    vmem = pl.BlockSpec(memory_space=pltpu.VMEM)
    scalars = pl.BlockSpec(memory_space=pltpu.SMEM)
    return pl.pallas_call(
        kernel,
        out_shape=outs,
        in_specs=[scalars] * smem + [vmem] * (len(args) - smem),
        out_specs=[vmem] * len(outs),
        scratch_shapes=list(scratch),
        compiler_params=pltpu.CompilerParams(vmem_limit_bytes=mib * MIB),
        name=name,
    )(*args)


def roles(band, strided):
    role = lax.axis_index("dp")
    pl.when(role == 0)(band)
    pl.when(role == 1)(strided)


def spot(g):
    place = lax.axis_index("seq")
    return lax.div(place, g), lax.rem(place, g)


def pack_swap_kernel(q_ref, k_ref, v_ref, out_ref):
    half = out_ref.shape[2]

    def take(start):
        for t, ref in enumerate((q_ref, k_ref, v_ref)):
            out_ref[t] = ref[:, start : start + half]

    roles(lambda: take(half), lambda: take(0))


def pack_fields_kernel(g, q_ref, k_ref, v_ref, other_ref, *out_refs):
    line, spot_ = spot(g)
    rows, half = other_ref.shape[1:]
    chunk = rows // g
    own = (q_ref, k_ref, v_ref)

    def band():
        for d in range(1, g):
            lanes = rows_at((spot_ ^ d) * HD, HD)
            for t in range(3):
                out_refs[d - 1][t * rows : (t + 1) * rows] = own[t][:, lanes]
                out_refs[d - 1][(3 + t) * rows : (4 + t) * rows] = other_ref[t, :, lanes]

    def strided():
        for d in range(1, g):
            there = rows_at((line ^ d) * chunk, chunk)
            for t in range(3):
                for h in range(HS):
                    at = t * rows + h * chunk
                    out_refs[d - 1][at : at + chunk] = own[t][there, half + h * HD : half + (h + 1) * HD]
                    at += 3 * rows
                    out_refs[d - 1][at : at + chunk] = other_ref[t, there, h * HD : (h + 1) * HD]

    roles(band, strided)


def att_grad_kernel(own_ref, other_ref, weight_ref, out_ref):
    out_ref[0] = nt(own_ref[...], weight_ref[...]).astype(BF)
    out_ref[1] = nt(other_ref[...], weight_ref[...]).astype(BF)


def strided_mask(rows, chunk, reach):
    row = lax.broadcasted_iota(jnp.int32, (rows, rows), 0)
    col = lax.broadcasted_iota(jnp.int32, (rows, rows), 1)
    apart = lax.div(row, chunk) - lax.div(col, chunk)
    same = lax.rem(row, chunk) == lax.rem(col, chunk)
    return same & (apart >= 0) & (apart < reach)


def softmax(scores, allowed):
    scores = jnp.where(allowed, scores, -1e30)
    raised = jnp.exp(scores - jnp.max(scores, axis=-1, keepdims=True))
    raised = jnp.where(allowed, raised, 0.0)
    return raised * (1.0 / jnp.sum(raised, axis=-1, keepdims=True))


def forward_kernel(g, reach_ref, q_ref, k_ref, v_ref, other_ref, att_ref, r1_ref, r2_ref, r3_ref,
                   fq_ref, fkv_ref, o1_ref, o2_ref, o3_ref, keep_ref):
    line, spot_ = spot(g)
    rows, half = other_ref.shape[1:]
    span = g * rows
    chunk = rows // g
    own = (q_ref, k_ref, v_ref)
    came = (r1_ref, r2_ref, r3_ref)
    back = (o1_ref, o2_ref, o3_ref)

    def put(i, t, start, size, value):
        if t == 0:
            fq_ref[rows_at(i * span + start, size)] = value
        else:
            fkv_ref[rows_at((i * 2 + t - 1) * span + start, size)] = value

    def band():
        lanes = rows_at(spot_ * HD, HD)
        for t in range(3):
            put(0, t, spot_ * rows, rows, own[t][:, lanes])
            put(1, t, spot_ * rows, rows, other_ref[t, :, lanes])
            for d in range(1, g):
                for i in range(2):
                    at = (i * 3 + t) * rows
                    put(i, t, (spot_ ^ d) * rows, rows, came[d - 1][at : at + rows])
        for d in range(1, g):
            lanes = rows_at((spot_ ^ d) * HD, HD)
            for i in range(2):
                back[d - 1][(2 + i) * rows : (3 + i) * rows] = att_ref[i, :, lanes]

    def strided():
        here = rows_at(line * chunk, chunk)
        for t in range(3):
            for h in range(HS):
                put(0, t, h * rows + line * chunk, chunk, own[t][here, half + h * HD : half + (h + 1) * HD])
                put(1, t, h * rows + line * chunk, chunk, other_ref[t, here, h * HD : (h + 1) * HD])
                for d in range(1, g):
                    for i in range(2):
                        at = (i * 3 + t) * rows + h * chunk
                        put(i, t, h * rows + (line ^ d) * chunk, chunk, came[d - 1][at : at + chunk])
        for i in range(2):
            for h in range(HS):
                allowed = strided_mask(rows, chunk, reach_ref[h])
                at = i * span + h * rows
                query = fq_ref[at : at + rows]
                key = fkv_ref[i * span + at : i * span + at + rows]
                value = fkv_ref[(i + 1) * span + at : (i + 1) * span + at + rows]
                probs = softmax(nt(query, key) * (HD ** (-0.5)), allowed)
                keep_ref[i, h] = nn(probs.astype(BF), value).astype(BF)
        for d in range(1, g):
            there = rows_at((line ^ d) * chunk, chunk)
            for i in range(2):
                for h in range(HS):
                    at = (i * HS + h) * chunk
                    back[d - 1][at : at + chunk] = keep_ref[i, h, there]
                    at += 2 * rows
                    back[d - 1][at : at + chunk] = att_ref[i, there, h * HD : (h + 1) * HD]

    roles(band, strided)


def heads_kernel(g, keep_ref, o1_ref, o2_ref, o3_ref, p1_ref, p2_ref, p3_ref, mine_ref):
    line, spot_ = spot(g)
    rows = keep_ref.shape[2]
    chunk = rows // g
    came = (o1_ref, o2_ref, o3_ref)
    outs = (mine_ref, p1_ref, p2_ref, p3_ref)

    def strided():
        for to in range(g):
            head = spot_ ^ to
            for i in range(2):
                outs[to][rows_at(i * rows + line * chunk, chunk)] = keep_ref[i, head, rows_at(line * chunk, chunk)]
                for d in range(1, g):
                    source = rows_at((i * HS + head) * chunk, chunk)
                    outs[to][rows_at(i * rows + (line ^ d) * chunk, chunk)] = came[d - 1][source]

    roles(lambda: None, strided)


def gradients(query, key, value, grad, probs, output):
    probs_low = probs.astype(BF)
    delta = jnp.sum(grad.astype(F32) * output.astype(F32), axis=-1, keepdims=True)
    dscores = (probs * (nt(grad, value) - delta)).astype(BF)
    scale = HD ** (-0.5)
    return nn(dscores, key) * scale, tn(dscores, query) * scale, tn(probs_low, grad)


def attention_kernel(g, width_ref, reach_ref, fq_ref, fkv_ref, halo_ref, att_ref, o1_ref, o2_ref, o3_ref,
                     out_ref, grads_ref, tail_ref, grad_s, key_s, value_s, dkey_s, dvalue_s):
    line, spot_ = spot(g)
    rows = att_ref.shape[1]
    span = g * rows
    chunk = rows // g
    came = (o1_ref, o2_ref, o3_ref)
    scale = HD ** (-0.5)

    def band():
        width = width_ref[spot_]
        row = lax.broadcasted_iota(jnp.int32, (rows, span + rows), 0)
        col = lax.broadcasted_iota(jnp.int32, (rows, span + rows), 1)
        block = lax.div(col, BLK)
        near = (block >= WMAX - width) & (col - span <= row)
        for i in range(2):
            grad_s[rows_at(spot_ * rows, rows)] = att_ref[i, :, rows_at(spot_ * HD, HD)]
            for d in range(1, g):
                grad_s[rows_at((spot_ ^ d) * rows, rows)] = came[d - 1][(2 + i) * rows : (3 + i) * rows]
            key_s[:span] = halo_ref[i * 2 * span : (i * 2 + 1) * span]
            key_s[span:] = fkv_ref[i * 2 * span : (i * 2 + 1) * span]
            value_s[:span] = halo_ref[(i * 2 + 1) * span : (i * 2 + 2) * span]
            value_s[span:] = fkv_ref[(i * 2 + 1) * span : (i * 2 + 2) * span]
            dkey_s[...] = jnp.zeros_like(dkey_s)
            dvalue_s[...] = jnp.zeros_like(dvalue_s)
            for b in range(g):
                window = slice(b * rows, b * rows + span + rows)
                mine = slice(b * rows, (b + 1) * rows)
                at = i * span + b * rows
                query, grad = fq_ref[at : at + rows], grad_s[mine]
                key, value = key_s[window], value_s[window]
                allowed = near & ((block + b >= g) | (line > 0))
                probs = softmax(nt(query, key) * scale, allowed)
                output = nn(probs.astype(BF), value).astype(BF)
                out_ref[at : at + rows] = output
                dquery, dkey, dvalue = gradients(query, key, value, grad, probs, output)
                grads_ref[i, 0, mine] = dquery
                dkey_s[window] += dkey
                dvalue_s[window] += dvalue
            grads_ref[i, 1] = dkey_s[span:]
            grads_ref[i, 2] = dvalue_s[span:]
            tail_ref[i * 2 * span : (i * 2 + 1) * span] = dkey_s[:span].astype(BF)
            tail_ref[(i * 2 + 1) * span : (i * 2 + 2) * span] = dvalue_s[:span].astype(BF)

    def strided():
        for i in range(2):
            for h in range(HS):
                own = att_ref[i, rows_at(line * chunk, chunk), h * HD : (h + 1) * HD]
                grad_s[rows_at(h * rows + line * chunk, chunk)] = own
                for d in range(1, g):
                    at = 2 * rows + (i * HS + h) * chunk
                    grad_s[rows_at(h * rows + (line ^ d) * chunk, chunk)] = came[d - 1][at : at + chunk]
            for h in range(HS):
                allowed = strided_mask(rows, chunk, reach_ref[h])
                mine = slice(h * rows, (h + 1) * rows)
                at = i * span + h * rows
                query, grad = fq_ref[at : at + rows], grad_s[mine]
                key = fkv_ref[i * span + at : i * span + at + rows]
                value = fkv_ref[(i + 1) * span + at : (i + 1) * span + at + rows]
                probs = softmax(nt(query, key) * scale, allowed)
                output = nn(probs.astype(BF), value).astype(BF)
                dquery, dkey, dvalue = gradients(query, key, value, grad, probs, output)
                grads_ref[i, 0, mine] = dquery
                grads_ref[i, 1, mine] = dkey
                grads_ref[i, 2, mine] = dvalue

    roles(band, strided)


def pack_grads_kernel(g, grads_ref, tail_ref, keep_ref, r1_ref, r2_ref, r3_ref):
    line, spot_ = spot(g)
    span = grads_ref.shape[2]
    rows = span // g
    chunk = rows // g
    outs = (keep_ref, r1_ref, r2_ref, r3_ref)

    def band():
        for d in range(g):
            block = (spot_ ^ d) * rows
            for i in range(2):
                for t in range(3):
                    total = grads_ref[i, t, rows_at(block, rows)]
                    if t:
                        total += tail_ref[rows_at((i * 2 + t - 1) * span + block, rows)].astype(F32)
                    outs[d][(i * 3 + t) * rows : (i * 3 + t + 1) * rows] = total.astype(BF)

    def strided():
        for d in range(g):
            for i in range(2):
                for t in range(3):
                    for h in range(HS):
                        at = (i * 3 + t) * rows + h * chunk
                        there = rows_at(h * rows + (line ^ d) * chunk, chunk)
                        outs[d][at : at + chunk] = grads_ref[i, t, there].astype(BF)

    roles(band, strided)


def sort_grads_kernel(g, keep_ref, r1_ref, r2_ref, r3_ref, own_ref, other_ref):
    line, spot_ = spot(g)
    rows = own_ref.shape[1]
    chunk = rows // g
    came = (keep_ref, r1_ref, r2_ref, r3_ref)

    def band():
        for d in range(g):
            lanes = rows_at((spot_ ^ d) * HD, HD)
            for t in range(3):
                own_ref[t, :, lanes] = came[d][t * rows : (t + 1) * rows]
                other_ref[t, :, lanes] = came[d][(3 + t) * rows : (4 + t) * rows]

    def strided():
        for d in range(g):
            there = rows_at((line ^ d) * chunk, chunk)
            for t in range(3):
                for h in range(HS):
                    at = t * rows + h * chunk
                    own_ref[t, there, h * HD : (h + 1) * HD] = came[d][at : at + chunk]
                    at += 3 * rows
                    other_ref[t, there, h * HD : (h + 1) * HD] = came[d][at : at + chunk]

    roles(band, strided)


def join_grads_kernel(own_ref, other_ref, dq_ref, dk_ref, dv_ref):
    half = own_ref.shape[2]

    def join(left, right):
        for t, ref in enumerate((dq_ref, dk_ref, dv_ref)):
            ref[:, :half] = left[t]
            ref[:, half:] = right[t]

    roles(lambda: join(own_ref, other_ref), lambda: join(other_ref, own_ref))


def weight_kernel(g, band_ref, mine_ref, p1_ref, p2_ref, p3_ref, og_ref, og_other_ref,
                  a1_ref, a2_ref, a3_ref, b1_ref, b2_ref, b3_ref,
                  keep_ref, z1_ref, z2_ref, z3_ref, sum_s):
    line, spot_ = spot(g)
    rows = og_ref.shape[0]
    span = g * rows
    chunk = sum_s.shape[0] // g
    outer = ((og_ref, a1_ref, a2_ref, a3_ref), (og_other_ref, b1_ref, b2_ref, b3_ref))
    heads = (mine_ref, p1_ref, p2_ref, p3_ref)

    def add(pick):
        total = None
        for i in range(2):
            for d in range(g):
                part = tn(pick(i, d), outer[i][d][...])
                total = part if total is None else total + part
        sum_s[...] = total

    roles(
        lambda: add(lambda i, d: band_ref[rows_at(i * span + (spot_ ^ d) * rows, rows)]),
        lambda: add(lambda i, d: heads[d][i * rows : (i + 1) * rows]),
    )
    keep_ref[...] = sum_s[rows_at(line * chunk, chunk)]
    for d, ref in enumerate((z1_ref, z2_ref, z3_ref), 1):
        ref[...] = sum_s[rows_at((line ^ d) * chunk, chunk)].astype(BF)


def sum_kernel(keep_ref, z1_ref, z2_ref, z3_ref, out_ref):
    total = keep_ref[...]
    for ref in (z1_ref, z2_ref, z3_ref):
        total += ref[...].astype(F32)
    out_ref[...] = total.astype(BF)


def gather_kernel(g, by_line, own_ref, g1_ref, g2_ref, g3_ref, out_ref):
    line, spot_ = spot(g)
    size = own_ref.shape[0]
    at = line if by_line else spot_
    for d, ref in enumerate((own_ref, g1_ref, g2_ref, g3_ref)):
        out_ref[rows_at((at ^ d) * size, size)] = ref[...]


def body_roles(g, queries, keys, values, out_grad, out_weight, band_width, col_reach):
    q, k, v, og = queries[0], keys[0], values[0], out_grad[0]
    rows, width = q.shape
    half = width // 2
    span = g * rows
    chunk = rows // g
    devices = lax.axis_size("seq")
    both = ("dp", "seq")

    def send(value, target):
        pairs = []
        for role in range(2):
            for line in range(g):
                for place in range(g):
                    to = target(role, line, place)
                    if to is not None and 0 <= to[0] < g:
                        pairs.append((role * devices + line * g + place, role * devices + to[0] * g + to[1]))
        return lax.ppermute(value, both, pairs)

    def swap(value):
        return lax.ppermute(value, "dp", [(0, 1), (1, 0)])

    def by_role(d):
        return lambda role, line, place: (line, place ^ d) if role == 0 else (line ^ d, place)

    def along_line(d):
        return lambda role, line, place: (line ^ d, place)

    def in_group(d):
        return lambda role, line, place: (line, place ^ d)

    def second(target):
        return lambda role, line, place: target(role, line, place) if role == 1 else None

    def shift(step):
        return lambda role, line, place: (line + step, place) if role == 0 else None

    steps = range(1, g)
    og_other = swap(og)
    (to_other,) = call(pack_swap_kernel, [shaped((3, rows, half))], [q, k, v], name="pack_swap")
    other = swap(to_other)
    fields = call(functools.partial(pack_fields_kernel, g), [shaped((6 * rows, HD))] * (g - 1),
                  [q, k, v, other], name="pack_fields")
    came = [send(fields[d - 1], by_role(d)) for d in steps]
    (att,) = call(att_grad_kernel, [shaped((2, rows, half))], [og, og_other, out_weight], name="att_grad")
    fq, fkv, *back = call(
        functools.partial(forward_kernel, g),
        [shaped((2 * span, HD)), shaped((4 * span, HD))] + [shaped((4 * rows, HD))] * (g - 1)
        + [shaped((2, HS, rows, HD))],
        [col_reach, q, k, v, other, att] + came, smem=1, name="forward",
    )
    keep = back.pop()
    back = [send(back[d - 1], by_role(d)) for d in steps]
    halo = send(fkv, shift(1))
    *to_heads, mine = call(functools.partial(heads_kernel, g), [shaped((2 * rows, HD))] * g,
                           [keep] + back, name="heads")
    heads = [send(to_heads[d - 1], second(in_group(d))) for d in steps]
    near = [send(og, in_group(d)) for d in steps]
    near_other = [swap(value) for value in near]
    band_out, grads, tail = call(
        functools.partial(attention_kernel, g),
        [shaped((2 * span, HD)), shaped((2, 3, span, HD), F32), shaped((4 * span, HD))],
        [band_width, col_reach, fq, fkv, halo, att] + back, smem=2,
        scratch=[pltpu.VMEM((span, HD), BF), pltpu.VMEM((2 * span, HD), BF), pltpu.VMEM((2 * span, HD), BF),
                 pltpu.VMEM((2 * span, HD), F32), pltpu.VMEM((2 * span, HD), F32)],
        name="attention",
    )
    piece = half // g // g
    parts = call(functools.partial(weight_kernel, g),
                 [shaped((piece, width), F32)] + [shaped((piece, width))] * (g - 1),
                 [band_out, mine] + heads + [og, og_other] + near + near_other,
                 scratch=[pltpu.VMEM((half // g, width), F32)], name="weight")
    summed = [send(parts[d], along_line(d)) for d in steps]
    (piece_sum,) = call(sum_kernel, [shaped((piece, width))], [parts[0]] + summed, name="sum")
    pieces = [send(piece_sum, along_line(d)) for d in steps]
    (head_rows,) = call(functools.partial(gather_kernel, g, True), [shaped((half // g, width))],
                        [piece_sum] + pieces, name="gather_line")
    others = [send(head_rows, in_group(d)) for d in steps]
    (weight_grad,) = call(functools.partial(gather_kernel, g, False), [shaped((half, width))],
                          [head_rows] + others, name="gather_group")
    tail = send(tail, shift(-1))
    returned = call(functools.partial(pack_grads_kernel, g), [shaped((6 * rows, HD))] * g,
                    [grads, tail], name="pack_grads")
    returned = [returned[0]] + [send(returned[d], by_role(d)) for d in steps]
    own, to_other = call(functools.partial(sort_grads_kernel, g), [shaped((3, rows, half))] * 2,
                         returned, name="sort_grads")
    dq, dk, dv = call(join_grads_kernel, [shaped((rows, width))] * 3, [own, swap(to_other)], name="join_grads")
    return dq[None], dk[None], dv[None], weight_grad


def from_behind(value, axis, steps):
    count = lax.axis_size(axis)
    leading, last = (max(0, -steps), min(count, count - steps))
    return lax.ppermute(value, axis, [(source, source + steps) for source in range(leading, last)])


def attend(query_g, key_g, value_g, grad_g, allowed):
    scale = query_g.shape[-1] ** (-0.5)
    scores = jnp.einsum("gqd,gkd->gqk", query_g, key_g, preferred_element_type=F32) * scale
    scores = jnp.where(allowed, scores, -1e30)
    peak = jnp.max(scores, axis=-1, keepdims=True)
    raised = jnp.where(allowed, jnp.exp(scores - peak), 0.0)
    probs = raised / jnp.sum(raised, axis=-1, keepdims=True)
    probs_low = probs.astype(BF)
    output = jnp.einsum("gqk,gkd->gqd", probs_low, value_g, preferred_element_type=F32).astype(BF)
    delta = jnp.sum(grad_g.astype(F32) * output.astype(F32), axis=-1, keepdims=True)
    dprobs = jnp.einsum("gqd,gkd->gqk", grad_g, value_g, preferred_element_type=F32)
    dscores = (probs * (dprobs - delta)).astype(BF)
    d_query = jnp.einsum("gqk,gkd->gqd", dscores, key_g, preferred_element_type=F32) * scale
    d_key = jnp.einsum("gqk,gqd->gkd", dscores, query_g, preferred_element_type=F32) * scale
    d_value = jnp.einsum("gqk,gqd->gkd", probs_low, grad_g, preferred_element_type=F32)
    return (output, d_query, d_key, d_value)


def band_mask(q_pos, k_pos, width):
    lower = (q_pos // BLK)[None, :, None] - width[:, None, None]
    causal = k_pos[None, None, :] <= q_pos[None, :, None]
    inside = k_pos[None, None, :] >= 0
    return causal & inside & ((k_pos // BLK)[None, None, :] >= lower)


def column_mask(count, reach):
    row_q = jnp.arange(count, dtype=jnp.int32)[None, :, None]
    row_k = jnp.arange(count, dtype=jnp.int32)[None, None, :]
    return (row_k <= row_q) & (row_q - row_k < reach[:, None, None])


def column_local(field, reach, devices):
    per_dev = IMW // devices
    count = field.shape[1] // per_dev
    grid = (
        field.reshape(4, count, per_dev, HS, HD)
        .transpose(0, 2, 3, 1, 4)
        .reshape(4, per_dev * HS, count, HD)
    )
    allowed = jnp.tile(column_mask(count, reach), (per_dev, 1, 1))
    output, d_query, d_key, d_value = attend(grid[0], grid[1], grid[2], grid[3], allowed)
    stacked = jnp.stack([output, d_query.astype(BF), d_key.astype(BF), d_value.astype(BF)])
    stacked = stacked.reshape(4, per_dev, HS, count, HD).transpose(0, 3, 1, 2, 4)
    return stacked.reshape(4, count * per_dev, 1, HS, HD)


def heads_first(field, count):
    return field.reshape(count, HB, HD).transpose(1, 0, 2)


def rows_first(field, count):
    return field.transpose(1, 0, 2).reshape(count, HB * HD)


def body_any(queries, keys, values, out_grad, out_weight, band_width, col_reach):
    query_all = queries[0]
    key_all = keys[0]
    value_all = values[0]
    grad_out = out_grad[0]
    rows = query_all.shape[0]
    devices = lax.axis_size("seq")
    place = lax.axis_index("seq")
    band_dim = HB * HD
    att_grad = jnp.einsum(
        "to,ao->ta",
        grad_out,
        lax.all_gather(out_weight, "dp", axis=0, tiled=True),
        preferred_element_type=F32,
    ).astype(BF)
    strided = jnp.stack([field[:, band_dim:] for field in (query_all, key_all, value_all, att_grad)])
    strided = strided.reshape(4, rows // devices, devices, HS, HD)
    column_major = lax.all_to_all(strided, "seq", split_axis=2, concat_axis=1, tiled=True)
    column_result = column_local(column_major, col_reach, devices)
    row_major = lax.all_to_all(
        column_result, "seq", split_axis=1, concat_axis=2, tiled=True
    ).reshape(4, rows, HS * HD)
    kv_own = (key_all[:, :band_dim], value_all[:, :band_dim])
    reach_dev = -(-(WMAX * BLK) // rows)
    earlier = []
    for hop in range(reach_dev, 0, -1):
        earlier.append(from_behind((kv_own[0], kv_own[1]), "seq", hop))
    key_window = jnp.concatenate([pair[0] for pair in earlier] + [kv_own[0]], 0)
    value_window = jnp.concatenate([pair[1] for pair in earlier] + [kv_own[1]], 0)
    width_all = (reach_dev + 1) * rows
    q_pos = place * rows + jnp.arange(rows, dtype=jnp.int32)
    k_pos = (place - reach_dev) * rows + jnp.arange(width_all, dtype=jnp.int32)
    allowed = band_mask(q_pos, k_pos, band_width)
    band_out, band_dq, band_dk, band_dv = attend(
        heads_first(query_all[:, :band_dim], rows),
        heads_first(key_window, width_all),
        heads_first(value_window, width_all),
        heads_first(att_grad[:, :band_dim], rows),
        allowed,
    )
    key_rows = rows_first(band_dk, width_all)
    value_rows = rows_first(band_dv, width_all)
    key_total = key_rows[reach_dev * rows :]
    value_total = value_rows[reach_dev * rows :]
    for hop in range(1, reach_dev + 1):
        slot = (reach_dev - hop) * rows
        key_total += from_behind(key_rows[slot : slot + rows].astype(BF), "seq", -hop).astype(F32)
        value_total += from_behind(value_rows[slot : slot + rows].astype(BF), "seq", -hop).astype(F32)
    attn_out = jnp.concatenate([rows_first(band_out, rows), row_major[0]], 1)
    query_grad = jnp.concatenate([rows_first(band_dq, rows).astype(BF), row_major[1]], 1)
    key_grad = jnp.concatenate([key_total.astype(BF), row_major[2]], 1)
    value_grad = jnp.concatenate([value_total.astype(BF), row_major[3]], 1)
    shared = lax.psum_scatter(
        jnp.einsum("ta,to->ao", attn_out, grad_out, preferred_element_type=F32).astype(BF),
        "dp",
        scatter_dimension=0,
        tiled=True,
    ).astype(F32)
    weight_grad = lax.psum(shared, "seq")
    return (query_grad[None], key_grad[None], value_grad[None], weight_grad.astype(BF))


def solution(mesh):
    def body(*args):
        rows = args[0].shape[1]
        devices = mesh.shape["seq"]
        g = IMW // rows
        fits = (
            mesh.shape["dp"] == 2
            and rows == BLK
            and devices == g * g
            and g == HB == HS == 4
            and WMAX * BLK == IMW
            and args[4].shape[0] == HB * HD == HS * HD
        )
        return body_roles(g, *args) if fits else body_any(*args)

    return jax.shard_map(
        body,
        mesh=mesh,
        in_specs=(
            P("dp", "seq", None),
            P("dp", "seq", None),
            P("dp", "seq", None),
            P("dp", "seq", None),
            P("dp", None),
            P(),
            P(),
        ),
        out_specs=(P("dp", "seq", None), P("dp", "seq", None), P("dp", "seq", None), P("dp", None)),
        check_vma=False,
    )
```

time: 237 us -> 102 us (0.43)
  waiting for transfers between devices: 131 us -> 40.4 us
  local copies, waits for them, and re-layouts: 18.8 us -> 2.88 us
  matrix products: 15.3 us -> 0 us
  between operations: 14.7 us -> 0.87 us
  Pallas kernels: 0 us -> 11.7 us
  starting transfers between devices: 52.5 us -> 46.2 us
  other arithmetic: 3.82 us -> 0 us
    psum x1 -> x0, waiting for transfers between devices: 96.5 us -> none  [body(): weight_grad = lax.psum(shared, 'seq')]
    ppermute x16 -> x32, waiting for transfers between devices: 16.8 us -> 40.4 us  [the longest x26 39.1 us: send(): return lax.ppermute(value, both, pairs)]
    all_to_all x2 -> x0, waiting for transfers between devices: 16.7 us -> none  [the longest x1 10.4 us: body(): lax.all_to_all(strided, 'seq', split_axis=2, concat_axis=1, tiled=True)]
    dot_general x13 -> x0, matrix products: 13.3 us -> none  [the longest x2 3.1 us: attend(): jnp.einsum('gqk,gqd->gkd', probs_low, grad_g, preferred_element_type=jnp....]
    pallas_call x0 -> x13, Pallas kernels: none -> 11.7 us  [call(): pl.pallas_call(kernel, out_shape=outs, in_specs=[scalars] * smem + [vmem]...]
    all_to_all x2 -> x0, starting transfers between devices: 10.1 us -> none  [the longest x1 6.02 us: body(): lax.all_to_all(strided, 'seq', split_axis=2, concat_axis=1, tiled=True)]
    slice x26 -> x0, local copies, waits for them, and re-layouts: 5.7 us -> none  [the longest x5 2.47 us: body(): key_rows[slot:slot + rows].astype(jnp.bfloat16)]
    ppermute x16 -> x32, starting transfers between devices: 42.1 us -> 46.2 us  [the longest x26 35.4 us: send(): return lax.ppermute(value, both, pairs)]
  transfers between devices with their start and end apart: 21 -> 32, of which waited for: 8 -> 14; matrix products, arithmetic and copies ran while one was open for 10% -> 0% of each run, Pallas kernels for 0% -> 3%
where the time goes in v1:
time: 102 us
  starting transfers between devices  46.2 us (45%)
  waiting for transfers between devices  40.4 us (40%)
  Pallas kernels  11.7 us (11%)
  local copies, waits for them, and re-layouts  2.88 us (3%)
    ppermute x26, waiting for transfers between devices, send(): return lax.ppermute(value, both, pairs)  39.1 us
    ppermute x26, starting transfers between devices, send(): return lax.ppermute(value, both, pairs)  35.4 us
    pallas_call x13, Pallas kernels, call(): pl.pallas_call(kernel, out_shape=outs, in_specs=[scalars] * smem + [vmem]...  11.7 us
    ppermute x6, starting transfers between devices, swap(): return lax.ppermute(value, 'dp', [(0, 1), (1, 0)])  10.7 us
    unnamed x20, local copies, waits for them, and re-layouts  2.88 us
  transfers between devices with their start and end apart: 32, of which 14 were waited for; matrix products, arithmetic and copies ran while one was open for 0% of the time, Pallas kernels for 3%

profile of v1, /device:TPU:0, one launch (start us, length us, event | category | flops | bytes accessed | tf_op | source)
XLA Modules:
  0.0 102.0 jit_solution(17113473303963192300)
XLA Ops:
  0.6 0.0 copy-start
  0.6 0.9 copy-done
  1.6 0.9 copy-done.2
  2.5 0.9 copy-done.4
  3.5 0.0 copy-start.1
  3.5 0.0 copy-start.3
  3.5 0.0 copy-start.5
  3.6 0.0 copy-start.8
  3.6 0.5 collective-permute-start
  4.1 0.1 collective-permute-start.1
  4.2 1.3 %collective-permute-done.other_ref = bf16[3,128,512]{2,1,0:T(8,128)(2,1)S(1)} collective-permute-done((bf16[3,128,512]{2,1,0:T(8,128)(2,1)S(1)}, bf16[3,128,512]{2,1,0:T(8,128)(2,1)S(1)}, u32[]{:S(2)}, u32[]{:S(2)}) %collective-permute-start) | collective-permute-done | bytes 393248 | tf_op jit(solution)/shard_map/ppermute | solution.py:408
  5.4 0.1 pack_fields.1
  5.6 2.9 %collective-permute-start.2 = (bf16[768,128]{1,0:T(8,128)(2,1)S(1)}, bf16[768,128]{1,0:T(8,128)(2,1)S(1)}, u32[]{:S(2)}, u32[]{:S(2)}) collective-permute-start(bf16[768,128]{1,0:T(8,128)(2,1)S(1)} %get-tuple-element.33), channel_id=1, source_target_pairs={{0,1},{1,0},{2,3},{3,2},{4,5},{5,4},{6,7},{7,6},{8,9},{9,8},{10,11... | collective-permute-start | bytes 589832 | tf_op jit(solution)/shard_map/ppermute | solution.py:405
  8.5 1.5 %collective-permute-start.3 = (bf16[768,128]{1,0:T(8,128)(2,1)S(1)}, bf16[768,128]{1,0:T(8,128)(2,1)S(1)}, u32[]{:S(2)}, u32[]{:S(2)}) collective-permute-start(bf16[768,128]{1,0:T(8,128)(2,1)S(1)} %get-tuple-element.34), channel_id=1, source_target_pairs={{0,2},{1,3},{2,0},{3,1},{4,6},{5,7},{6,4},{7,5},{8,10},{9,11},{10,... | collective-permute-start | bytes 589832 | tf_op jit(solution)/shard_map/ppermute | solution.py:405
  10.0 0.0 collective-permute-start.4
  10.0 0.0 collective-permute-done.1.other_ref.og_other_ref
  10.1 0.8 att_grad.1.att_ref
  10.9 1.3 %collective-permute-done.2.r1_ref = bf16[768,128]{1,0:T(8,128)(2,1)S(1)} collective-permute-done((bf16[768,128]{1,0:T(8,128)(2,1)S(1)}, bf16[768,128]{1,0:T(8,128)(2,1)S(1)}, u32[]{:S(2)}, u32[]{:S(2)}) %collective-permute-start.2) | collective-permute-done | bytes 196640 | tf_op jit(solution)/shard_map/ppermute | solution.py:405
  12.2 3.2 %collective-permute-done.3.r2_ref = bf16[768,128]{1,0:T(8,128)(2,1)S(1)} collective-permute-done((bf16[768,128]{1,0:T(8,128)(2,1)S(1)}, bf16[768,128]{1,0:T(8,128)(2,1)S(1)}, u32[]{:S(2)}, u32[]{:S(2)}) %collective-permute-start.3) | collective-permute-done | bytes 196640 | tf_op jit(solution)/shard_map/ppermute | solution.py:405
  15.4 1.2 %collective-permute-done.4.r3_ref = bf16[768,128]{1,0:T(8,128)(2,1)S(1)} collective-permute-done((bf16[768,128]{1,0:T(8,128)(2,1)S(1)}, bf16[768,128]{1,0:T(8,128)(2,1)S(1)}, u32[]{:S(2)}, u32[]{:S(2)}) %collective-permute-start.4) | collective-permute-done | bytes 196640 | tf_op jit(solution)/shard_map/ppermute | solution.py:405
  16.6 0.7 forward.1
  17.3 3.5 %collective-permute-start.5 = (bf16[2048,128]{1,0:T(8,128)(2,1)S(1)}, bf16[2048,128]{1,0:T(8,128)(2,1)S(1)}, u32[]{:S(2)}, u32[]{:S(2)}) collective-permute-start(bf16[2048,128]{1,0:T(8,128)(2,1)S(1)} %get-tuple-element.37.fkv_ref), channel_id=1, source_target_pairs={{0,4},{1,5},{2,6},{3,7},{4,8},{5,9},{6,10},{7,11},{8,12},{9,13},{1... | collective-permute-start | bytes 1572872 | tf_op jit(solution)/shard_map/ppermute | solution.py:405
  20.8 0.7 collective-permute-start.6
  21.5 1.1 %collective-permute-start.7 = (bf16[512,128]{1,0:T(8,128)(2,1)S(1)}, bf16[512,128]{1,0:T(8,128)(2,1)S(1)}, u32[]{:S(2)}, u32[]{:S(2)}) collective-permute-start(bf16[512,128]{1,0:T(8,128)(2,1)S(1)} %get-tuple-element.39), channel_id=1, source_target_pairs={{0,2},{1,3},{2,0},{3,1},{4,6},{5,7},{6,4},{7,5},{8,10},{9,11},{10,... | collective-permute-start | bytes 393224 | tf_op jit(solution)/shard_map/ppermute | solution.py:405
  22.6 1.7 %collective-permute-start.8 = (bf16[512,128]{1,0:T(8,128)(2,1)S(1)}, bf16[512,128]{1,0:T(8,128)(2,1)S(1)}, u32[]{:S(2)}, u32[]{:S(2)}) collective-permute-start(bf16[512,128]{1,0:T(8,128)(2,1)S(1)} %get-tuple-element.40), channel_id=1, source_target_pairs={{0,3},{1,2},{2,1},{3,0},{4,7},{5,6},{6,5},{7,4},{8,11},{9,10},{10,... | collective-permute-start | bytes 393224 | tf_op jit(solution)/shard_map/ppermute | solution.py:405
  24.4 1.5 %collective-permute-done.6.o1_ref = bf16[512,128]{1,0:T(8,128)(2,1)S(1)} collective-permute-done((bf16[512,128]{1,0:T(8,128)(2,1)S(1)}, bf16[512,128]{1,0:T(8,128)(2,1)S(1)}, u32[]{:S(2)}, u32[]{:S(2)}) %collective-permute-start.6) | collective-permute-done | bytes 131104 | tf_op jit(solution)/shard_map/ppermute | solution.py:405
  25.9 0.6 collective-permute-done.7.o2_ref
  26.5 2.0 %collective-permute-done.8.o3_ref = bf16[512,128]{1,0:T(8,128)(2,1)S(1)} collective-permute-done((bf16[512,128]{1,0:T(8,128)(2,1)S(1)}, bf16[512,128]{1,0:T(8,128)(2,1)S(1)}, u32[]{:S(2)}, u32[]{:S(2)}) %collective-permute-start.8) | collective-permute-done | bytes 131104 | tf_op jit(solution)/shard_map/ppermute | solution.py:405
  28.5 1.3 %collective-permute-done.5.halo_ref = bf16[2048,128]{1,0:T(8,128)(2,1)S(1)} collective-permute-done((bf16[2048,128]{1,0:T(8,128)(2,1)S(1)}, bf16[2048,128]{1,0:T(8,128)(2,1)S(1)}, u32[]{:S(2)}, u32[]{:S(2)}) %collective-permute-start.5) | collective-permute-done | bytes 524320 | tf_op jit(solution)/shard_map/ppermute | solution.py:405
  29.8 6.9 %attention.1 = (bf16[1024,128]{1,0:T(8,128)(2,1)S(1)}, f32[2,3,512,128]{3,2,1,0:T(8,128)S(1)}, bf16[2048,128]{1,0:T(8,128)(2,1)S(1)}) custom-call(s32[4]{0:T(128)S(1)} %copy-done.9, s32[4]{0:T(128)S(1)} %copy-done.8, bf16[1024,128]{1,0:T(8,128)(2,1)S(1)} %get-tuple-element.36.fq_ref, bf16[2048,128]{1,0:T(8,128)(2,1)S(1)} %get-tuple-element.37.fkv_ref, ...), custom_call_target="tpu_custom_call" | custom-call | tf_op jit(solution)/shard_map/attention/pallas_call | solution.py:45
  36.7 1.3 %collective-permute-start.9 = (bf16[2048,128]{1,0:T(8,128)(2,1)S(1)}, bf16[2048,128]{1,0:T(8,128)(2,1)S(1)}, u32[]{:S(2)}, u32[]{:S(2)}) collective-permute-start(bf16[2048,128]{1,0:T(8,128)(2,1)S(1)} %get-tuple-element.42), channel_id=1, source_target_pairs={{4,0},{5,1},{6,2},{7,3},{8,4},{9,5},{10,6},{11,7},{12,8},{13,9},{1... | collective-permute-start | bytes 1572872 | tf_op jit(solution)/shard_map/ppermute | solution.py:405
  38.0 0.3 collective-permute-start.17
  38.3 0.8 collective-permute-start.18
  39.1 2.5 %collective-permute-start.19 = (bf16[128,1024]{1,0:T(8,128)(2,1)S(1)}, bf16[128,1024]{1,0:T(8,128)(2,1)S(1)}, u32[]{:S(2)}, u32[]{:S(2)}) collective-permute-start(bf16[128,1024]{1,0:T(8,128)(2,1)S(1)} %bitcast.20), channel_id=1, source_target_pairs={{0,3},{1,2},{2,1},{3,0},{4,7},{5,6},{6,5},{7,4},{8,11},{9,10},{10,... | collective-permute-start | bytes 786440 | tf_op jit(solution)/shard_map/ppermute | solution.py:405
  41.6 5.6 %collective-permute-done.17.a1_ref = bf16[128,1024]{1,0:T(8,128)(2,1)S(1)} collective-permute-done((bf16[128,1024]{1,0:T(8,128)(2,1)S(1)}, bf16[128,1024]{1,0:T(8,128)(2,1)S(1)}, u32[]{:S(2)}, u32[]{:S(2)}) %collective-permute-start.17) | collective-permute-done | bytes 262176 | tf_op jit(solution)/shard_map/ppermute | solution.py:405
  47.2 0.5 collective-permute-start.21
  47.7 5.5 %collective-permute-done.19.a3_ref = bf16[128,1024]{1,0:T(8,128)(2,1)S(1)} collective-permute-done((bf16[128,1024]{1,0:T(8,128)(2,1)S(1)}, bf16[128,1024]{1,0:T(8,128)(2,1)S(1)}, u32[]{:S(2)}, u32[]{:S(2)}) %collective-permute-start.19) | collective-permute-done | bytes 262176 | tf_op jit(solution)/shard_map/ppermute | solution.py:405
  53.2 0.1 collective-permute-start.22
  53.3 0.0 collective-permute-done.9.tail_ref
  53.3 0.1 pack_grads.1
  53.5 1.4 %collective-permute-start.10 = (bf16[768,128]{1,0:T(8,128)(2,1)S(1)}, bf16[768,128]{1,0:T(8,128)(2,1)S(1)}, u32[]{:S(2)}, u32[]{:S(2)}) collective-permute-start(bf16[768,128]{1,0:T(8,128)(2,1)S(1)} %get-tuple-element.44), channel_id=1, source_target_pairs={{0,1},{1,0},{2,3},{3,2},{4,5},{5,4},{6,7},{7,6},{8,9},{9,8},{10,11... | collective-permute-start | bytes 589832 | tf_op jit(solution)/shard_map/ppermute | solution.py:405
  54.9 1.5 %collective-permute-start.11 = (bf16[768,128]{1,0:T(8,128)(2,1)S(1)}, bf16[768,128]{1,0:T(8,128)(2,1)S(1)}, u32[]{:S(2)}, u32[]{:S(2)}) collective-permute-start(bf16[768,128]{1,0:T(8,128)(2,1)S(1)} %get-tuple-element.45), channel_id=1, source_target_pairs={{0,2},{1,3},{2,0},{3,1},{4,6},{5,7},{6,4},{7,5},{8,10},{9,11},{10,... | collective-permute-start | bytes 589832 | tf_op jit(solution)/shard_map/ppermute | solution.py:405
  56.4 0.7 collective-permute-start.12
  57.0 0.7 collective-permute-start.14
  57.7 0.7 collective-permute-start.15
  58.4 0.7 collective-permute-start.16
  59.1 0.8 weight.1
  59.9 2.4 %collective-permute-start.23 = (bf16[32,1024]{1,0:T(8,128)(2,1)S(1)}, bf16[32,1024]{1,0:T(8,128)(2,1)S(1)}, u32[]{:S(2)}, u32[]{:S(2)}) collective-permute-start(bf16[32,1024]{1,0:T(8,128)(2,1)S(1)} %get-tuple-element.59), channel_id=1, source_target_pairs={{0,4},{1,5},{2,6},{3,7},{4,0},{5,1},{6,2},{7,3},{8,12},{9,13},{10,... | collective-permute-start | bytes 196616 | tf_op jit(solution)/shard_map/ppermute | solution.py:405
  62.3 1.7 %collective-permute-start.24 = (bf16[32,1024]{1,0:T(8,128)(2,1)S(1)}, bf16[32,1024]{1,0:T(8,128)(2,1)S(1)}, u32[]{:S(2)}, u32[]{:S(2)}) collective-permute-start(bf16[32,1024]{1,0:T(8,128)(2,1)S(1)} %get-tuple-element.60), channel_id=1, source_target_pairs={{0,8},{1,9},{2,10},{3,11},{4,12},{5,13},{6,14},{7,15},{8,0},{9,1},... | collective-permute-start | bytes 196616 | tf_op jit(solution)/shard_map/ppermute | solution.py:405
  64.0 1.4 %collective-permute-start.25 = (bf16[32,1024]{1,0:T(8,128)(2,1)S(1)}, bf16[32,1024]{1,0:T(8,128)(2,1)S(1)}, u32[]{:S(2)}, u32[]{:S(2)}) collective-permute-start(bf16[32,1024]{1,0:T(8,128)(2,1)S(1)} %get-tuple-element.61), channel_id=1, source_target_pairs={{0,12},{1,13},{2,14},{3,15},{4,8},{5,9},{6,10},{7,11},{8,4},{9,5},... | collective-permute-start | bytes 196616 | tf_op jit(solution)/shard_map/ppermute | solution.py:405
  65.4 0.1 sort_grads.1
  65.5 9.5 %collective-permute-start.13 = (bf16[3,128,512]{2,1,0:T(8,128)(2,1)S(1)}, bf16[3,128,512]{2,1,0:T(8,128)(2,1)S(1)}, u32[]{:S(2)}, u32[]{:S(2)}) collective-permute-start(bf16[3,128,512]{2,1,0:T(8,128)(2,1)S(1)} %get-tuple-element.48), channel_id=1, source_target_pairs={{0,16},{16,0},{1,17},{17,1},{2,18},{18,2},{3,19},{19,3},{4,20},{20... | collective-permute-start | bytes 1179656 | tf_op jit(solution)/shard_map/ppermute | solution.py:408
  75.1 0.1 collective-permute-start.26
  75.2 2.9 %collective-permute-start.27 = (bf16[32,1024]{1,0:T(8,128)(2,1)S(1)}, bf16[32,1024]{1,0:T(8,128)(2,1)S(1)}, u32[]{:S(2)}, u32[]{:S(2)}) collective-permute-start(bf16[32,1024]{1,0:T(8,128)(2,1)S(1)} %sum.1.own_ref), channel_id=1, source_target_pairs={{0,8},{1,9},{2,10},{3,11},{4,12},{5,13},{6,14},{7,15},{8,0},{9,1},... | collective-permute-start | bytes 196616 | tf_op jit(solution)/shard_map/ppermute | solution.py:405
  78.2 1.4 %collective-permute-start.28 = (bf16[32,1024]{1,0:T(8,128)(2,1)S(1)}, bf16[32,1024]{1,0:T(8,128)(2,1)S(1)}, u32[]{:S(2)}, u32[]{:S(2)}) collective-permute-start(bf16[32,1024]{1,0:T(8,128)(2,1)S(1)} %sum.1.own_ref), channel_id=1, source_target_pairs={{0,12},{1,13},{2,14},{3,15},{4,8},{5,9},{6,10},{7,11},{8,4},{9,5},... | collective-permute-start | bytes 196616 | tf_op jit(solution)/shard_map/ppermute | solution.py:405
  79.6 1.0 collective-permute-done.27.g2_ref
  80.6 4.5 %collective-permute-done.28.g3_ref = bf16[32,1024]{1,0:T(8,128)(2,1)S(1)} collective-permute-done((bf16[32,1024]{1,0:T(8,128)(2,1)S(1)}, bf16[32,1024]{1,0:T(8,128)(2,1)S(1)}, u32[]{:S(2)}, u32[]{:S(2)}) %collective-permute-start.28) | collective-permute-done | bytes 65568 | tf_op jit(solution)/shard_map/ppermute | solution.py:405
  85.1 1.0 collective-permute-start.29
  86.0 1.1 %collective-permute-start.30 = (bf16[128,1024]{1,0:T(8,128)(2,1)S(1)}, bf16[128,1024]{1,0:T(8,128)(2,1)S(1)}, u32[]{:S(2)}, u32[]{:S(2)}) collective-permute-start(bf16[128,1024]{1,0:T(8,128)(2,1)S(1)} %gather_line.1.own_ref), channel_id=1, source_target_pairs={{0,2},{1,3},{2,0},{3,1},{4,6},{5,7},{6,4},{7,5},{8,10},{9,11},{10,... | collective-permute-start | bytes 786440 | tf_op jit(solution)/shard_map/ppermute | solution.py:405
  87.1 1.5 %collective-permute-start.31 = (bf16[128,1024]{1,0:T(8,128)(2,1)S(1)}, bf16[128,1024]{1,0:T(8,128)(2,1)S(1)}, u32[]{:S(2)}, u32[]{:S(2)}) collective-permute-start(bf16[128,1024]{1,0:T(8,128)(2,1)S(1)} %gather_line.1.own_ref), channel_id=1, source_target_pairs={{0,3},{1,2},{2,1},{3,0},{4,7},{5,6},{6,5},{7,4},{8,11},{9,10},{10,... | collective-permute-start | bytes 786440 | tf_op jit(solution)/shard_map/ppermute | solution.py:405
  88.6 5.6 %collective-permute-done.29.g1_ref = bf16[128,1024]{1,0:T(8,128)(2,1)S(1)} collective-permute-done((bf16[128,1024]{1,0:T(8,128)(2,1)S(1)}, bf16[128,1024]{1,0:T(8,128)(2,1)S(1)}, u32[]{:S(2)}, u32[]{:S(2)}) %collective-permute-start.29) | collective-permute-done | bytes 262176 | tf_op jit(solution)/shard_map/ppermute | solution.py:405
  94.3 5.8 %collective-permute-done.30.g2_ref = bf16[128,1024]{1,0:T(8,128)(2,1)S(1)} collective-permute-done((bf16[128,1024]{1,0:T(8,128)(2,1)S(1)}, bf16[128,1024]{1,0:T(8,128)(2,1)S(1)}, u32[]{:S(2)}, u32[]{:S(2)}) %collective-permute-start.30) | collective-permute-done | bytes 262176 | tf_op jit(solution)/shard_map/ppermute | solution.py:405
  100.0 1.1 %gather_group.1 = bf16[512,1024]{1,0:T(8,128)(2,1)} custom-call(bf16[128,1024]{1,0:T(8,128)(2,1)S(1)} %gather_line.1.own_ref, bf16[128,1024]{1,0:T(8,128)(2,1)S(1)} %collective-permute-done.29.g1_ref, bf16[128,1024]{1,0:T(8,128)(2,1)S(1)} %collective-permute-done.30.g2_ref, bf16[128,1024]{1,0:T(8,128)(2,1)S(1)} %collective-permute-done.31.g3_ref), custom_call_target="tpu_custom_call" | custom-call | tf_op jit(solution)/shard_map/gather_group/pallas_call | solution.py:45
  101.1 0.9 join_grads.1
  (33 shorter events, 0.2 us)
Async XLA Ops:
  0.6 1.0 copy-start
  1.6 0.9 copy-start.2
  2.5 0.9 copy-start.4
  3.5 6.6 %copy-start.6 = (bf16[1,128,1024]{2,1,0:T(8,128)(2,1)S(1)}, bf16[1,128,1024]{2,1,0:T(8,128)(2,1)}, u32[]{:S(2)}) copy-start(bf16[1,128,1024]{2,1,0:T(8,128)(2,1)} %param.10) | copy-start | bytes 786436
  3.5 6.6 %copy-start.7 = (bf16[512,1024]{1,0:T(8,128)(2,1)S(1)}, bf16[512,1024]{1,0:T(8,128)(2,1)}, u32[]{:S(2)}) copy-start(bf16[512,1024]{1,0:T(8,128)(2,1)} %weight_ref.1) | copy-start | bytes 3145732
  3.5 13.1 %copy-start.1 = (bf16[1,128,1024]{2,1,0:T(8,128)(2,1)S(1)}, bf16[1,128,1024]{2,1,0:T(8,128)(2,1)}, u32[]{:S(2)}) copy-start(bf16[1,128,1024]{2,1,0:T(8,128)(2,1)} %param.7) | copy-start | bytes 786436
  3.5 13.1 %copy-start.3 = (bf16[1,128,1024]{2,1,0:T(8,128)(2,1)S(1)}, bf16[1,128,1024]{2,1,0:T(8,128)(2,1)}, u32[]{:S(2)}) copy-start(bf16[1,128,1024]{2,1,0:T(8,128)(2,1)} %param.8) | copy-start | bytes 786436
  3.5 13.1 %copy-start.5 = (bf16[1,128,1024]{2,1,0:T(8,128)(2,1)S(1)}, bf16[1,128,1024]{2,1,0:T(8,128)(2,1)}, u32[]{:S(2)}) copy-start(bf16[1,128,1024]{2,1,0:T(8,128)(2,1)} %param.9) | copy-start | bytes 786436
  3.6 13.0 %copy-start.8 = (s32[4]{0:T(128)S(1)}, s32[4]{0:T(128)}, u32[]{:S(2)}) copy-start(s32[4]{0:T(128)} %reach_ref.3) | copy-start | bytes 52
  3.6 1.9 %collective-permute-start = (bf16[3,128,512]{2,1,0:T(8,128)(2,1)S(1)}, bf16[3,128,512]{2,1,0:T(8,128)(2,1)S(1)}, u32[]{:S(2)}, u32[]{:S(2)}) collective-permute-start(bf16[3,128,512]{2,1,0:T(8,128)(2,1)S(1)} %pack_swap.1), channel_id=1, source_target_pairs={{0,16},{16,0},{1,17},{17,1},{2,18},{18,2},{3,19},{19,3},{4,20},{20... | collective-permute-start | bytes 1179656 | tf_op jit(solution)/shard_map/ppermute | solution.py:408
  4.1 6.0 %collective-permute-start.1 = (bf16[128,1024]{1,0:T(8,128)(2,1)}, bf16[128,1024]{1,0:T(8,128)(2,1)S(1)}, u32[]{:S(2)}, u32[]{:S(2)}) collective-permute-start(bf16[128,1024]{1,0:T(8,128)(2,1)} %bitcast.16), channel_id=1, source_target_pairs={{0,16},{16,0},{1,17},{17,1},{2,18},{18,2},{3,19},{19,3},{4,20},{20... | collective-permute-start | bytes 786440 | tf_op jit(solution)/shard_map/ppermute | solution.py:408
  5.6 6.6 %collective-permute-start.2 = (bf16[768,128]{1,0:T(8,128)(2,1)S(1)}, bf16[768,128]{1,0:T(8,128)(2,1)S(1)}, u32[]{:S(2)}, u32[]{:S(2)}) collective-permute-start(bf16[768,128]{1,0:T(8,128)(2,1)S(1)} %get-tuple-element.33), channel_id=1, source_target_pairs={{0,1},{1,0},{2,3},{3,2},{4,5},{5,4},{6,7},{7,6},{8,9},{9,8},{10,11... | collective-permute-start | bytes 589832 | tf_op jit(solution)/shard_map/ppermute | solution.py:405
  8.5 6.8 %collective-permute-start.3 = (bf16[768,128]{1,0:T(8,128)(2,1)S(1)}, bf16[768,128]{1,0:T(8,128)(2,1)S(1)}, u32[]{:S(2)}, u32[]{:S(2)}) collective-permute-start(bf16[768,128]{1,0:T(8,128)(2,1)S(1)} %get-tuple-element.34), channel_id=1, source_target_pairs={{0,2},{1,3},{2,0},{3,1},{4,6},{5,7},{6,4},{7,5},{8,10},{9,11},{10,... | collective-permute-start | bytes 589832 | tf_op jit(solution)/shard_map/ppermute | solution.py:405
  10.0 19.8 %copy-start.9 = (s32[4]{0:T(128)S(1)}, s32[4]{0:T(128)}, u32[]{:S(2)}) copy-start(s32[4]{0:T(128)} %width_ref.1) | copy-start | bytes 52
  10.0 6.6 %collective-permute-start.4 = (bf16[768,128]{1,0:T(8,128)(2,1)S(1)}, bf16[768,128]{1,0:T(8,128)(2,1)S(1)}, u32[]{:S(2)}, u32[]{:S(2)}) collective-permute-start(bf16[768,128]{1,0:T(8,128)(2,1)S(1)} %get-tuple-element.35), channel_id=1, source_target_pairs={{0,3},{1,2},{2,1},{3,0},{4,7},{5,6},{6,5},{7,4},{8,11},{9,10},{10,... | collective-permute-start | bytes 589832 | tf_op jit(solution)/shard_map/ppermute | solution.py:405
  17.3 12.5 %collective-permute-start.5 = (bf16[2048,128]{1,0:T(8,128)(2,1)S(1)}, bf16[2048,128]{1,0:T(8,128)(2,1)S(1)}, u32[]{:S(2)}, u32[]{:S(2)}) collective-permute-start(bf16[2048,128]{1,0:T(8,128)(2,1)S(1)} %get-tuple-element.37.fkv_ref), channel_id=1, source_target_pairs={{0,4},{1,5},{2,6},{3,7},{4,8},{5,9},{6,10},{7,11},{8,12},{9,13},{1... | collective-permute-start | bytes 1572872 | tf_op jit(solution)/shard_map/ppermute | solution.py:405
  20.8 5.0 %collective-permute-start.6 = (bf16[512,128]{1,0:T(8,128)(2,1)S(1)}, bf16[512,128]{1,0:T(8,128)(2,1)S(1)}, u32[]{:S(2)}, u32[]{:S(2)}) collective-permute-start(bf16[512,128]{1,0:T(8,128)(2,1)S(1)} %get-tuple-element.38), channel_id=1, source_target_pairs={{0,1},{1,0},{2,3},{3,2},{4,5},{5,4},{6,7},{7,6},{8,9},{9,8},{10,11... | collective-permute-start | bytes 393224 | tf_op jit(solution)/shard_map/ppermute | solution.py:405
  21.5 5.0 %collective-permute-start.7 = (bf16[512,128]{1,0:T(8,128)(2,1)S(1)}, bf16[512,128]{1,0:T(8,128)(2,1)S(1)}, u32[]{:S(2)}, u32[]{:S(2)}) collective-permute-start(bf16[512,128]{1,0:T(8,128)(2,1)S(1)} %get-tuple-element.39), channel_id=1, source_target_pairs={{0,2},{1,3},{2,0},{3,1},{4,6},{5,7},{6,4},{7,5},{8,10},{9,11},{10,... | collective-permute-start | bytes 393224 | tf_op jit(solution)/shard_map/ppermute | solution.py:405
  22.6 5.9 %collective-permute-start.8 = (bf16[512,128]{1,0:T(8,128)(2,1)S(1)}, bf16[512,128]{1,0:T(8,128)(2,1)S(1)}, u32[]{:S(2)}, u32[]{:S(2)}) collective-permute-start(bf16[512,128]{1,0:T(8,128)(2,1)S(1)} %get-tuple-element.40), channel_id=1, source_target_pairs={{0,3},{1,2},{2,1},{3,0},{4,7},{5,6},{6,5},{7,4},{8,11},{9,10},{10,... | collective-permute-start | bytes 393224 | tf_op jit(solution)/shard_map/ppermute | solution.py:405
  36.7 16.6 %collective-permute-start.9 = (bf16[2048,128]{1,0:T(8,128)(2,1)S(1)}, bf16[2048,128]{1,0:T(8,128)(2,1)S(1)}, u32[]{:S(2)}, u32[]{:S(2)}) collective-permute-start(bf16[2048,128]{1,0:T(8,128)(2,1)S(1)} %get-tuple-element.42), channel_id=1, source_target_pairs={{4,0},{5,1},{6,2},{7,3},{8,4},{9,5},{10,6},{11,7},{12,8},{13,9},{1... | collective-permute-start | bytes 1572872 | tf_op jit(solution)/shard_map/ppermute | solution.py:405
  38.0 9.2 %collective-permute-start.17 = (bf16[128,1024]{1,0:T(8,128)(2,1)S(1)}, bf16[128,1024]{1,0:T(8,128)(2,1)S(1)}, u32[]{:S(2)}, u32[]{:S(2)}) collective-permute-start(bf16[128,1024]{1,0:T(8,128)(2,1)S(1)} %bitcast.18), channel_id=1, source_target_pairs={{0,1},{1,0},{2,3},{3,2},{4,5},{5,4},{6,7},{7,6},{8,9},{9,8},{10,11... | collective-permute-start | bytes 786440 | tf_op jit(solution)/shard_map/ppermute | solution.py:405
  38.3 8.9 %collective-permute-start.18 = (bf16[128,1024]{1,0:T(8,128)(2,1)S(1)}, bf16[128,1024]{1,0:T(8,128)(2,1)S(1)}, u32[]{:S(2)}, u32[]{:S(2)}) collective-permute-start(bf16[128,1024]{1,0:T(8,128)(2,1)S(1)} %bitcast.19), channel_id=1, source_target_pairs={{0,2},{1,3},{2,0},{3,1},{4,6},{5,7},{6,4},{7,5},{8,10},{9,11},{10,... | collective-permute-start | bytes 786440 | tf_op jit(solution)/shard_map/ppermute | solution.py:405
  39.1 14.1 %collective-permute-start.19 = (bf16[128,1024]{1,0:T(8,128)(2,1)S(1)}, bf16[128,1024]{1,0:T(8,128)(2,1)S(1)}, u32[]{:S(2)}, u32[]{:S(2)}) collective-permute-start(bf16[128,1024]{1,0:T(8,128)(2,1)S(1)} %bitcast.20), channel_id=1, source_target_pairs={{0,3},{1,2},{2,1},{3,0},{4,7},{5,6},{6,5},{7,4},{8,11},{9,10},{10,... | collective-permute-start | bytes 786440 | tf_op jit(solution)/shard_map/ppermute | solution.py:405
  47.2 9.2 %collective-permute-start.20 = (bf16[128,1024]{1,0:T(8,128)(2,1)S(1)}, bf16[128,1024]{1,0:T(8,128)(2,1)S(1)}, u32[]{:S(2)}, u32[]{:S(2)}) collective-permute-start(bf16[128,1024]{1,0:T(8,128)(2,1)S(1)} %collective-permute-done.17.a1_ref), channel_id=1, source_target_pairs={{0,16},{16,0},{1,17},{17,1},{2,18},{18,2},{3,19},{19,3},{4,20},{20... | collective-permute-start | bytes 786440 | tf_op jit(solution)/shard_map/ppermute | solution.py:408
  47.2 9.8 %collective-permute-start.21 = (bf16[128,1024]{1,0:T(8,128)(2,1)S(1)}, bf16[128,1024]{1,0:T(8,128)(2,1)S(1)}, u32[]{:S(2)}, u32[]{:S(2)}) collective-permute-start(bf16[128,1024]{1,0:T(8,128)(2,1)S(1)} %collective-permute-done.18.a2_ref), channel_id=1, source_target_pairs={{0,16},{16,0},{1,17},{17,1},{2,18},{18,2},{3,19},{19,3},{4,20},{20... | collective-permute-start | bytes 786440 | tf_op jit(solution)/shard_map/ppermute | solution.py:408
  53.2 4.5 %collective-permute-start.22 = (bf16[128,1024]{1,0:T(8,128)(2,1)S(1)}, bf16[128,1024]{1,0:T(8,128)(2,1)S(1)}, u32[]{:S(2)}, u32[]{:S(2)}) collective-permute-start(bf16[128,1024]{1,0:T(8,128)(2,1)S(1)} %collective-permute-done.19.a3_ref), channel_id=1, source_target_pairs={{0,16},{16,0},{1,17},{17,1},{2,18},{18,2},{3,19},{19,3},{4,20},{20... | collective-permute-start | bytes 786440 | tf_op jit(solution)/shard_map/ppermute | solution.py:408
  53.5 10.5 %collective-permute-start.10 = (bf16[768,128]{1,0:T(8,128)(2,1)S(1)}, bf16[768,128]{1,0:T(8,128)(2,1)S(1)}, u32[]{:S(2)}, u32[]{:S(2)}) collective-permute-start(bf16[768,128]{1,0:T(8,128)(2,1)S(1)} %get-tuple-element.44), channel_id=1, source_target_pairs={{0,1},{1,0},{2,3},{3,2},{4,5},{5,4},{6,7},{7,6},{8,9},{9,8},{10,11... | collective-permute-start | bytes 589832 | tf_op jit(solution)/shard_map/ppermute | solution.py:405
  54.9 10.5 %collective-permute-start.11 = (bf16[768,128]{1,0:T(8,128)(2,1)S(1)}, bf16[768,128]{1,0:T(8,128)(2,1)S(1)}, u32[]{:S(2)}, u32[]{:S(2)}) collective-permute-start(bf16[768,128]{1,0:T(8,128)(2,1)S(1)} %get-tuple-element.45), channel_id=1, source_target_pairs={{0,2},{1,3},{2,0},{3,1},{4,6},{5,7},{6,4},{7,5},{8,10},{9,11},{10,... | collective-permute-start | bytes 589832 | tf_op jit(solution)/shard_map/ppermute | solution.py:405
  56.4 9.0 %collective-permute-start.12 = (bf16[768,128]{1,0:T(8,128)(2,1)S(1)}, bf16[768,128]{1,0:T(8,128)(2,1)S(1)}, u32[]{:S(2)}, u32[]{:S(2)}) collective-permute-start(bf16[768,128]{1,0:T(8,128)(2,1)S(1)} %get-tuple-element.46), channel_id=1, source_target_pairs={{0,3},{1,2},{2,1},{3,0},{4,7},{5,6},{6,5},{7,4},{8,11},{9,10},{10,... | collective-permute-start | bytes 589832 | tf_op jit(solution)/shard_map/ppermute | solution.py:405
  57.0 1.3 %collective-permute-start.14 = (bf16[256,128]{1,0:T(8,128)(2,1)S(1)}, bf16[256,128]{1,0:T(8,128)(2,1)S(1)}, u32[]{:S(2)}, u32[]{:S(2)}) collective-permute-start(bf16[256,128]{1,0:T(8,128)(2,1)S(1)} %get-tuple-element.55), channel_id=1, source_target_pairs={{16,17},{17,16},{18,19},{19,18},{20,21},{21,20},{22,23},{23,22},{2... | collective-permute-start | bytes 196616 | tf_op jit(solution)/shard_map/ppermute | solution.py:405
  57.7 1.4 %collective-permute-start.15 = (bf16[256,128]{1,0:T(8,128)(2,1)S(1)}, bf16[256,128]{1,0:T(8,128)(2,1)S(1)}, u32[]{:S(2)}, u32[]{:S(2)}) collective-permute-start(bf16[256,128]{1,0:T(8,128)(2,1)S(1)} %get-tuple-element.56), channel_id=1, source_target_pairs={{16,18},{17,19},{18,16},{19,17},{20,22},{21,23},{22,20},{23,21},{2... | collective-permute-start | bytes 196616 | tf_op jit(solution)/shard_map/ppermute | solution.py:405
  58.4 0.7 collective-permute-start.16
  59.9 15.2 %collective-permute-start.23 = (bf16[32,1024]{1,0:T(8,128)(2,1)S(1)}, bf16[32,1024]{1,0:T(8,128)(2,1)S(1)}, u32[]{:S(2)}, u32[]{:S(2)}) collective-permute-start(bf16[32,1024]{1,0:T(8,128)(2,1)S(1)} %get-tuple-element.59), channel_id=1, source_target_pairs={{0,4},{1,5},{2,6},{3,7},{4,0},{5,1},{6,2},{7,3},{8,12},{9,13},{10,... | collective-permute-start | bytes 196616 | tf_op jit(solution)/shard_map/ppermute | solution.py:405
  62.3 12.8 %collective-permute-start.24 = (bf16[32,1024]{1,0:T(8,128)(2,1)S(1)}, bf16[32,1024]{1,0:T(8,128)(2,1)S(1)}, u32[]{:S(2)}, u32[]{:S(2)}) collective-permute-start(bf16[32,1024]{1,0:T(8,128)(2,1)S(1)} %get-tuple-element.60), channel_id=1, source_target_pairs={{0,8},{1,9},{2,10},{3,11},{4,12},{5,13},{6,14},{7,15},{8,0},{9,1},... | collective-permute-start | bytes 196616 | tf_op jit(solution)/shard_map/ppermute | solution.py:405
  64.0 11.0 %collective-permute-start.25 = (bf16[32,1024]{1,0:T(8,128)(2,1)S(1)}, bf16[32,1024]{1,0:T(8,128)(2,1)S(1)}, u32[]{:S(2)}, u32[]{:S(2)}) collective-permute-start(bf16[32,1024]{1,0:T(8,128)(2,1)S(1)} %get-tuple-element.61), channel_id=1, source_target_pairs={{0,12},{1,13},{2,14},{3,15},{4,8},{5,9},{6,10},{7,11},{8,4},{9,5},... | collective-permute-start | bytes 196616 | tf_op jit(solution)/shard_map/ppermute | solution.py:405
  65.5 35.5 %collective-permute-start.13 = (bf16[3,128,512]{2,1,0:T(8,128)(2,1)S(1)}, bf16[3,128,512]{2,1,0:T(8,128)(2,1)S(1)}, u32[]{:S(2)}, u32[]{:S(2)}) collective-permute-start(bf16[3,128,512]{2,1,0:T(8,128)(2,1)S(1)} %get-tuple-element.48), channel_id=1, source_target_pairs={{0,16},{16,0},{1,17},{17,1},{2,18},{18,2},{3,19},{19,3},{4,20},{20... | collective-permute-start | bytes 1179656 | tf_op jit(solution)/shard_map/ppermute | solution.py:408
  75.1 4.5 %collective-permute-start.26 = (bf16[32,1024]{1,0:T(8,128)(2,1)S(1)}, bf16[32,1024]{1,0:T(8,128)(2,1)S(1)}, u32[]{:S(2)}, u32[]{:S(2)}) collective-permute-start(bf16[32,1024]{1,0:T(8,128)(2,1)S(1)} %sum.1.own_ref), channel_id=1, source_target_pairs={{0,4},{1,5},{2,6},{3,7},{4,0},{5,1},{6,2},{7,3},{8,12},{9,13},{10,... | collective-permute-start | bytes 196616 | tf_op jit(solution)/shard_map/ppermute | solution.py:405
  75.2 5.3 %collective-permute-start.27 = (bf16[32,1024]{1,0:T(8,128)(2,1)S(1)}, bf16[32,1024]{1,0:T(8,128)(2,1)S(1)}, u32[]{:S(2)}, u32[]{:S(2)}) collective-permute-start(bf16[32,1024]{1,0:T(8,128)(2,1)S(1)} %sum.1.own_ref), channel_id=1, source_target_pairs={{0,8},{1,9},{2,10},{3,11},{4,12},{5,13},{6,14},{7,15},{8,0},{9,1},... | collective-permute-start | bytes 196616 | tf_op jit(solution)/shard_map/ppermute | solution.py:405
  78.2 6.9 %collective-permute-start.28 = (bf16[32,1024]{1,0:T(8,128)(2,1)S(1)}, bf16[32,1024]{1,0:T(8,128)(2,1)S(1)}, u32[]{:S(2)}, u32[]{:S(2)}) collective-permute-start(bf16[32,1024]{1,0:T(8,128)(2,1)S(1)} %sum.1.own_ref), channel_id=1, source_target_pairs={{0,12},{1,13},{2,14},{3,15},{4,8},{5,9},{6,10},{7,11},{8,4},{9,5},... | collective-permute-start | bytes 196616 | tf_op jit(solution)/shard_map/ppermute | solution.py:405
  85.1 9.2 %collective-permute-start.29 = (bf16[128,1024]{1,0:T(8,128)(2,1)S(1)}, bf16[128,1024]{1,0:T(8,128)(2,1)S(1)}, u32[]{:S(2)}, u32[]{:S(2)}) collective-permute-start(bf16[128,1024]{1,0:T(8,128)(2,1)S(1)} %gather_line.1.own_ref), channel_id=1, source_target_pairs={{0,1},{1,0},{2,3},{3,2},{4,5},{5,4},{6,7},{7,6},{8,9},{9,8},{10,11... | collective-permute-start | bytes 786440 | tf_op jit(solution)/shard_map/ppermute | solution.py:405
  86.0 14.0 %collective-permute-start.30 = (bf16[128,1024]{1,0:T(8,128)(2,1)S(1)}, bf16[128,1024]{1,0:T(8,128)(2,1)S(1)}, u32[]{:S(2)}, u32[]{:S(2)}) collective-permute-start(bf16[128,1024]{1,0:T(8,128)(2,1)S(1)} %gather_line.1.own_ref), channel_id=1, source_target_pairs={{0,2},{1,3},{2,0},{3,1},{4,6},{5,7},{6,4},{7,5},{8,10},{9,11},{10,... | collective-permute-start | bytes 786440 | tf_op jit(solution)/shard_map/ppermute | solution.py:405
  87.1 12.9 %collective-permute-start.31 = (bf16[128,1024]{1,0:T(8,128)(2,1)S(1)}, bf16[128,1024]{1,0:T(8,128)(2,1)S(1)}, u32[]{:S(2)}, u32[]{:S(2)}) collective-permute-start(bf16[128,1024]{1,0:T(8,128)(2,1)S(1)} %gather_line.1.own_ref), channel_id=1, source_target_pairs={{0,3},{1,2},{2,1},{3,0},{4,7},{5,6},{6,5},{7,4},{8,11},{9,10},{10,... | collective-permute-start | bytes 786440 | tf_op jit(solution)/shard_map/ppermute | solution.py:405

commit v2 on v1

v2 whole, which is shorter than its diff:
```python
import functools
import math

import jax
import jax.numpy as jnp
from jax import lax
from jax.experimental import pallas as pl
from jax.experimental.pallas import tpu as pltpu
from jax.sharding import PartitionSpec as P

HD = 128
HB = 4
HS = 4
IMW = 512
BLK = 128
WMAX = 4

BF = jnp.bfloat16
F32 = jnp.float32
MIB = 1 << 20


def nn(a, b):
    return lax.dot_general(a, b, (((1,), (0,)), ((), ())), preferred_element_type=F32)


def nt(a, b):
    return lax.dot_general(a, b, (((1,), (1,)), ((), ())), preferred_element_type=F32)


def tn(a, b):
    return lax.dot_general(a, b, (((0,), (0,)), ((), ())), preferred_element_type=F32)


def rows_at(start, size):
    return pl.ds(pl.multiple_of(start, size), size)


def shaped(shape, dtype=BF):
    return jax.ShapeDtypeStruct(shape, dtype)


def call(kernel, outs, args, smem=0, left=0, left_out=False, scratch=(), mib=16, us=0.01, name=None):
    vmem = pl.BlockSpec(memory_space=pltpu.VMEM)
    anywhere = pl.BlockSpec(memory_space=pl.ANY)
    scalars = pl.BlockSpec(memory_space=pltpu.SMEM)
    return pl.pallas_call(
        kernel,
        out_shape=outs,
        in_specs=[scalars] * smem + [vmem] * (len(args) - smem - left) + [anywhere] * left,
        out_specs=[anywhere if left_out else vmem] * len(outs),
        scratch_shapes=list(scratch),
        compiler_params=pltpu.CompilerParams(vmem_limit_bytes=mib * MIB),
        cost_estimate=pl.CostEstimate(flops=0, bytes_accessed=int(us * 3.69e6), transcendentals=0),
        name=name,
    )(*args)


def roles(band, strided):
    role = lax.axis_index("dp")
    pl.when(role == 0)(band)
    pl.when(role == 1)(strided)


def spot(g):
    place = lax.axis_index("seq")
    return lax.div(place, g), lax.rem(place, g)


def read_field(own_ref, other_ref, att_ref, i, t):
    if t == 3:
        return lambda rows, lanes: att_ref[i, rows, lanes]
    return lambda rows, lanes: (own_ref, other_ref)[i][t, rows, lanes]


def pack_fields_kernel(g, own_ref, other_ref, att_ref, *out_refs):
    line, spot_ = spot(g)
    rows = own_ref.shape[1]
    chunk = rows // g
    fields = [(i, t, read_field(own_ref, other_ref, att_ref, i, t)) for i in range(2) for t in range(4)]

    def band():
        for d in range(1, g):
            for i, t, read in fields:
                at = (i * 4 + t) * rows
                out_refs[d - 1][at : at + rows] = read(slice(None), rows_at((spot_ ^ d) * HD, HD))

    def strided():
        for d in range(1, g):
            there = rows_at((line ^ d) * chunk, chunk)
            for i, t, read in fields:
                for h in range(HS):
                    at = (i * 4 + t) * rows + h * chunk
                    out_refs[d - 1][at : at + chunk] = read(there, slice(h * HD, (h + 1) * HD))

    roles(band, strided)


def att_grad_kernel(own_ref, other_ref, weight_ref, out_ref):
    out_ref[0] = nt(own_ref[...], weight_ref[...]).astype(BF)
    out_ref[1] = nt(other_ref[...], weight_ref[...]).astype(BF)


def strided_bias(rows, chunk, reach):
    key = lax.broadcasted_iota(jnp.int32, (rows, rows), 0)
    query = lax.broadcasted_iota(jnp.int32, (rows, rows), 1)
    apart = lax.div(query, chunk) - lax.div(key, chunk)
    same = lax.rem(key, chunk) == lax.rem(query, chunk)
    return jnp.where(same & (apart >= 0) & (apart < reach), 0.0, -1e30)


def score_grads(probs, probs_low, dprobs):
    delta = jnp.sum(probs_low.astype(F32) * dprobs, axis=0, keepdims=True)
    return (probs * (dprobs - delta)).astype(BF), delta


SCALE = HD ** (-0.5)
SCALE_2 = SCALE / math.log(2)


def softmax(scores, bias):
    scores = scores * SCALE_2 + bias
    peak = jnp.max(scores, axis=0, keepdims=True)
    raised = jnp.exp2(scores - peak)
    total = jnp.sum(raised, axis=0, keepdims=True)
    return raised * (1.0 / total), peak + jnp.log2(total)


def forward_kernel(g, reach_ref, own_ref, other_ref, att_ref, r1_ref, r2_ref, r3_ref,
                   fqg_ref, fkv_ref, o1_ref, o2_ref, o3_ref, keep_ref, grads_ref):
    line, spot_ = spot(g)
    rows = own_ref.shape[1]
    span = g * rows
    chunk = rows // g
    came = (r1_ref, r2_ref, r3_ref)
    back = (o1_ref, o2_ref, o3_ref)
    fields = [(i, t, read_field(own_ref, other_ref, att_ref, i, t)) for i in range(2) for t in range(4)]

    def put(i, t, start, size, value):
        ref = (fqg_ref, fkv_ref, fkv_ref, fqg_ref)[t]
        ref[rows_at((t // 2 * 2 + i) * span + start, size)] = value

    def band():
        for i, t, read in fields:
            at = (i * 4 + t) * rows
            put(i, t, spot_ * rows, rows, read(slice(None), rows_at(spot_ * HD, HD)))
            for d in range(1, g):
                put(i, t, (spot_ ^ d) * rows, rows, came[d - 1][at : at + rows])

    def strided():
        here = rows_at(line * chunk, chunk)
        for i, t, read in fields:
            for h in range(HS):
                at = (i * 4 + t) * rows + h * chunk
                put(i, t, h * rows + line * chunk, chunk, read(here, slice(h * HD, (h + 1) * HD)))
                for d in range(1, g):
                    put(i, t, h * rows + (line ^ d) * chunk, chunk, came[d - 1][at : at + chunk])
        each = [(i, h) for h in range(HS) for i in range(2)]

        def head(t, i, h):
            at = (t // 2 * 2 + i) * span + h * rows
            return (fqg_ref, fkv_ref, fkv_ref, fqg_ref)[t][at : at + rows]

        scores, dprobs, probs = {}, {}, {}
        for i, h in each:
            scores[i, h] = nt(head(1, i, h), head(0, i, h))
            dprobs[i, h] = nt(head(2, i, h), head(3, i, h))
        for h in range(HS):
            bias = strided_bias(rows, chunk, reach_ref[h])
            for i in range(2):
                probs[i, h], _ = softmax(scores[i, h], bias)
        for i, h in each:
            keep_ref[i, h] = tn(probs[i, h].astype(BF), head(2, i, h)).astype(BF)
        for d in range(1, g):
            there = rows_at((line ^ d) * chunk, chunk)
            for i, h in each:
                at = (i * HS + h) * chunk
                back[d - 1][at : at + chunk] = keep_ref[i, h, there]
        for i, h in each:
            mine = slice(h * rows, (h + 1) * rows)
            probs_low = probs[i, h].astype(BF)
            dscores, _ = score_grads(probs[i, h], probs_low, dprobs[i, h])
            grads_ref[i, 0, mine] = (tn(dscores, head(1, i, h)) * SCALE).astype(BF)
            grads_ref[i, 1, mine] = (nn(dscores, head(0, i, h)) * SCALE).astype(BF)
            grads_ref[i, 2, mine] = nn(probs_low, head(3, i, h)).astype(BF)

    roles(band, strided)


def heads_kernel(g, keep_ref, o1_ref, o2_ref, o3_ref, p1_ref, p2_ref, p3_ref, mine_ref):
    line, spot_ = spot(g)
    rows = keep_ref.shape[2]
    chunk = rows // g
    came = (o1_ref, o2_ref, o3_ref)
    outs = (mine_ref, p1_ref, p2_ref, p3_ref)

    def strided():
        for to in range(g):
            head = spot_ ^ to
            for i in range(2):
                outs[to][rows_at(i * rows + line * chunk, chunk)] = keep_ref[i, head, rows_at(line * chunk, chunk)]
                for d in range(1, g):
                    source = rows_at((i * HS + head) * chunk, chunk)
                    outs[to][rows_at(i * rows + (line ^ d) * chunk, chunk)] = came[d - 1][source]

    roles(lambda: None, strided)


def attention_kernel(g, width_ref, fqg_ref, fkv_ref, halo_ref, order_ref,
                     out_ref, dquery_ref, dkv_ref, stats_ref, key_s, value_s, key_t, value_t):
    line, spot_ = spot(g)
    span = dquery_ref.shape[1]
    rows = span // g

    def band():
        width = width_ref[spot_]
        key_at = lax.broadcasted_iota(jnp.int32, (span + rows, rows), 0)
        query_at = lax.broadcasted_iota(jnp.int32, (span + rows, rows), 1)
        block = lax.div(key_at, BLK)
        near = (block >= WMAX - width) & (key_at - span <= query_at)
        for i in range(2):
            for t, ref in enumerate((key_s, value_s)):
                here = slice((t * 2 + i) * span, (t * 2 + i + 1) * span)
                ref[i, :span] = halo_ref[here]
                ref[i, span:] = fkv_ref[here]
            key_t[i] = key_s[i].T
            value_t[i] = value_s[i].T
        for b in reversed(range(g)):
            bias = jnp.where(near & ((block + b >= g) | (line > 0)), 0.0, -1e30)
            window = slice(b * rows, b * rows + span + rows)
            mine = slice(b * rows, (b + 1) * rows)
            own = slice(span - b * rows, span + rows)
            for i in range(2):
                query = fqg_ref[i * span + b * rows : i * span + (b + 1) * rows]
                grad = fqg_ref[(2 + i) * span + b * rows : (2 + i) * span + (b + 1) * rows]
                probs, total = softmax(nt(key_s[i, window], query), bias)
                probs_low = probs.astype(BF)
                out_ref[i, :, mine] = nn(value_t[i, :, window], probs_low).astype(BF)
                dscores, delta = score_grads(probs, probs_low, nt(value_s[i, window], grad))
                stats_ref[i * 8 : i * 8 + 1, mine] = total
                stats_ref[i * 8 + 1 : i * 8 + 2, mine] = delta
                dquery_ref[i, mine] = (nn(key_t[i, :, window], dscores) * SCALE).astype(BF).T
                dkey = nn(dscores[own], query) * SCALE
                dvalue = nn(probs_low[own], grad)
                if b == g - 1:
                    dkv_ref[i, 0] = dkey
                    dkv_ref[i, 1] = dvalue
                else:
                    dkv_ref[i, 0, : (b + 1) * rows] += dkey
                    dkv_ref[i, 1, : (b + 1) * rows] += dvalue

    roles(band, lambda: None)


def tail_kernel(g, width_ref, fkv_ref, next_ref, stats_ref, dkv_ref, out_ref):
    line, spot_ = spot(g)
    span = dkv_ref.shape[2]
    rows = span // g

    def band():
        out_ref[...] = dkv_ref[...]

        @pl.when(line < g - 1)
        def _():
            width = width_ref[spot_]
            for b in range(g):
                block = lax.div(lax.broadcasted_iota(jnp.int32, (span - b * rows, rows), 0), BLK)
                bias = jnp.where(block >= WMAX - width, 0.0, -1e30)
                mine = slice(b * rows, (b + 1) * rows)
                for i in range(2):
                    query = next_ref[i * span + b * rows : i * span + (b + 1) * rows]
                    grad = next_ref[(2 + i) * span + b * rows : (2 + i) * span + (b + 1) * rows]
                    key = fkv_ref[i * span + b * rows : (i + 1) * span]
                    value = fkv_ref[(2 + i) * span + b * rows : (3 + i) * span]
                    total = stats_ref[i * 8 : i * 8 + 1, mine]
                    delta = stats_ref[i * 8 + 1 : i * 8 + 2, mine]
                    probs = jnp.exp2(nt(key, query) * SCALE_2 + bias - total)
                    dscores = (probs * (nt(value, grad) - delta)).astype(BF)
                    out_ref[i, 0, b * rows :] += nn(dscores, query) * SCALE
                    out_ref[i, 1, b * rows :] += nn(probs.astype(BF), grad)

    roles(band, lambda: None)


def weight_kernel(g, out_ref, mine_ref, p1_ref, p2_ref, p3_ref, og_ref, og_other_ref,
                  a1_ref, a2_ref, a3_ref, b1_ref, b2_ref, b3_ref, part_ref, z1_ref, z2_ref, z3_ref, sum_s):
    line, spot_ = spot(g)
    rows = og_ref.shape[0]
    chunk = rows // g
    heads = (mine_ref, p1_ref, p2_ref, p3_ref)

    outer = ((og_ref, a1_ref, a2_ref, a3_ref), (og_other_ref, b1_ref, b2_ref, b3_ref))

    def add(part):
        sum_s[...] = sum(part(i, d) for i in range(2) for d in range(g))

    roles(
        lambda: add(lambda i, d: nn(out_ref[i, :, rows_at((spot_ ^ d) * rows, rows)], outer[i][d][...])),
        lambda: add(lambda i, d: tn(heads[d][i * rows : (i + 1) * rows], outer[i][d][...])),
    )
    part_ref[...] = sum_s[rows_at(line * chunk, chunk)]
    for d, ref in enumerate((z1_ref, z2_ref, z3_ref), 1):
        ref[...] = sum_s[rows_at((line ^ d) * chunk, chunk)].astype(BF)


def pack_grads_kernel(g, dquery_ref, dkv_ref, strided_ref, keep_ref, r1_ref, r2_ref, r3_ref):
    line, spot_ = spot(g)
    span = dquery_ref.shape[1]
    rows = span // g
    chunk = rows // g
    outs = (keep_ref, r1_ref, r2_ref, r3_ref)

    def band():
        for d in range(g):
            block = rows_at((spot_ ^ d) * rows, rows)
            for i in range(2):
                for t in range(3):
                    value = dquery_ref[i, block] if t == 0 else dkv_ref[i, t - 1, block].astype(BF)
                    outs[d][(i * 3 + t) * rows : (i * 3 + t + 1) * rows] = value

    def strided():
        for d in range(g):
            for i in range(2):
                for t in range(3):
                    for h in range(HS):
                        at = (i * 3 + t) * rows + h * chunk
                        there = rows_at(h * rows + (line ^ d) * chunk, chunk)
                        outs[d][at : at + chunk] = strided_ref[i, t, there]

    roles(band, strided)


def sort_grads_kernel(g, keep_ref, r1_ref, r2_ref, r3_ref, own_ref, *rest):
    line, spot_ = spot(g)
    rows = own_ref.shape[1]
    chunk = rows // g
    came = (keep_ref, r1_ref, r2_ref, r3_ref)
    piece_refs, other_s = rest[:-1], rest[-1]

    def band():
        for d in range(g):
            lanes = rows_at((spot_ ^ d) * HD, HD)
            for t in range(3):
                own_ref[t, :, lanes] = came[d][t * rows : (t + 1) * rows]
                other_s[t * rows : (t + 1) * rows, lanes] = came[d][(3 + t) * rows : (4 + t) * rows]

    def strided():
        for d in range(g):
            for t in range(3):
                for h in range(HS):
                    lanes = slice(h * HD, (h + 1) * HD)
                    at = t * rows + h * chunk
                    own_ref[t, rows_at((line ^ d) * chunk, chunk), lanes] = came[d][at : at + chunk]
                    there = rows_at(t * rows + (line ^ d) * chunk, chunk)
                    other_s[there, lanes] = came[d][3 * rows + at : 3 * rows + at + chunk]

    roles(band, strided)
    for n, ref in enumerate(piece_refs):
        ref[...] = other_s[n * ref.shape[0] : (n + 1) * ref.shape[0]]


def sum_kernel(keep_ref, z1_ref, z2_ref, z3_ref, out_ref):
    total = keep_ref[...]
    for ref in (z1_ref, z2_ref, z3_ref):
        total += ref[...].astype(F32)
    out_ref[...] = total.astype(BF)


def gather_kernel(g, own_ref, g1_ref, g2_ref, g3_ref, out_ref):
    line, _ = spot(g)
    size = own_ref.shape[0]
    for d, ref in enumerate((own_ref, g1_ref, g2_ref, g3_ref)):
        out_ref[rows_at((line ^ d) * size, size)] = ref[...]


def finish_kernel(g, own_ref, b0_ref, b1_ref, b2_ref, b3_ref, r0_ref, r1_ref, r2_ref, r3_ref,
                  dq_ref, dk_ref, dv_ref, weight_ref, sems):
    _, spot_ = spot(g)
    rows, half = own_ref.shape[1:]
    size = r0_ref.shape[0]
    pieces = (b0_ref, b1_ref, b2_ref, b3_ref)
    outs = (dq_ref, dk_ref, dv_ref)
    piece = b0_ref.shape[0]

    def run(own_at, other_at):
        copies = [
            (ref, weight_ref.at[rows_at((spot_ ^ d) * size, size)])
            for d, ref in enumerate((r0_ref, r1_ref, r2_ref, r3_ref))
        ]
        for t in range(3):
            copies.append((own_ref.at[t], outs[t].at[:, pl.ds(own_at, half)]))
        for n in range(4):
            start, stop = n * piece, (n + 1) * piece
            while start < stop:
                t = start // rows
                size_ = min(stop, (t + 1) * rows) - start
                copies.append((pieces[n].at[pl.ds(start - n * piece, size_)],
                               outs[t].at[pl.ds(start - t * rows, size_), pl.ds(other_at, half)]))
                start += size_
        copies = [pltpu.make_async_copy(src, dst, sems.at[n]) for n, (src, dst) in enumerate(copies)]
        for copy in copies:
            copy.start()
        for copy in copies:
            copy.wait()

    roles(lambda: run(0, half), lambda: run(half, 0))


def body_roles(g, queries, keys, values, out_grad, out_weight, band_width, col_reach):
    q, k, v, og = queries[0], keys[0], values[0], out_grad[0]
    rows, width = q.shape
    half = width // 2
    span = g * rows
    chunk = rows // g
    devices = lax.axis_size("seq")
    both = ("dp", "seq")

    def send(value, target):
        pairs = []
        for role in range(2):
            for line in range(g):
                for place in range(g):
                    to = target(role, line, place)
                    if to is None:
                        continue
                    to_role, to_line, to_place = to
                    pairs.append((role * devices + line * g + place, to_role * devices + to_line * g + to_place))
        return lax.ppermute(value, both, pairs)

    def swap(value):
        return lax.ppermute(value, "dp", [(0, 1), (1, 0)])

    def by_role(d):
        return lambda role, line, place: (0, line, place ^ d) if role == 0 else (1, line ^ d, place)

    def along_line(d):
        return lambda role, line, place: (role, line ^ d, place)

    def in_group(d):
        return lambda role, line, place: (role, line, place ^ d)

    def shift(step):
        return lambda role, line, place: (0, line + step, place) if role == 0 and 0 <= line + step < g else None

    def ring(step):
        def target(role, line, place):
            to = line + (step if role == 0 else -step)
            return (role, to, place) if 0 <= to < g else (1 - role, line, place)

        return target

    steps = range(1, g)
    role = lax.axis_index("dp")
    og_other = swap(og)
    to_other = jnp.stack([lax.dynamic_slice(value, (0, (1 - role) * half), (rows, half)) for value in (q, k, v)])
    own = jnp.stack([lax.dynamic_slice(value, (0, role * half), (rows, half)) for value in (q, k, v)])
    other = swap(to_other)
    (att,) = call(att_grad_kernel, [shaped((2, rows, half))], [og, og_other, out_weight], name="att_grad")
    packed = call(functools.partial(pack_fields_kernel, g), [shaped((8 * rows, HD))] * (g - 1),
                  [own, other, att], name="pack_fields")
    came = [send(packed[d - 1], by_role(d)) for d in steps]
    near = [send(og, in_group(d)) for d in steps]
    near_other = [swap(value) for value in near]
    fqg, fkv, *back, keep, strided_grads = call(
        functools.partial(forward_kernel, g),
        [shaped((4 * span, HD))] * 2 + [shaped((2 * rows, HD))] * (g - 1)
        + [shaped((2, HS, rows, HD)), shaped((2, 3, span, HD))],
        [col_reach, own, other, att] + came, smem=1, name="forward",
    )
    halo = send(fkv, shift(1))
    following = send(fqg, shift(-1))
    back = [send(back[d - 1], by_role(d)) for d in steps]
    *to_heads, mine = call(functools.partial(heads_kernel, g), [shaped((2 * rows, HD))] * g,
                           [keep] + back, name="heads")
    heads = [send(to_heads[d - 1], in_group(d)) for d in steps]
    band_out, dquery, dkv, stats = call(
        functools.partial(attention_kernel, g),
        [shaped((2, HD, span)), shaped((2, span, HD)), shaped((2, 2, span, HD), F32), shaped((16, span), F32)],
        [band_width, fqg, fkv, halo, following], smem=1, left=1,
        scratch=[pltpu.VMEM((2, 2 * span, HD), BF), pltpu.VMEM((2, 2 * span, HD), BF),
                 pltpu.VMEM((2, HD, 2 * span), BF), pltpu.VMEM((2, HD, 2 * span), BF)],
        mib=24, name="attention",
    )
    piece = half // g // g
    parts = call(
        functools.partial(weight_kernel, g), [shaped((piece, width), F32)] + [shaped((piece, width))] * (g - 1),
        [band_out, mine] + heads + [og, og_other] + near + near_other,
        scratch=[pltpu.VMEM((half // g, width), F32)], name="weight",
    )
    summed = [send(parts[d], along_line(d)) for d in steps]
    stats = send(stats, ring(-1))
    (dkv,) = call(functools.partial(tail_kernel, g), [shaped(dkv.shape, F32)],
                  [band_width, fkv, following, stats, dkv], smem=1, name="tail")
    (piece_sum,) = call(sum_kernel, [shaped((piece, width))], [parts[0]] + summed, name="sum")
    pieces = [send(piece_sum, along_line(d)) for d in steps]
    (head_rows,) = call(functools.partial(gather_kernel, g), [shaped((half // g, width))],
                        [piece_sum] + pieces, name="gather_line")
    others = [send(head_rows, in_group(d)) for d in steps]
    returned = call(functools.partial(pack_grads_kernel, g), [shaped((6 * rows, HD))] * g,
                    [dquery, dkv, strided_grads], name="pack_grads")
    returned = [returned[0]] + [send(returned[d], by_role(d)) for d in steps]
    own, *to_other = call(functools.partial(sort_grads_kernel, g),
                          [shaped((3, rows, half))] + [shaped((3 * rows // 4, half))] * 4, returned,
                          scratch=[pltpu.VMEM((3 * rows, half), BF)], name="sort_grads")
    dq, dk, dv, weight_grad = call(
        functools.partial(finish_kernel, g), [shaped((rows, width))] * 3 + [shaped((half, width))],
        [own] + [swap(value) for value in to_other] + [head_rows] + others, left_out=True,
        scratch=[pltpu.SemaphoreType.DMA((g + 12,))], name="finish",
    )
    return dq[None], dk[None], dv[None], weight_grad


def from_behind(value, axis, steps):
    count = lax.axis_size(axis)
    leading, last = (max(0, -steps), min(count, count - steps))
    return lax.ppermute(value, axis, [(source, source + steps) for source in range(leading, last)])


def attend(query_g, key_g, value_g, grad_g, allowed):
    scale = query_g.shape[-1] ** (-0.5)
    scores = jnp.einsum("gqd,gkd->gqk", query_g, key_g, preferred_element_type=F32) * scale
    scores = jnp.where(allowed, scores, -1e30)
    peak = jnp.max(scores, axis=-1, keepdims=True)
    raised = jnp.where(allowed, jnp.exp(scores - peak), 0.0)
    probs = raised / jnp.sum(raised, axis=-1, keepdims=True)
    probs_low = probs.astype(BF)
    output = jnp.einsum("gqk,gkd->gqd", probs_low, value_g, preferred_element_type=F32).astype(BF)
    delta = jnp.sum(grad_g.astype(F32) * output.astype(F32), axis=-1, keepdims=True)
    dprobs = jnp.einsum("gqd,gkd->gqk", grad_g, value_g, preferred_element_type=F32)
    dscores = (probs * (dprobs - delta)).astype(BF)
    d_query = jnp.einsum("gqk,gkd->gqd", dscores, key_g, preferred_element_type=F32) * scale
    d_key = jnp.einsum("gqk,gqd->gkd", dscores, query_g, preferred_element_type=F32) * scale
    d_value = jnp.einsum("gqk,gqd->gkd", probs_low, grad_g, preferred_element_type=F32)
    return (output, d_query, d_key, d_value)


def band_mask(q_pos, k_pos, width):
    lower = (q_pos // BLK)[None, :, None] - width[:, None, None]
    causal = k_pos[None, None, :] <= q_pos[None, :, None]
    inside = k_pos[None, None, :] >= 0
    return causal & inside & ((k_pos // BLK)[None, None, :] >= lower)


def column_mask(count, reach):
    row_q = jnp.arange(count, dtype=jnp.int32)[None, :, None]
    row_k = jnp.arange(count, dtype=jnp.int32)[None, None, :]
    return (row_k <= row_q) & (row_q - row_k < reach[:, None, None])


def column_local(field, reach, devices):
    per_dev = IMW // devices
    count = field.shape[1] // per_dev
    grid = (
        field.reshape(4, count, per_dev, HS, HD)
        .transpose(0, 2, 3, 1, 4)
        .reshape(4, per_dev * HS, count, HD)
    )
    allowed = jnp.tile(column_mask(count, reach), (per_dev, 1, 1))
    output, d_query, d_key, d_value = attend(grid[0], grid[1], grid[2], grid[3], allowed)
    stacked = jnp.stack([output, d_query.astype(BF), d_key.astype(BF), d_value.astype(BF)])
    stacked = stacked.reshape(4, per_dev, HS, count, HD).transpose(0, 3, 1, 2, 4)
    return stacked.reshape(4, count * per_dev, 1, HS, HD)


def heads_first(field, count):
    return field.reshape(count, HB, HD).transpose(1, 0, 2)


def rows_first(field, count):
    return field.transpose(1, 0, 2).reshape(count, HB * HD)


def body_any(queries, keys, values, out_grad, out_weight, band_width, col_reach):
    query_all = queries[0]
    key_all = keys[0]
    value_all = values[0]
    grad_out = out_grad[0]
    rows = query_all.shape[0]
    devices = lax.axis_size("seq")
    place = lax.axis_index("seq")
    band_dim = HB * HD
    att_grad = jnp.einsum(
        "to,ao->ta",
        grad_out,
        lax.all_gather(out_weight, "dp", axis=0, tiled=True),
        preferred_element_type=F32,
    ).astype(BF)
    strided = jnp.stack([field[:, band_dim:] for field in (query_all, key_all, value_all, att_grad)])
    strided = strided.reshape(4, rows // devices, devices, HS, HD)
    column_major = lax.all_to_all(strided, "seq", split_axis=2, concat_axis=1, tiled=True)
    column_result = column_local(column_major, col_reach, devices)
    row_major = lax.all_to_all(
        column_result, "seq", split_axis=1, concat_axis=2, tiled=True
    ).reshape(4, rows, HS * HD)
    kv_own = (key_all[:, :band_dim], value_all[:, :band_dim])
    reach_dev = -(-(WMAX * BLK) // rows)
    earlier = []
    for hop in range(reach_dev, 0, -1):
        earlier.append(from_behind((kv_own[0], kv_own[1]), "seq", hop))
    key_window = jnp.concatenate([pair[0] for pair in earlier] + [kv_own[0]], 0)
    value_window = jnp.concatenate([pair[1] for pair in earlier] + [kv_own[1]], 0)
    width_all = (reach_dev + 1) * rows
    q_pos = place * rows + jnp.arange(rows, dtype=jnp.int32)
    k_pos = (place - reach_dev) * rows + jnp.arange(width_all, dtype=jnp.int32)
    allowed = band_mask(q_pos, k_pos, band_width)
    band_out, band_dq, band_dk, band_dv = attend(
        heads_first(query_all[:, :band_dim], rows),
        heads_first(key_window, width_all),
        heads_first(value_window, width_all),
        heads_first(att_grad[:, :band_dim], rows),
        allowed,
    )
    key_rows = rows_first(band_dk, width_all)
    value_rows = rows_first(band_dv, width_all)
    key_total = key_rows[reach_dev * rows :]
    value_total = value_rows[reach_dev * rows :]
    for hop in range(1, reach_dev + 1):
        slot = (reach_dev - hop) * rows
        key_total += from_behind(key_rows[slot : slot + rows].astype(BF), "seq", -hop).astype(F32)
        value_total += from_behind(value_rows[slot : slot + rows].astype(BF), "seq", -hop).astype(F32)
    attn_out = jnp.concatenate([rows_first(band_out, rows), row_major[0]], 1)
    query_grad = jnp.concatenate([rows_first(band_dq, rows).astype(BF), row_major[1]], 1)
    key_grad = jnp.concatenate([key_total.astype(BF), row_major[2]], 1)
    value_grad = jnp.concatenate([value_total.astype(BF), row_major[3]], 1)
    shared = lax.psum_scatter(
        jnp.einsum("ta,to->ao", attn_out, grad_out, preferred_element_type=F32).astype(BF),
        "dp",
        scatter_dimension=0,
        tiled=True,
    ).astype(F32)
    weight_grad = lax.psum(shared, "seq")
    return (query_grad[None], key_grad[None], value_grad[None], weight_grad.astype(BF))


def solution(mesh):
    def body(*args):
        rows = args[0].shape[1]
        devices = mesh.shape["seq"]
        g = IMW // rows
        fits = (
            mesh.shape["dp"] == 2
            and rows == BLK
            and devices == g * g
            and g == HB == HS == 4
            and WMAX * BLK == IMW
            and args[4].shape[0] == HB * HD == HS * HD
        )
        return body_roles(g, *args) if fits else body_any(*args)

    return jax.shard_map(
        body,
        mesh=mesh,
        in_specs=(
            P("dp", "seq", None),
            P("dp", "seq", None),
            P("dp", "seq", None),
            P("dp", "seq", None),
            P("dp", None),
            P(),
            P(),
        ),
        out_specs=(P("dp", "seq", None), P("dp", "seq", None), P("dp", "seq", None), P("dp", None)),
        check_vma=False,
    )
```

time: 102 us -> 85.7 us (0.84)
  waiting for transfers between devices: 40.4 us -> 27.9 us
  starting transfers between devices: 46.2 us -> 43.6 us
  local copies, waits for them, and re-layouts: 2.88 us -> 1.63 us
    ppermute x26 -> x27, waiting for transfers between devices: 39.1 us -> 25 us  [send(): return lax.ppermute(value, both, pairs)]
    ppermute x6 -> x9, starting transfers between devices: 10.7 us -> 3.87 us  [swap(): return lax.ppermute(value, 'dp', [(0, 1), (1, 0)])]
    ppermute x26 -> x27, starting transfers between devices: 35.4 us -> 39.7 us  [send(): return lax.ppermute(value, both, pairs)]
    unnamed x20 -> x12, local copies, waits for them, and re-layouts: 2.88 us -> 0.55 us
    ppermute x6 -> x9, waiting for transfers between devices: 1.28 us -> 2.86 us  [swap(): return lax.ppermute(value, 'dp', [(0, 1), (1, 0)])]
    dynamic_slice x0 -> x2, local copies, waits for them, and re-layouts: none -> 1.08 us  [body_roles(): lax.dynamic_slice(value, (0, (1 - role) * half), (rows, half))]
    pallas_call x13 -> x12, Pallas kernels: 11.7 us -> 11.4 us  [call(): pl.pallas_call(kernel, out_shape=outs, in_specs=[scalars] * smem + [vmem]...]
  transfers between devices with their start and end apart: 32 -> 36, of which waited for: 14 -> 16; matrix products, arithmetic and copies ran while one was open for 0% -> 0% of each run, Pallas kernels for 3% -> 12%
where the time goes in v2:
time: 85.7 us; the launch traced here: 85.5 us
  starting transfers between devices  43.6 us (51%)
  waiting for transfers between devices  27.9 us (33%)
  Pallas kernels  11.4 us (13%)
  local copies, waits for them, and re-layouts  1.63 us (2%)
  between operations  0.88 us (1%)
    ppermute x27, starting transfers between devices, send(): return lax.ppermute(value, both, pairs)  39.7 us
    ppermute x27, waiting for transfers between devices, send(): return lax.ppermute(value, both, pairs)  25 us
    pallas_call x12, Pallas kernels, call(): pl.pallas_call(kernel, out_shape=outs, in_specs=[scalars] * smem + [vmem]...  11.4 us
    ppermute x9, starting transfers between devices, swap(): return lax.ppermute(value, 'dp', [(0, 1), (1, 0)])  3.87 us
    ppermute x9, waiting for transfers between devices, swap(): return lax.ppermute(value, 'dp', [(0, 1), (1, 0)])  2.86 us
  transfers between devices with their start and end apart: 36, of which 16 were waited for; matrix products, arithmetic and copies ran while one was open for 0% of the time, Pallas kernels for 12%

profile of v2, /device:TPU:0, one launch (start us, length us, event | category | flops | bytes accessed | tf_op | source)
XLA Modules:
  0.0 85.5 jit_solution(10450742334225491487)
XLA Ops:
  0.7 1.0 %constant_dynamic-slice_fusion.2 = (bf16[1,128,512]{2,1,0:T(8,128)(2,1)S(1)}, bf16[1,128,512]{2,1,0:T(8,128)(2,1)S(1)}) fusion(bf16[1,128,1024]{2,1,0:T(8,128)(2,1)} %param.7, s32[]{:T(128)S(6)} %select_n.5, s32[]{:T(128)S(6)} %select_n.4), kind=kLoop, calls=%fused_computation.4 | loop fusion | bytes 524296 | tf_op jit(solution)/shard_map/dynamic_slice | solution.py:455
  1.7 0.1 copy-done.5
  1.8 0.0 copy-start
  1.9 0.5 collective-permute-start
  2.4 0.4 copy-done
  2.9 0.5 collective-permute-start.1
  3.4 1.1 %collective-permute-done.1.other_ref.og_other_ref = bf16[128,1024]{1,0:T(8,128)(2,1)S(1)} collective-permute-done((bf16[128,1024]{1,0:T(8,128)(2,1)S(1)}, bf16[128,1024]{1,0:T(8,128)(2,1)S(1)}, u32[]{:S(2)}, u32[]{:S(2)}) %collective-permute-start.1) | collective-permute-done | bytes 262176 | tf_op jit(solution)/shard_map/ppermute | solution.py:431
  4.5 0.8 att_grad.1.att_ref
  5.3 0.2 pack_fields.1
  5.5 2.9 %collective-permute-start.2 = (bf16[1024,128]{1,0:T(8,128)(2,1)S(1)}, bf16[1024,128]{1,0:T(8,128)(2,1)S(1)}, u32[]{:S(2)}, u32[]{:S(2)}) collective-permute-start(bf16[1024,128]{1,0:T(8,128)(2,1)S(1)} %get-tuple-element.39), channel_id=1, source_target_pairs={{0,1},{1,0},{2,3},{3,2},{4,5},{5,4},{6,7},{7,6},{8,9},{9,8},{10,11... | collective-permute-start | bytes 786440 | tf_op jit(solution)/shard_map/ppermute | solution.py:428
  8.4 1.5 %collective-permute-start.3 = (bf16[1024,128]{1,0:T(8,128)(2,1)S(1)}, bf16[1024,128]{1,0:T(8,128)(2,1)S(1)}, u32[]{:S(2)}, u32[]{:S(2)}) collective-permute-start(bf16[1024,128]{1,0:T(8,128)(2,1)S(1)} %get-tuple-element.40), channel_id=1, source_target_pairs={{0,2},{1,3},{2,0},{3,1},{4,6},{5,7},{6,4},{7,5},{8,10},{9,11},{10,... | collective-permute-start | bytes 786440 | tf_op jit(solution)/shard_map/ppermute | solution.py:428
  9.9 0.0 collective-permute-start.4
  10.0 1.9 %collective-permute-start.21 = (bf16[128,1024]{1,0:T(8,128)(2,1)S(1)}, bf16[128,1024]{1,0:T(8,128)(2,1)S(1)}, u32[]{:S(2)}, u32[]{:S(2)}) collective-permute-start(bf16[128,1024]{1,0:T(8,128)(2,1)S(1)} %bitcast.6), channel_id=1, source_target_pairs={{0,1},{1,0},{2,3},{3,2},{4,5},{5,4},{6,7},{7,6},{8,9},{9,8},{10,11... | collective-permute-start | bytes 786440 | tf_op jit(solution)/shard_map/ppermute | solution.py:428
  11.9 1.5 %collective-permute-start.22 = (bf16[128,1024]{1,0:T(8,128)(2,1)S(1)}, bf16[128,1024]{1,0:T(8,128)(2,1)S(1)}, u32[]{:S(2)}, u32[]{:S(2)}) collective-permute-start(bf16[128,1024]{1,0:T(8,128)(2,1)S(1)} %bitcast.7), channel_id=1, source_target_pairs={{0,2},{1,3},{2,0},{3,1},{4,6},{5,7},{6,4},{7,5},{8,10},{9,11},{10,... | collective-permute-start | bytes 786440 | tf_op jit(solution)/shard_map/ppermute | solution.py:428
  13.4 0.0 collective-permute-done.2.r1_ref
  13.4 2.3 %collective-permute-start.23 = (bf16[128,1024]{1,0:T(8,128)(2,1)S(1)}, bf16[128,1024]{1,0:T(8,128)(2,1)S(1)}, u32[]{:S(2)}, u32[]{:S(2)}) collective-permute-start(bf16[128,1024]{1,0:T(8,128)(2,1)S(1)} %bitcast.8), channel_id=1, source_target_pairs={{0,3},{1,2},{2,1},{3,0},{4,7},{5,6},{6,5},{7,4},{8,11},{9,10},{10,... | collective-permute-start | bytes 786440 | tf_op jit(solution)/shard_map/ppermute | solution.py:428
  15.8 0.6 collective-permute-done.3.r2_ref
  16.3 3.8 %collective-permute-done.4.r3_ref = bf16[1024,128]{1,0:T(8,128)(2,1)S(1)} collective-permute-done((bf16[1024,128]{1,0:T(8,128)(2,1)S(1)}, bf16[1024,128]{1,0:T(8,128)(2,1)S(1)}, u32[]{:S(2)}, u32[]{:S(2)}) %collective-permute-start.4) | collective-permute-done | bytes 262176 | tf_op jit(solution)/shard_map/ppermute | solution.py:428
  20.1 0.7 forward.1
  20.8 4.3 %collective-permute-start.5 = (bf16[2048,128]{1,0:T(8,128)(2,1)S(1)}, bf16[2048,128]{1,0:T(8,128)(2,1)S(1)}, u32[]{:S(2)}, u32[]{:S(2)}) collective-permute-start(bf16[2048,128]{1,0:T(8,128)(2,1)S(1)} %get-tuple-element.43.fkv_ref), channel_id=1, source_target_pairs={{0,4},{1,5},{2,6},{3,7},{4,8},{5,9},{6,10},{7,11},{8,12},{9,13},{1... | collective-permute-start | bytes 1572872 | tf_op jit(solution)/shard_map/ppermute | solution.py:428
  25.1 1.3 %collective-permute-start.6 = (bf16[2048,128]{1,0:T(8,128)(2,1)S(1)}, bf16[2048,128]{1,0:T(8,128)(2,1)S(1)}, u32[]{:S(2)}, u32[]{:S(2)}) collective-permute-start(bf16[2048,128]{1,0:T(8,128)(2,1)S(1)} %get-tuple-element.42.fqg_ref), channel_id=1, source_target_pairs={{4,0},{5,1},{6,2},{7,3},{8,4},{9,5},{10,6},{11,7},{12,8},{13,9},{1... | collective-permute-start | bytes 1572872 | tf_op jit(solution)/shard_map/ppermute | solution.py:428
  26.4 1.6 %collective-permute-start.15 = (bf16[256,128]{1,0:T(8,128)(2,1)S(1)}, bf16[256,128]{1,0:T(8,128)(2,1)S(1)}, u32[]{:S(2)}, u32[]{:S(2)}) collective-permute-start(bf16[256,128]{1,0:T(8,128)(2,1)S(1)} %get-tuple-element.59), channel_id=1, source_target_pairs={{0,1},{1,0},{2,3},{3,2},{4,5},{5,4},{6,7},{7,6},{8,9},{9,8},{10,11... | collective-permute-start | bytes 196616 | tf_op jit(solution)/shard_map/ppermute | solution.py:428
  28.0 0.9 %collective-permute-done.22.a2_ref = bf16[128,1024]{1,0:T(8,128)(2,1)S(1)} collective-permute-done((bf16[128,1024]{1,0:T(8,128)(2,1)S(1)}, bf16[128,1024]{1,0:T(8,128)(2,1)S(1)}, u32[]{:S(2)}, u32[]{:S(2)}) %collective-permute-start.22) | collective-permute-done | bytes 262176 | tf_op jit(solution)/shard_map/ppermute | solution.py:428
  28.8 1.5 %collective-permute-start.16 = (bf16[256,128]{1,0:T(8,128)(2,1)S(1)}, bf16[256,128]{1,0:T(8,128)(2,1)S(1)}, u32[]{:S(2)}, u32[]{:S(2)}) collective-permute-start(bf16[256,128]{1,0:T(8,128)(2,1)S(1)} %get-tuple-element.60), channel_id=1, source_target_pairs={{0,2},{1,3},{2,0},{3,1},{4,6},{5,7},{6,4},{7,5},{8,10},{9,11},{10,... | collective-permute-start | bytes 196616 | tf_op jit(solution)/shard_map/ppermute | solution.py:428
  30.4 0.4 collective-permute-done.15.o1_ref
  30.7 1.4 %collective-permute-start.17 = (bf16[256,128]{1,0:T(8,128)(2,1)S(1)}, bf16[256,128]{1,0:T(8,128)(2,1)S(1)}, u32[]{:S(2)}, u32[]{:S(2)}) collective-permute-start(bf16[256,128]{1,0:T(8,128)(2,1)S(1)} %get-tuple-element.61), channel_id=1, source_target_pairs={{0,3},{1,2},{2,1},{3,0},{4,7},{5,6},{6,5},{7,4},{8,11},{9,10},{10,... | collective-permute-start | bytes 196616 | tf_op jit(solution)/shard_map/ppermute | solution.py:428
  32.2 1.0 %collective-permute-done.16.o2_ref = bf16[256,128]{1,0:T(8,128)(2,1)S(1)} collective-permute-done((bf16[256,128]{1,0:T(8,128)(2,1)S(1)}, bf16[256,128]{1,0:T(8,128)(2,1)S(1)}, u32[]{:S(2)}, u32[]{:S(2)}) %collective-permute-start.16) | collective-permute-done | bytes 65568 | tf_op jit(solution)/shard_map/ppermute | solution.py:428
  33.1 1.1 %collective-permute-start.25 = (bf16[128,1024]{1,0:T(8,128)(2,1)S(1)}, bf16[128,1024]{1,0:T(8,128)(2,1)S(1)}, u32[]{:S(2)}, u32[]{:S(2)}) collective-permute-start(bf16[128,1024]{1,0:T(8,128)(2,1)S(1)} %collective-permute-done.22.a2_ref), channel_id=1, source_target_pairs={{0,16},{16,0},{1,17},{17,1},{2,18},{18,2},{3,19},{19,3},{4,20},{20... | collective-permute-start | bytes 786440 | tf_op jit(solution)/shard_map/ppermute | solution.py:431
  34.2 1.7 %collective-permute-done.17.o3_ref = bf16[256,128]{1,0:T(8,128)(2,1)S(1)} collective-permute-done((bf16[256,128]{1,0:T(8,128)(2,1)S(1)}, bf16[256,128]{1,0:T(8,128)(2,1)S(1)}, u32[]{:S(2)}, u32[]{:S(2)}) %collective-permute-start.17) | collective-permute-done | bytes 65568 | tf_op jit(solution)/shard_map/ppermute | solution.py:428
  35.9 0.7 collective-permute-start.26
  36.6 0.8 collective-permute-start.18
  37.5 0.5 collective-permute-start.19
  38.0 2.2 %collective-permute-start.20 = (bf16[256,128]{1,0:T(8,128)(2,1)S(1)}, bf16[256,128]{1,0:T(8,128)(2,1)S(1)}, u32[]{:S(2)}, u32[]{:S(2)}) collective-permute-start(bf16[256,128]{1,0:T(8,128)(2,1)S(1)} %get-tuple-element.65), channel_id=1, source_target_pairs={{0,3},{1,2},{2,1},{3,0},{4,7},{5,6},{6,5},{7,4},{8,11},{9,10},{10,... | collective-permute-start | bytes 196616 | tf_op jit(solution)/shard_map/ppermute | solution.py:428
  40.1 5.1 %attention.1 = (bf16[2,128,512]{2,1,0:T(8,128)(2,1)S(1)}, bf16[2,512,128]{2,1,0:T(8,128)(2,1)S(1)}, f32[2,2,512,128]{3,2,1,0:T(8,128)S(1)}, f32[16,512]{1,0:T(8,128)S(1)}) custom-call(s32[4]{0:T(128)S(1)} %copy-done.2, bf16[2048,128]{1,0:T(8,128)(2,1)S(1)} %get-tuple-element.42.fqg_ref, bf16[2048,128]{1,0:T(8,128)(2,1)S(1)} %get-tuple-element.43.fkv_ref, ...), custom_call_target="tpu_custom_call" | custom-call | bytes 36900 | tf_op jit(solution)/shard_map/attention/pallas_call | solution.py:47
  45.2 0.0 collective-permute-start.7
  45.3 0.7 weight.1
  46.0 2.1 %collective-permute-start.27 = (bf16[32,1024]{1,0:T(8,128)(2,1)S(1)}, bf16[32,1024]{1,0:T(8,128)(2,1)S(1)}, u32[]{:S(2)}, u32[]{:S(2)}) collective-permute-start(bf16[32,1024]{1,0:T(8,128)(2,1)S(1)} %get-tuple-element.67), channel_id=1, source_target_pairs={{0,4},{1,5},{2,6},{3,7},{4,0},{5,1},{6,2},{7,3},{8,12},{9,13},{10,... | collective-permute-start | bytes 196616 | tf_op jit(solution)/shard_map/ppermute | solution.py:428
  48.1 3.0 %collective-permute-start.28 = (bf16[32,1024]{1,0:T(8,128)(2,1)S(1)}, bf16[32,1024]{1,0:T(8,128)(2,1)S(1)}, u32[]{:S(2)}, u32[]{:S(2)}) collective-permute-start(bf16[32,1024]{1,0:T(8,128)(2,1)S(1)} %get-tuple-element.68), channel_id=1, source_target_pairs={{0,8},{1,9},{2,10},{3,11},{4,12},{5,13},{6,14},{7,15},{8,0},{9,1},... | collective-permute-start | bytes 196616 | tf_op jit(solution)/shard_map/ppermute | solution.py:428
  51.1 2.3 %tail.1.dkv_ref = f32[2,2,512,128]{3,2,1,0:T(8,128)S(1)} custom-call(s32[4]{0:T(128)S(1)} %copy-done.2, bf16[2048,128]{1,0:T(8,128)(2,1)S(1)} %get-tuple-element.43.fkv_ref, bf16[2048,128]{1,0:T(8,128)(2,1)S(1)} %collective-permute-done.6.order_ref.next_ref, f32[16,512]{1,0:T(8,128)S(1)} %collective-permute-done.7.stats_ref, ...), custom_call_target="tpu_custom_call" | custom-call | bytes 36900 | tf_op jit(solution)/shard_map/tail/pallas_call | solution.py:47
  53.4 0.1 pack_grads.1
  53.5 1.6 %collective-permute-start.8 = (bf16[768,128]{1,0:T(8,128)(2,1)S(1)}, bf16[768,128]{1,0:T(8,128)(2,1)S(1)}, u32[]{:S(2)}, u32[]{:S(2)}) collective-permute-start(bf16[768,128]{1,0:T(8,128)(2,1)S(1)} %get-tuple-element.49), channel_id=1, source_target_pairs={{0,1},{1,0},{2,3},{3,2},{4,5},{5,4},{6,7},{7,6},{8,9},{9,8},{10,11... | collective-permute-start | bytes 589832 | tf_op jit(solution)/shard_map/ppermute | solution.py:428
  55.0 0.5 collective-permute-start.9
  55.6 1.5 %collective-permute-start.10 = (bf16[768,128]{1,0:T(8,128)(2,1)S(1)}, bf16[768,128]{1,0:T(8,128)(2,1)S(1)}, u32[]{:S(2)}, u32[]{:S(2)}) collective-permute-start(bf16[768,128]{1,0:T(8,128)(2,1)S(1)} %get-tuple-element.51), channel_id=1, source_target_pairs={{0,3},{1,2},{2,1},{3,0},{4,7},{5,6},{6,5},{7,4},{8,11},{9,10},{10,... | collective-permute-start | bytes 589832 | tf_op jit(solution)/shard_map/ppermute | solution.py:428
  57.1 0.9 %collective-permute-done.29.z3_ref = bf16[32,1024]{1,0:T(8,128)(2,1)S(1)} collective-permute-done((bf16[32,1024]{1,0:T(8,128)(2,1)S(1)}, bf16[32,1024]{1,0:T(8,128)(2,1)S(1)}, u32[]{:S(2)}, u32[]{:S(2)}) %collective-permute-start.29) | collective-permute-done | bytes 65568 | tf_op jit(solution)/shard_map/ppermute | solution.py:428
  58.0 0.1 collective-permute-start.30
  58.1 1.9 %collective-permute-start.31 = (bf16[32,1024]{1,0:T(8,128)(2,1)S(1)}, bf16[32,1024]{1,0:T(8,128)(2,1)S(1)}, u32[]{:S(2)}, u32[]{:S(2)}) collective-permute-start(bf16[32,1024]{1,0:T(8,128)(2,1)S(1)} %sum.1.own_ref), channel_id=1, source_target_pairs={{0,8},{1,9},{2,10},{3,11},{4,12},{5,13},{6,14},{7,15},{8,0},{9,1},... | collective-permute-start | bytes 196616 | tf_op jit(solution)/shard_map/ppermute | solution.py:428
  60.0 4.1 %collective-permute-done.30.g1_ref = bf16[32,1024]{1,0:T(8,128)(2,1)S(1)} collective-permute-done((bf16[32,1024]{1,0:T(8,128)(2,1)S(1)}, bf16[32,1024]{1,0:T(8,128)(2,1)S(1)}, u32[]{:S(2)}, u32[]{:S(2)}) %collective-permute-start.30) | collective-permute-done | bytes 65568 | tf_op jit(solution)/shard_map/ppermute | solution.py:428
  64.1 1.8 %collective-permute-start.32 = (bf16[32,1024]{1,0:T(8,128)(2,1)S(1)}, bf16[32,1024]{1,0:T(8,128)(2,1)S(1)}, u32[]{:S(2)}, u32[]{:S(2)}) collective-permute-start(bf16[32,1024]{1,0:T(8,128)(2,1)S(1)} %sum.1.own_ref), channel_id=1, source_target_pairs={{0,12},{1,13},{2,14},{3,15},{4,8},{5,9},{6,10},{7,11},{8,4},{9,5},... | collective-permute-start | bytes 196616 | tf_op jit(solution)/shard_map/ppermute | solution.py:428
  65.9 0.3 collective-permute-done.31.g2_ref
  66.2 4.0 %collective-permute-done.32.g3_ref = bf16[32,1024]{1,0:T(8,128)(2,1)S(1)} collective-permute-done((bf16[32,1024]{1,0:T(8,128)(2,1)S(1)}, bf16[32,1024]{1,0:T(8,128)(2,1)S(1)}, u32[]{:S(2)}, u32[]{:S(2)}) %collective-permute-start.32) | collective-permute-done | bytes 65568 | tf_op jit(solution)/shard_map/ppermute | solution.py:428
  70.3 1.4 %collective-permute-start.33 = (bf16[128,1024]{1,0:T(8,128)(2,1)S(1)}, bf16[128,1024]{1,0:T(8,128)(2,1)S(1)}, u32[]{:S(2)}, u32[]{:S(2)}) collective-permute-start(bf16[128,1024]{1,0:T(8,128)(2,1)S(1)} %gather_line.1.r0_ref), channel_id=1, source_target_pairs={{0,1},{1,0},{2,3},{3,2},{4,5},{5,4},{6,7},{7,6},{8,9},{9,8},{10,11... | collective-permute-start | bytes 786440 | tf_op jit(solution)/shard_map/ppermute | solution.py:428
  71.7 0.5 collective-permute-start.34
  72.2 1.6 %collective-permute-start.35 = (bf16[128,1024]{1,0:T(8,128)(2,1)S(1)}, bf16[128,1024]{1,0:T(8,128)(2,1)S(1)}, u32[]{:S(2)}, u32[]{:S(2)}) collective-permute-start(bf16[128,1024]{1,0:T(8,128)(2,1)S(1)} %gather_line.1.r0_ref), channel_id=1, source_target_pairs={{0,3},{1,2},{2,1},{3,0},{4,7},{5,6},{6,5},{7,4},{8,11},{9,10},{10,... | collective-permute-start | bytes 786440 | tf_op jit(solution)/shard_map/ppermute | solution.py:428
  73.9 0.2 sort_grads.1
  74.0 0.1 collective-permute-start.11
  74.1 0.5 collective-permute-start.12
  74.6 0.8 collective-permute-done.11.b0_ref
  75.4 0.2 collective-permute-start.13
  75.6 0.4 collective-permute-start.14
  75.9 0.8 collective-permute-done.13.b2_ref
  76.7 0.2 collective-permute-done.14.b3_ref
  76.9 2.7 %collective-permute-done.33.r1_ref = bf16[128,1024]{1,0:T(8,128)(2,1)S(1)} collective-permute-done((bf16[128,1024]{1,0:T(8,128)(2,1)S(1)}, bf16[128,1024]{1,0:T(8,128)(2,1)S(1)}, u32[]{:S(2)}, u32[]{:S(2)}) %collective-permute-start.33) | collective-permute-done | bytes 262176 | tf_op jit(solution)/shard_map/ppermute | solution.py:428
  79.6 4.6 %collective-permute-done.34.r2_ref = bf16[128,1024]{1,0:T(8,128)(2,1)S(1)} collective-permute-done((bf16[128,1024]{1,0:T(8,128)(2,1)S(1)}, bf16[128,1024]{1,0:T(8,128)(2,1)S(1)}, u32[]{:S(2)}, u32[]{:S(2)}) %collective-permute-start.34) | collective-permute-done | bytes 262176 | tf_op jit(solution)/shard_map/ppermute | solution.py:428
  84.2 1.3 %finish.1 = (bf16[128,1024]{1,0:T(8,128)(2,1)}, bf16[128,1024]{1,0:T(8,128)(2,1)}, bf16[128,1024]{1,0:T(8,128)(2,1)}, bf16[512,1024]{1,0:T(8,128)(2,1)}) custom-call(bf16[3,128,512]{2,1,0:T(8,128)(2,1)S(1)} %get-tuple-element.52.own_ref, bf16[96,512]{1,0:T(8,128)(2,1)S(1)} %collective-permute-done.11.b0_ref, ...), custom_call_target="tpu_custom_call" | custom-call | bytes 36900 | tf_op jit(solution)/shard_map/finish/pallas_call | solution.py:47
  (36 shorter events, 0.3 us)
Async XLA Ops:
  0.6 1.1 %copy-start.4 = (bf16[1,128,1024]{2,1,0:T(8,128)(2,1)S(1)}, bf16[1,128,1024]{2,1,0:T(8,128)(2,1)}, u32[]{:S(2)}) copy-start(bf16[1,128,1024]{2,1,0:T(8,128)(2,1)} %param.9) | copy-start | bytes 786436
  0.6 1.1 %copy-start.5 = (bf16[1,128,1024]{2,1,0:T(8,128)(2,1)S(1)}, bf16[1,128,1024]{2,1,0:T(8,128)(2,1)}, u32[]{:S(2)}) copy-start(bf16[1,128,1024]{2,1,0:T(8,128)(2,1)} %param.8) | copy-start | bytes 786436
  1.8 2.7 %copy-start.1 = (bf16[512,1024]{1,0:T(8,128)(2,1)S(1)}, bf16[512,1024]{1,0:T(8,128)(2,1)}, u32[]{:S(2)}) copy-start(bf16[512,1024]{1,0:T(8,128)(2,1)} %weight_ref.1) | copy-start | bytes 3145732
  1.8 1.0 %copy-start = (bf16[1,128,1024]{2,1,0:T(8,128)(2,1)S(1)}, bf16[1,128,1024]{2,1,0:T(8,128)(2,1)}, u32[]{:S(2)}) copy-start(bf16[1,128,1024]{2,1,0:T(8,128)(2,1)} %param.10) | copy-start | bytes 786436
  1.9 3.4 %collective-permute-start = (bf16[3,128,512]{2,1,0:T(8,128)(2,1)S(1)}, bf16[3,128,512]{2,1,0:T(8,128)(2,1)S(1)}, u32[]{:S(2)}, u32[]{:S(2)}) collective-permute-start(bf16[3,128,512]{2,1,0:T(8,128)(2,1)S(1)} %pad_maximum_fusion.1), channel_id=1, source_target_pairs={{0,16},{16,0},{1,17},{17,1},{2,18},{18,2},{3,19},{19,3},{4,20},{20... | collective-permute-start | bytes 1179656 | tf_op jit(solution)/shard_map/ppermute | solution.py:431
  2.9 1.6 %collective-permute-start.1 = (bf16[128,1024]{1,0:T(8,128)(2,1)S(1)}, bf16[128,1024]{1,0:T(8,128)(2,1)S(1)}, u32[]{:S(2)}, u32[]{:S(2)}) collective-permute-start(bf16[128,1024]{1,0:T(8,128)(2,1)S(1)} %bitcast.4), channel_id=1, source_target_pairs={{0,16},{16,0},{1,17},{17,1},{2,18},{18,2},{3,19},{19,3},{4,20},{20... | collective-permute-start | bytes 786440 | tf_op jit(solution)/shard_map/ppermute | solution.py:431
  5.5 7.9 %collective-permute-start.2 = (bf16[1024,128]{1,0:T(8,128)(2,1)S(1)}, bf16[1024,128]{1,0:T(8,128)(2,1)S(1)}, u32[]{:S(2)}, u32[]{:S(2)}) collective-permute-start(bf16[1024,128]{1,0:T(8,128)(2,1)S(1)} %get-tuple-element.39), channel_id=1, source_target_pairs={{0,1},{1,0},{2,3},{3,2},{4,5},{5,4},{6,7},{7,6},{8,9},{9,8},{10,11... | collective-permute-start | bytes 786440 | tf_op jit(solution)/shard_map/ppermute | solution.py:428
  8.4 11.7 %copy-start.3 = (s32[4]{0:T(128)S(1)}, s32[4]{0:T(128)}, u32[]{:S(2)}) copy-start(s32[4]{0:T(128)} %reach_ref.1) | copy-start | bytes 52
  8.4 7.9 %collective-permute-start.3 = (bf16[1024,128]{1,0:T(8,128)(2,1)S(1)}, bf16[1024,128]{1,0:T(8,128)(2,1)S(1)}, u32[]{:S(2)}, u32[]{:S(2)}) collective-permute-start(bf16[1024,128]{1,0:T(8,128)(2,1)S(1)} %get-tuple-element.40), channel_id=1, source_target_pairs={{0,2},{1,3},{2,0},{3,1},{4,6},{5,7},{6,4},{7,5},{8,10},{9,11},{10,... | collective-permute-start | bytes 786440 | tf_op jit(solution)/shard_map/ppermute | solution.py:428
  9.9 10.2 %collective-permute-start.4 = (bf16[1024,128]{1,0:T(8,128)(2,1)S(1)}, bf16[1024,128]{1,0:T(8,128)(2,1)S(1)}, u32[]{:S(2)}, u32[]{:S(2)}) collective-permute-start(bf16[1024,128]{1,0:T(8,128)(2,1)S(1)} %get-tuple-element.41), channel_id=1, source_target_pairs={{0,3},{1,2},{2,1},{3,0},{4,7},{5,6},{6,5},{7,4},{8,11},{9,10},{10,... | collective-permute-start | bytes 786440 | tf_op jit(solution)/shard_map/ppermute | solution.py:428
  10.0 16.4 %collective-permute-start.21 = (bf16[128,1024]{1,0:T(8,128)(2,1)S(1)}, bf16[128,1024]{1,0:T(8,128)(2,1)S(1)}, u32[]{:S(2)}, u32[]{:S(2)}) collective-permute-start(bf16[128,1024]{1,0:T(8,128)(2,1)S(1)} %bitcast.6), channel_id=1, source_target_pairs={{0,1},{1,0},{2,3},{3,2},{4,5},{5,4},{6,7},{7,6},{8,9},{9,8},{10,11... | collective-permute-start | bytes 786440 | tf_op jit(solution)/shard_map/ppermute | solution.py:428
  11.9 16.9 %collective-permute-start.22 = (bf16[128,1024]{1,0:T(8,128)(2,1)S(1)}, bf16[128,1024]{1,0:T(8,128)(2,1)S(1)}, u32[]{:S(2)}, u32[]{:S(2)}) collective-permute-start(bf16[128,1024]{1,0:T(8,128)(2,1)S(1)} %bitcast.7), channel_id=1, source_target_pairs={{0,2},{1,3},{2,0},{3,1},{4,6},{5,7},{6,4},{7,5},{8,10},{9,11},{10,... | collective-permute-start | bytes 786440 | tf_op jit(solution)/shard_map/ppermute | solution.py:428
  13.4 16.9 %collective-permute-start.23 = (bf16[128,1024]{1,0:T(8,128)(2,1)S(1)}, bf16[128,1024]{1,0:T(8,128)(2,1)S(1)}, u32[]{:S(2)}, u32[]{:S(2)}) collective-permute-start(bf16[128,1024]{1,0:T(8,128)(2,1)S(1)} %bitcast.8), channel_id=1, source_target_pairs={{0,3},{1,2},{2,1},{3,0},{4,7},{5,6},{6,5},{7,4},{8,11},{9,10},{10,... | collective-permute-start | bytes 786440 | tf_op jit(solution)/shard_map/ppermute | solution.py:428
  20.8 16.7 %collective-permute-start.5 = (bf16[2048,128]{1,0:T(8,128)(2,1)S(1)}, bf16[2048,128]{1,0:T(8,128)(2,1)S(1)}, u32[]{:S(2)}, u32[]{:S(2)}) collective-permute-start(bf16[2048,128]{1,0:T(8,128)(2,1)S(1)} %get-tuple-element.43.fkv_ref), channel_id=1, source_target_pairs={{0,4},{1,5},{2,6},{3,7},{4,8},{5,9},{6,10},{7,11},{8,12},{9,13},{1... | collective-permute-start | bytes 1572872 | tf_op jit(solution)/shard_map/ppermute | solution.py:428
  25.1 12.9 %collective-permute-start.6 = (bf16[2048,128]{1,0:T(8,128)(2,1)S(1)}, bf16[2048,128]{1,0:T(8,128)(2,1)S(1)}, u32[]{:S(2)}, u32[]{:S(2)}) collective-permute-start(bf16[2048,128]{1,0:T(8,128)(2,1)S(1)} %get-tuple-element.42.fqg_ref), channel_id=1, source_target_pairs={{4,0},{5,1},{6,2},{7,3},{8,4},{9,5},{10,6},{11,7},{12,8},{13,9},{1... | collective-permute-start | bytes 1572872 | tf_op jit(solution)/shard_map/ppermute | solution.py:428
  26.4 4.3 %collective-permute-start.15 = (bf16[256,128]{1,0:T(8,128)(2,1)S(1)}, bf16[256,128]{1,0:T(8,128)(2,1)S(1)}, u32[]{:S(2)}, u32[]{:S(2)}) collective-permute-start(bf16[256,128]{1,0:T(8,128)(2,1)S(1)} %get-tuple-element.59), channel_id=1, source_target_pairs={{0,1},{1,0},{2,3},{3,2},{4,5},{5,4},{6,7},{7,6},{8,9},{9,8},{10,11... | collective-permute-start | bytes 196616 | tf_op jit(solution)/shard_map/ppermute | solution.py:428
  28.8 4.3 %collective-permute-start.16 = (bf16[256,128]{1,0:T(8,128)(2,1)S(1)}, bf16[256,128]{1,0:T(8,128)(2,1)S(1)}, u32[]{:S(2)}, u32[]{:S(2)}) collective-permute-start(bf16[256,128]{1,0:T(8,128)(2,1)S(1)} %get-tuple-element.60), channel_id=1, source_target_pairs={{0,2},{1,3},{2,0},{3,1},{4,6},{5,7},{6,4},{7,5},{8,10},{9,11},{10,... | collective-permute-start | bytes 196616 | tf_op jit(solution)/shard_map/ppermute | solution.py:428
  30.4 6.3 %collective-permute-start.24 = (bf16[128,1024]{1,0:T(8,128)(2,1)S(1)}, bf16[128,1024]{1,0:T(8,128)(2,1)S(1)}, u32[]{:S(2)}, u32[]{:S(2)}) collective-permute-start(bf16[128,1024]{1,0:T(8,128)(2,1)S(1)} %collective-permute-done.21.a1_ref), channel_id=1, source_target_pairs={{0,16},{16,0},{1,17},{17,1},{2,18},{18,2},{3,19},{19,3},{4,20},{20... | collective-permute-start | bytes 786440 | tf_op jit(solution)/shard_map/ppermute | solution.py:431
  30.7 5.2 %collective-permute-start.17 = (bf16[256,128]{1,0:T(8,128)(2,1)S(1)}, bf16[256,128]{1,0:T(8,128)(2,1)S(1)}, u32[]{:S(2)}, u32[]{:S(2)}) collective-permute-start(bf16[256,128]{1,0:T(8,128)(2,1)S(1)} %get-tuple-element.61), channel_id=1, source_target_pairs={{0,3},{1,2},{2,1},{3,0},{4,7},{5,6},{6,5},{7,4},{8,11},{9,10},{10,... | collective-permute-start | bytes 196616 | tf_op jit(solution)/shard_map/ppermute | solution.py:428
  33.1 12.1 %collective-permute-start.25 = (bf16[128,1024]{1,0:T(8,128)(2,1)S(1)}, bf16[128,1024]{1,0:T(8,128)(2,1)S(1)}, u32[]{:S(2)}, u32[]{:S(2)}) collective-permute-start(bf16[128,1024]{1,0:T(8,128)(2,1)S(1)} %collective-permute-done.22.a2_ref), channel_id=1, source_target_pairs={{0,16},{16,0},{1,17},{17,1},{2,18},{18,2},{3,19},{19,3},{4,20},{20... | collective-permute-start | bytes 786440 | tf_op jit(solution)/shard_map/ppermute | solution.py:431
  35.9 9.4 %collective-permute-start.26 = (bf16[128,1024]{1,0:T(8,128)(2,1)S(1)}, bf16[128,1024]{1,0:T(8,128)(2,1)S(1)}, u32[]{:S(2)}, u32[]{:S(2)}) collective-permute-start(bf16[128,1024]{1,0:T(8,128)(2,1)S(1)} %collective-permute-done.23.a3_ref), channel_id=1, source_target_pairs={{0,16},{16,0},{1,17},{17,1},{2,18},{18,2},{3,19},{19,3},{4,20},{20... | collective-permute-start | bytes 786440 | tf_op jit(solution)/shard_map/ppermute | solution.py:431
  36.6 8.6 %collective-permute-start.18 = (bf16[256,128]{1,0:T(8,128)(2,1)S(1)}, bf16[256,128]{1,0:T(8,128)(2,1)S(1)}, u32[]{:S(2)}, u32[]{:S(2)}) collective-permute-start(bf16[256,128]{1,0:T(8,128)(2,1)S(1)} %get-tuple-element.63), channel_id=1, source_target_pairs={{0,1},{1,0},{2,3},{3,2},{4,5},{5,4},{6,7},{7,6},{8,9},{9,8},{10,11... | collective-permute-start | bytes 196616 | tf_op jit(solution)/shard_map/ppermute | solution.py:428
  37.5 2.7 %copy-start.2 = (s32[4]{0:T(128)S(1)}, s32[4]{0:T(128)}, u32[]{:S(2)}) copy-start(s32[4]{0:T(128)} %width_ref.3) | copy-start | bytes 52
  37.5 7.8 %collective-permute-start.19 = (bf16[256,128]{1,0:T(8,128)(2,1)S(1)}, bf16[256,128]{1,0:T(8,128)(2,1)S(1)}, u32[]{:S(2)}, u32[]{:S(2)}) collective-permute-start(bf16[256,128]{1,0:T(8,128)(2,1)S(1)} %get-tuple-element.64), channel_id=1, source_target_pairs={{0,2},{1,3},{2,0},{3,1},{4,6},{5,7},{6,4},{7,5},{8,10},{9,11},{10,... | collective-permute-start | bytes 196616 | tf_op jit(solution)/shard_map/ppermute | solution.py:428
  38.0 7.3 %collective-permute-start.20 = (bf16[256,128]{1,0:T(8,128)(2,1)S(1)}, bf16[256,128]{1,0:T(8,128)(2,1)S(1)}, u32[]{:S(2)}, u32[]{:S(2)}) collective-permute-start(bf16[256,128]{1,0:T(8,128)(2,1)S(1)} %get-tuple-element.65), channel_id=1, source_target_pairs={{0,3},{1,2},{2,1},{3,0},{4,7},{5,6},{6,5},{7,4},{8,11},{9,10},{10,... | collective-permute-start | bytes 196616 | tf_op jit(solution)/shard_map/ppermute | solution.py:428
  45.2 5.8 %collective-permute-start.7 = (f32[16,512]{1,0:T(8,128)S(1)}, f32[16,512]{1,0:T(8,128)S(1)}, u32[]{:S(2)}, u32[]{:S(2)}) collective-permute-start(f32[16,512]{1,0:T(8,128)S(1)} %get-tuple-element.45), channel_id=1, source_target_pairs={{0,16},{1,17},{2,18},{3,19},{4,0},{5,1},{6,2},{7,3},{8,4},{9,5},{1... | collective-permute-start | bytes 98312 | tf_op jit(solution)/shard_map/ppermute | solution.py:428
  46.0 9.5 %collective-permute-start.27 = (bf16[32,1024]{1,0:T(8,128)(2,1)S(1)}, bf16[32,1024]{1,0:T(8,128)(2,1)S(1)}, u32[]{:S(2)}, u32[]{:S(2)}) collective-permute-start(bf16[32,1024]{1,0:T(8,128)(2,1)S(1)} %get-tuple-element.67), channel_id=1, source_target_pairs={{0,4},{1,5},{2,6},{3,7},{4,0},{5,1},{6,2},{7,3},{8,12},{9,13},{10,... | collective-permute-start | bytes 196616 | tf_op jit(solution)/shard_map/ppermute | solution.py:428
  48.1 9.0 %collective-permute-start.28 = (bf16[32,1024]{1,0:T(8,128)(2,1)S(1)}, bf16[32,1024]{1,0:T(8,128)(2,1)S(1)}, u32[]{:S(2)}, u32[]{:S(2)}) collective-permute-start(bf16[32,1024]{1,0:T(8,128)(2,1)S(1)} %get-tuple-element.68), channel_id=1, source_target_pairs={{0,8},{1,9},{2,10},{3,11},{4,12},{5,13},{6,14},{7,15},{8,0},{9,1},... | collective-permute-start | bytes 196616 | tf_op jit(solution)/shard_map/ppermute | solution.py:428
  51.1 6.9 %collective-permute-start.29 = (bf16[32,1024]{1,0:T(8,128)(2,1)S(1)}, bf16[32,1024]{1,0:T(8,128)(2,1)S(1)}, u32[]{:S(2)}, u32[]{:S(2)}) collective-permute-start(bf16[32,1024]{1,0:T(8,128)(2,1)S(1)} %get-tuple-element.69), channel_id=1, source_target_pairs={{0,12},{1,13},{2,14},{3,15},{4,8},{5,9},{6,10},{7,11},{8,4},{9,5},... | collective-permute-start | bytes 196616 | tf_op jit(solution)/shard_map/ppermute | solution.py:428
  53.5 18.7 %collective-permute-start.8 = (bf16[768,128]{1,0:T(8,128)(2,1)S(1)}, bf16[768,128]{1,0:T(8,128)(2,1)S(1)}, u32[]{:S(2)}, u32[]{:S(2)}) collective-permute-start(bf16[768,128]{1,0:T(8,128)(2,1)S(1)} %get-tuple-element.49), channel_id=1, source_target_pairs={{0,1},{1,0},{2,3},{3,2},{4,5},{5,4},{6,7},{7,6},{8,9},{9,8},{10,11... | collective-permute-start | bytes 589832 | tf_op jit(solution)/shard_map/ppermute | solution.py:428
  55.0 18.8 %collective-permute-start.9 = (bf16[768,128]{1,0:T(8,128)(2,1)S(1)}, bf16[768,128]{1,0:T(8,128)(2,1)S(1)}, u32[]{:S(2)}, u32[]{:S(2)}) collective-permute-start(bf16[768,128]{1,0:T(8,128)(2,1)S(1)} %get-tuple-element.50), channel_id=1, source_target_pairs={{0,2},{1,3},{2,0},{3,1},{4,6},{5,7},{6,4},{7,5},{8,10},{9,11},{10,... | collective-permute-start | bytes 589832 | tf_op jit(solution)/shard_map/ppermute | solution.py:428
  55.6 18.3 %collective-permute-start.10 = (bf16[768,128]{1,0:T(8,128)(2,1)S(1)}, bf16[768,128]{1,0:T(8,128)(2,1)S(1)}, u32[]{:S(2)}, u32[]{:S(2)}) collective-permute-start(bf16[768,128]{1,0:T(8,128)(2,1)S(1)} %get-tuple-element.51), channel_id=1, source_target_pairs={{0,3},{1,2},{2,1},{3,0},{4,7},{5,6},{6,5},{7,4},{8,11},{9,10},{10,... | collective-permute-start | bytes 589832 | tf_op jit(solution)/shard_map/ppermute | solution.py:428
  58.0 6.1 %collective-permute-start.30 = (bf16[32,1024]{1,0:T(8,128)(2,1)S(1)}, bf16[32,1024]{1,0:T(8,128)(2,1)S(1)}, u32[]{:S(2)}, u32[]{:S(2)}) collective-permute-start(bf16[32,1024]{1,0:T(8,128)(2,1)S(1)} %sum.1.own_ref), channel_id=1, source_target_pairs={{0,4},{1,5},{2,6},{3,7},{4,0},{5,1},{6,2},{7,3},{8,12},{9,13},{10,... | collective-permute-start | bytes 196616 | tf_op jit(solution)/shard_map/ppermute | solution.py:428
  58.1 8.1 %collective-permute-start.31 = (bf16[32,1024]{1,0:T(8,128)(2,1)S(1)}, bf16[32,1024]{1,0:T(8,128)(2,1)S(1)}, u32[]{:S(2)}, u32[]{:S(2)}) collective-permute-start(bf16[32,1024]{1,0:T(8,128)(2,1)S(1)} %sum.1.own_ref), channel_id=1, source_target_pairs={{0,8},{1,9},{2,10},{3,11},{4,12},{5,13},{6,14},{7,15},{8,0},{9,1},... | collective-permute-start | bytes 196616 | tf_op jit(solution)/shard_map/ppermute | solution.py:428
  64.1 6.2 %collective-permute-start.32 = (bf16[32,1024]{1,0:T(8,128)(2,1)S(1)}, bf16[32,1024]{1,0:T(8,128)(2,1)S(1)}, u32[]{:S(2)}, u32[]{:S(2)}) collective-permute-start(bf16[32,1024]{1,0:T(8,128)(2,1)S(1)} %sum.1.own_ref), channel_id=1, source_target_pairs={{0,12},{1,13},{2,14},{3,15},{4,8},{5,9},{6,10},{7,11},{8,4},{9,5},... | collective-permute-start | bytes 196616 | tf_op jit(solution)/shard_map/ppermute | solution.py:428
  70.3 9.3 %collective-permute-start.33 = (bf16[128,1024]{1,0:T(8,128)(2,1)S(1)}, bf16[128,1024]{1,0:T(8,128)(2,1)S(1)}, u32[]{:S(2)}, u32[]{:S(2)}) collective-permute-start(bf16[128,1024]{1,0:T(8,128)(2,1)S(1)} %gather_line.1.r0_ref), channel_id=1, source_target_pairs={{0,1},{1,0},{2,3},{3,2},{4,5},{5,4},{6,7},{7,6},{8,9},{9,8},{10,11... | collective-permute-start | bytes 786440 | tf_op jit(solution)/shard_map/ppermute | solution.py:428
  71.7 12.5 %collective-permute-start.34 = (bf16[128,1024]{1,0:T(8,128)(2,1)S(1)}, bf16[128,1024]{1,0:T(8,128)(2,1)S(1)}, u32[]{:S(2)}, u32[]{:S(2)}) collective-permute-start(bf16[128,1024]{1,0:T(8,128)(2,1)S(1)} %gather_line.1.r0_ref), channel_id=1, source_target_pairs={{0,2},{1,3},{2,0},{3,1},{4,6},{5,7},{6,4},{7,5},{8,10},{9,11},{10,... | collective-permute-start | bytes 786440 | tf_op jit(solution)/shard_map/ppermute | solution.py:428
  72.2 12.0 %collective-permute-start.35 = (bf16[128,1024]{1,0:T(8,128)(2,1)S(1)}, bf16[128,1024]{1,0:T(8,128)(2,1)S(1)}, u32[]{:S(2)}, u32[]{:S(2)}) collective-permute-start(bf16[128,1024]{1,0:T(8,128)(2,1)S(1)} %gather_line.1.r0_ref), channel_id=1, source_target_pairs={{0,3},{1,2},{2,1},{3,0},{4,7},{5,6},{6,5},{7,4},{8,11},{9,10},{10,... | collective-permute-start | bytes 786440 | tf_op jit(solution)/shard_map/ppermute | solution.py:428
  74.0 1.4 %collective-permute-start.11 = (bf16[96,512]{1,0:T(8,128)(2,1)S(1)}, bf16[96,512]{1,0:T(8,128)(2,1)S(1)}, u32[]{:S(2)}, u32[]{:S(2)}) collective-permute-start(bf16[96,512]{1,0:T(8,128)(2,1)S(1)} %get-tuple-element.53), channel_id=1, source_target_pairs={{0,16},{16,0},{1,17},{17,1},{2,18},{18,2},{3,19},{19,3},{4,20},{20... | collective-permute-start | bytes 294920 | tf_op jit(solution)/shard_map/ppermute | solution.py:431
  74.1 1.4 %collective-permute-start.12 = (bf16[96,512]{1,0:T(8,128)(2,1)S(1)}, bf16[96,512]{1,0:T(8,128)(2,1)S(1)}, u32[]{:S(2)}, u32[]{:S(2)}) collective-permute-start(bf16[96,512]{1,0:T(8,128)(2,1)S(1)} %get-tuple-element.54), channel_id=1, source_target_pairs={{0,16},{16,0},{1,17},{17,1},{2,18},{18,2},{3,19},{19,3},{4,20},{20... | collective-permute-start | bytes 294920 | tf_op jit(solution)/shard_map/ppermute | solution.py:431
  75.4 1.3 %collective-permute-start.13 = (bf16[96,512]{1,0:T(8,128)(2,1)S(1)}, bf16[96,512]{1,0:T(8,128)(2,1)S(1)}, u32[]{:S(2)}, u32[]{:S(2)}) collective-permute-start(bf16[96,512]{1,0:T(8,128)(2,1)S(1)} %get-tuple-element.55), channel_id=1, source_target_pairs={{0,16},{16,0},{1,17},{17,1},{2,18},{18,2},{3,19},{19,3},{4,20},{20... | collective-permute-start | bytes 294920 | tf_op jit(solution)/shard_map/ppermute | solution.py:431
  75.6 1.3 %collective-permute-start.14 = (bf16[96,512]{1,0:T(8,128)(2,1)S(1)}, bf16[96,512]{1,0:T(8,128)(2,1)S(1)}, u32[]{:S(2)}, u32[]{:S(2)}) collective-permute-start(bf16[96,512]{1,0:T(8,128)(2,1)S(1)} %get-tuple-element.56), channel_id=1, source_target_pairs={{0,16},{16,0},{1,17},{17,1},{2,18},{18,2},{3,19},{19,3},{4,20},{20... | collective-permute-start | bytes 294920 | tf_op jit(solution)/shard_map/ppermute | solution.py:431

commit v3 on v2

--- a/solution.py
+++ b/solution.py
@@ -40,20 +40,24 @@
     return jax.ShapeDtypeStruct(shape, dtype)
 
 
-def call(kernel, outs, args, smem=0, left=0, left_out=False, scratch=(), mib=16, us=0.01, name=None):
+def call(kernel, outs, args, smem=0, left_out=False, order=(), scratch=(), mib=16, name=None):
     vmem = pl.BlockSpec(memory_space=pltpu.VMEM)
+    scalars = pl.BlockSpec(memory_space=pltpu.SMEM)
     anywhere = pl.BlockSpec(memory_space=pl.ANY)
-    scalars = pl.BlockSpec(memory_space=pltpu.SMEM)
+    count = len(args)
+
+    def body(*refs):
+        kernel(*refs[:count], *refs[count + len(order) :])
+
     return pl.pallas_call(
-        kernel,
+        body,
         out_shape=outs,
-        in_specs=[scalars] * smem + [vmem] * (len(args) - smem - left) + [anywhere] * left,
+        in_specs=[scalars] * smem + [vmem] * (count - smem) + [anywhere] * len(order),
         out_specs=[anywhere if left_out else vmem] * len(outs),
         scratch_shapes=list(scratch),
         compiler_params=pltpu.CompilerParams(vmem_limit_bytes=mib * MIB),
-        cost_estimate=pl.CostEstimate(flops=0, bytes_accessed=int(us * 3.69e6), transcendentals=0),
         name=name,
-    )(*args)
+    )(*args, *order)
 
 
 def roles(band, strided):
@@ -206,7 +210,7 @@
     roles(lambda: None, strided)
 
 
-def attention_kernel(g, width_ref, fqg_ref, fkv_ref, halo_ref, order_ref,
+def attention_kernel(g, width_ref, fqg_ref, fkv_ref, halo_ref,
                      out_ref, dquery_ref, dkv_ref, stats_ref, key_s, value_s, key_t, value_t):
     line, spot_ = spot(g)
     span = dquery_ref.shape[1]
@@ -220,9 +224,9 @@
         near = (block >= WMAX - width) & (key_at - span <= query_at)
         for i in range(2):
             for t, ref in enumerate((key_s, value_s)):
-                here = slice((t * 2 + i) * span, (t * 2 + i + 1) * span)
-                ref[i, :span] = halo_ref[here]
-                ref[i, span:] = fkv_ref[here]
+                at = (t * 2 + i) * span
+                ref[i, span:] = fkv_ref[at : at + span]
+                ref[i, :span] = halo_ref[at : at + span]
             key_t[i] = key_s[i].T
             value_t[i] = value_s[i].T
         for b in reversed(range(g)):
@@ -269,7 +273,8 @@
                 mine = slice(b * rows, (b + 1) * rows)
                 for i in range(2):
                     query = next_ref[i * span + b * rows : i * span + (b + 1) * rows]
-                    grad = next_ref[(2 + i) * span + b * rows : (2 + i) * span + (b + 1) * rows]
+                    at = (2 + i) * span + b * rows
+                    grad = next_ref[at : at + rows]
                     key = fkv_ref[i * span + b * rows : (i + 1) * span]
                     value = fkv_ref[(2 + i) * span + b * rows : (3 + i) * span]
                     total = stats_ref[i * 8 : i * 8 + 1, mine]
@@ -282,14 +287,17 @@
     roles(band, lambda: None)
 
 
-def weight_kernel(g, out_ref, mine_ref, p1_ref, p2_ref, p3_ref, og_ref, og_other_ref,
-                  a1_ref, a2_ref, a3_ref, b1_ref, b2_ref, b3_ref, part_ref, z1_ref, z2_ref, z3_ref, sum_s):
+def copy_kernel(in_ref, out_ref):
+    out_ref[...] = in_ref[...]
+
+
+def weight_kernel(g, out_ref, *refs):
+    heads, (og_ref, og_other_ref), near = refs[:g], refs[g : g + 2], refs[g + 2 : -g - 1]
+    part_ref, z_refs, sum_s = refs[-g - 1], refs[-g:-1], refs[-1]
     line, spot_ = spot(g)
     rows = og_ref.shape[0]
     chunk = rows // g
-    heads = (mine_ref, p1_ref, p2_ref, p3_ref)
-
-    outer = ((og_ref, a1_ref, a2_ref, a3_ref), (og_other_ref, b1_ref, b2_ref, b3_ref))
+    outer = ((og_ref, *near[: g - 1]), (og_other_ref, *near[g - 1 :]))
 
     def add(part):
         sum_s[...] = sum(part(i, d) for i in range(2) for d in range(g))
@@ -299,64 +307,27 @@
         lambda: add(lambda i, d: tn(heads[d][i * rows : (i + 1) * rows], outer[i][d][...])),
     )
     part_ref[...] = sum_s[rows_at(line * chunk, chunk)]
-    for d, ref in enumerate((z1_ref, z2_ref, z3_ref), 1):
+    for d, ref in enumerate(z_refs, 1):
         ref[...] = sum_s[rows_at((line ^ d) * chunk, chunk)].astype(BF)
 
 
-def pack_grads_kernel(g, dquery_ref, dkv_ref, strided_ref, keep_ref, r1_ref, r2_ref, r3_ref):
-    line, spot_ = spot(g)
-    span = dquery_ref.shape[1]
-    rows = span // g
-    chunk = rows // g
-    outs = (keep_ref, r1_ref, r2_ref, r3_ref)
+def exchange_kernel(dquery_ref, dkv_ref, strided_ref, keep_ref, *rest):
+    piece_refs, send_s = rest[:-1], rest[-1]
 
     def band():
-        for d in range(g):
-            block = rows_at((spot_ ^ d) * rows, rows)
-            for i in range(2):
-                for t in range(3):
-                    value = dquery_ref[i, block] if t == 0 else dkv_ref[i, t - 1, block].astype(BF)
-                    outs[d][(i * 3 + t) * rows : (i * 3 + t + 1) * rows] = value
+        for i, ref in enumerate((keep_ref, send_s)):
+            ref[0] = dquery_ref[i]
+            ref[1] = dkv_ref[i, 0].astype(BF)
+            ref[2] = dkv_ref[i, 1].astype(BF)
 
     def strided():
-        for d in range(g):
-            for i in range(2):
-                for t in range(3):
-                    for h in range(HS):
-                        at = (i * 3 + t) * rows + h * chunk
-                        there = rows_at(h * rows + (line ^ d) * chunk, chunk)
-                        outs[d][at : at + chunk] = strided_ref[i, t, there]
+        keep_ref[...] = strided_ref[0]
+        send_s[...] = strided_ref[1]
 
     roles(band, strided)
-
-
-def sort_grads_kernel(g, keep_ref, r1_ref, r2_ref, r3_ref, own_ref, *rest):
-    line, spot_ = spot(g)
-    rows = own_ref.shape[1]
-    chunk = rows // g
-    came = (keep_ref, r1_ref, r2_ref, r3_ref)
-    piece_refs, other_s = rest[:-1], rest[-1]
-
-    def band():
-        for d in range(g):
-            lanes = rows_at((spot_ ^ d) * HD, HD)
-            for t in range(3):
-                own_ref[t, :, lanes] = came[d][t * rows : (t + 1) * rows]
-                other_s[t * rows : (t + 1) * rows, lanes] = came[d][(3 + t) * rows : (4 + t) * rows]
-
-    def strided():
-        for d in range(g):
-            for t in range(3):
-                for h in range(HS):
-                    lanes = slice(h * HD, (h + 1) * HD)
-                    at = t * rows + h * chunk
-                    own_ref[t, rows_at((line ^ d) * chunk, chunk), lanes] = came[d][at : at + chunk]
-                    there = rows_at(t * rows + (line ^ d) * chunk, chunk)
-                    other_s[there, lanes] = came[d][3 * rows + at : 3 * rows + at + chunk]
-
-    roles(band, strided)
+    size = piece_refs[0].shape[1]
     for n, ref in enumerate(piece_refs):
-        ref[...] = other_s[n * ref.shape[0] : (n + 1) * ref.shape[0]]
+        ref[...] = send_s[:, n * size : (n + 1) * size]
 
 
 def sum_kernel(keep_ref, z1_ref, z2_ref, z3_ref, out_ref):
@@ -366,44 +337,63 @@
     out_ref[...] = total.astype(BF)
 
 
-def gather_kernel(g, own_ref, g1_ref, g2_ref, g3_ref, out_ref):
-    line, _ = spot(g)
-    size = own_ref.shape[0]
+def gather_kernel(g, pieces, own_ref, g1_ref, g2_ref, g3_ref, keep_ref, *refs):
+    line, spot_ = spot(g)
+    swapped_refs, out_refs, swapped = refs[:pieces], refs[pieces:-1], refs[-1]
+    half_span = swapped_refs[0].shape[1]
+    for n, ref in enumerate(swapped_refs):
+        swapped[:, n * half_span : (n + 1) * half_span] = ref[...]
+    size, width = own_ref.shape
+    span = keep_ref.shape[1]
+    rows = span // g
+    chunk = rows // g
+    columns = width // HD
+    to_group, to_line = out_refs[:g], out_refs[g:]
     for d, ref in enumerate((own_ref, g1_ref, g2_ref, g3_ref)):
-        out_ref[rows_at((line ^ d) * size, size)] = ref[...]
-
-
-def finish_kernel(g, own_ref, b0_ref, b1_ref, b2_ref, b3_ref, r0_ref, r1_ref, r2_ref, r3_ref,
-                  dq_ref, dk_ref, dv_ref, weight_ref, sems):
-    _, spot_ = spot(g)
-    rows, half = own_ref.shape[1:]
-    size = r0_ref.shape[0]
-    pieces = (b0_ref, b1_ref, b2_ref, b3_ref)
-    outs = (dq_ref, dk_ref, dv_ref)
-    piece = b0_ref.shape[0]
-
-    def run(own_at, other_at):
-        copies = [
-            (ref, weight_ref.at[rows_at((spot_ ^ d) * size, size)])
-            for d, ref in enumerate((r0_ref, r1_ref, r2_ref, r3_ref))
-        ]
-        for t in range(3):
-            copies.append((own_ref.at[t], outs[t].at[:, pl.ds(own_at, half)]))
-        for n in range(4):
-            start, stop = n * piece, (n + 1) * piece
-            while start < stop:
-                t = start // rows
-                size_ = min(stop, (t + 1) * rows) - start
-                copies.append((pieces[n].at[pl.ds(start - n * piece, size_)],
-                               outs[t].at[pl.ds(start - t * rows, size_), pl.ds(other_at, half)]))
-                start += size_
-        copies = [pltpu.make_async_copy(src, dst, sems.at[n]) for n, (src, dst) in enumerate(copies)]
-        for copy in copies:
-            copy.start()
-        for copy in copies:
-            copy.wait()
-
-    roles(lambda: run(0, half), lambda: run(half, 0))
+        for n in range(columns):
+            for out_ref in to_group:
+                out_ref[rows_at(n * g * size + (line ^ d) * size, size)] = ref[:, n * HD : (n + 1) * HD]
+
+    def grads(band, strided):
+        for d in range(g):
+            for t in range(3):
+                at = columns * g * size + t * rows
+                to_group[d][at : at + rows] = band[t, rows_at((spot_ ^ d) * rows, rows)]
+                for h in range(HS):
+                    there = rows_at(h * rows + (line ^ d) * chunk, chunk)
+                    to_line[d][(t * HS + h) * chunk : (t * HS + h + 1) * chunk] = strided[t, there]
+
+    roles(lambda: grads(keep_ref, swapped), lambda: grads(swapped, keep_ref))
+
+
+def finish_kernel(g, *refs):
+    from_group, from_line = refs[:g], refs[g : 2 * g]
+    outs, weight_ref, grads_s, weight_s, sems = refs[2 * g : 2 * g + 3], *refs[2 * g + 3 :]
+    line, spot_ = spot(g)
+    rows, width = grads_s.shape[1:]
+    half = width // 2
+    chunk = rows // g
+    size = weight_s.shape[0] // g
+    columns = width // HD
+    copies = []
+    for t in range(3):
+        for d in range(g):
+            at = columns * size + t * rows
+            grads_s[t, :, rows_at((spot_ ^ d) * HD, HD)] = from_group[d][at : at + rows]
+            for h in range(HS):
+                lanes = slice(half + h * HD, half + (h + 1) * HD)
+                at = (t * HS + h) * chunk
+                grads_s[t, rows_at((line ^ d) * chunk, chunk), lanes] = from_line[d][at : at + chunk]
+        copies.append(pltpu.make_async_copy(grads_s.at[t], outs[t], sems.at[t]))
+        copies[-1].start()
+    for d in range(g):
+        there = rows_at((spot_ ^ d) * size, size)
+        for n in range(columns):
+            weight_s[there, n * HD : (n + 1) * HD] = from_group[d][n * size : (n + 1) * size]
+        copies.append(pltpu.make_async_copy(weight_s.at[there], weight_ref.at[there], sems.at[3 + d]))
+        copies[-1].start()
+    for copy in copies:
+        copy.wait()
 
 
 def body_roles(g, queries, keys, values, out_grad, out_weight, band_width, col_reach):
@@ -467,20 +457,21 @@
         + [shaped((2, HS, rows, HD)), shaped((2, 3, span, HD))],
         [col_reach, own, other, att] + came, smem=1, name="forward",
     )
+    back = [send(back[d - 1], by_role(d)) for d in steps]
     halo = send(fkv, shift(1))
-    following = send(fqg, shift(-1))
-    back = [send(back[d - 1], by_role(d)) for d in steps]
-    *to_heads, mine = call(functools.partial(heads_kernel, g), [shaped((2 * rows, HD))] * g,
-                           [keep] + back, name="heads")
-    heads = [send(to_heads[d - 1], in_group(d)) for d in steps]
+    *to_heads, mine = call(functools.partial(heads_kernel, g), [shaped((2 * rows, HD))] * g, [keep] + back,
+                           name="heads")
     band_out, dquery, dkv, stats = call(
         functools.partial(attention_kernel, g),
-        [shaped((2, HD, span)), shaped((2, span, HD)), shaped((2, 2, span, HD), F32), shaped((16, span), F32)],
-        [band_width, fqg, fkv, halo, following], smem=1, left=1,
+        [shaped((2, HD, span)), shaped((2, span, HD)), shaped((2, 2, span, HD), F32), shaped((48, span), F32)],
+        [band_width, fqg, fkv, halo], smem=1,
         scratch=[pltpu.VMEM((2, 2 * span, HD), BF), pltpu.VMEM((2, 2 * span, HD), BF),
                  pltpu.VMEM((2, HD, 2 * span), BF), pltpu.VMEM((2, HD, 2 * span), BF)],
         mib=24, name="attention",
     )
+    (fqg_copy,) = call(copy_kernel, [shaped(fqg.shape)], [fqg], name="copy")
+    following = send(fqg_copy, shift(-1))
+    heads = [send(to_heads[d - 1], in_group(d)) for d in steps]
     piece = half // g // g
     parts = call(
         functools.partial(weight_kernel, g), [shaped((piece, width), F32)] + [shaped((piece, width))] * (g - 1),
@@ -490,22 +481,26 @@
     summed = [send(parts[d], along_line(d)) for d in steps]
     stats = send(stats, ring(-1))
     (dkv,) = call(functools.partial(tail_kernel, g), [shaped(dkv.shape, F32)],
-                  [band_width, fkv, following, stats, dkv], smem=1, name="tail")
-    (piece_sum,) = call(sum_kernel, [shaped((piece, width))], [parts[0]] + summed, name="sum")
+                  [band_width, fkv, following, stats, dkv], smem=1, order=[summed[-1]], name="tail")
+    (piece_sum,) = call(sum_kernel, [shaped((piece, width))], [parts[0]] + summed, order=[dkv], name="sum")
     pieces = [send(piece_sum, along_line(d)) for d in steps]
-    (head_rows,) = call(functools.partial(gather_kernel, g), [shaped((half // g, width))],
-                        [piece_sum] + pieces, name="gather_line")
-    others = [send(head_rows, in_group(d)) for d in steps]
-    returned = call(functools.partial(pack_grads_kernel, g), [shaped((6 * rows, HD))] * g,
-                    [dquery, dkv, strided_grads], name="pack_grads")
-    returned = [returned[0]] + [send(returned[d], by_role(d)) for d in steps]
-    own, *to_other = call(functools.partial(sort_grads_kernel, g),
-                          [shaped((3, rows, half))] + [shaped((3 * rows // 4, half))] * 4, returned,
-                          scratch=[pltpu.VMEM((3 * rows, half), BF)], name="sort_grads")
+    grads_kept, *to_other = call(
+        exchange_kernel, [shaped((3, span, HD))] + [shaped((3, span // 2, HD))] * 2,
+        [dquery, dkv, strided_grads], order=[piece_sum], scratch=[pltpu.VMEM((3, span, HD), BF)], name="exchange",
+    )
+    packed = call(
+        functools.partial(gather_kernel, g, len(to_other)),
+        [shaped((half // g * width // HD + 3 * rows, HD))] * g + [shaped((3 * rows, HD))] * g,
+        [piece_sum] + pieces + [grads_kept] + [swap(value) for value in to_other],
+        scratch=[pltpu.VMEM((3, span, HD), BF)], name="gather_line",
+    )
+    from_group = [packed[0]] + [send(packed[d], in_group(d)) for d in steps]
+    from_line = [packed[g]] + [send(packed[g + d], along_line(d)) for d in steps]
     dq, dk, dv, weight_grad = call(
         functools.partial(finish_kernel, g), [shaped((rows, width))] * 3 + [shaped((half, width))],
-        [own] + [swap(value) for value in to_other] + [head_rows] + others, left_out=True,
-        scratch=[pltpu.SemaphoreType.DMA((g + 12,))], name="finish",
+        from_group + from_line, left_out=True,
+        scratch=[pltpu.VMEM((3, rows, width), BF), pltpu.VMEM((half, width), BF), pltpu.SemaphoreType.DMA((3 + g,))],
+        name="finish",
     )
     return dq[None], dk[None], dv[None], weight_grad
 

time: 85.7 us -> 83.8 us (0.978)
  waiting for transfers between devices: 27.9 us -> 25.8 us
    ppermute x9 -> x7, waiting for transfers between devices: 2.86 us -> 1.13 us  [swap(): return lax.ppermute(value, 'dp', [(0, 1), (1, 0)])]
    ppermute x9 -> x7, starting transfers between devices: 3.87 us -> 3.55 us  [swap(): return lax.ppermute(value, 'dp', [(0, 1), (1, 0)])]
  transfers between devices with their start and end apart: 36 -> 34, of which waited for: 16 -> 14; matrix products, arithmetic and copies ran while one was open for 0% -> 0% of each run, Pallas kernels for 12% -> 12%
where the time goes in v3:
time: 83.8 us; the launch traced here: 83.6 us
  starting transfers between devices  43.6 us (52%)
  waiting for transfers between devices  25.8 us (31%)
  Pallas kernels  11.6 us (14%)
  local copies, waits for them, and re-layouts  1.63 us (2%)
  between operations  0.88 us (1%)
    ppermute x27, starting transfers between devices, send(): return lax.ppermute(value, both, pairs)  40 us
    ppermute x27, waiting for transfers between devices, send(): return lax.ppermute(value, both, pairs)  24.7 us
    pallas_call x12, Pallas kernels, call(): pl.pallas_call(body, out_shape=outs, in_specs=[scalars] * smem + [vmem] *...  11.6 us
    ppermute x7, starting transfers between devices, swap(): return lax.ppermute(value, 'dp', [(0, 1), (1, 0)])  3.55 us
  transfers between devices with their start and end apart: 34, of which 14 were waited for; matrix products, arithmetic and copies ran while one was open for 0% of the time, Pallas kernels for 12%

profile of v3, /device:TPU:0, one launch (start us, length us, event | category | flops | bytes accessed | tf_op | source)
XLA Modules:
  0.0 83.6 jit_solution(8777921637837506502)
XLA Ops:
  0.7 1.0 %constant_dynamic-slice_fusion.2 = (bf16[1,128,512]{2,1,0:T(8,128)(2,1)S(1)}, bf16[1,128,512]{2,1,0:T(8,128)(2,1)S(1)}) fusion(bf16[1,128,1024]{2,1,0:T(8,128)(2,1)} %param.7, s32[]{:T(128)S(6)} %select_n.5, s32[]{:T(128)S(6)} %select_n.4), kind=kLoop, calls=%fused_computation.4 | loop fusion | bytes 524296 | tf_op jit(solution)/shard_map/dynamic_slice | solution.py:445
  1.7 0.1 copy-done.5
  1.8 0.0 copy-start
  1.9 0.5 collective-permute-start
  2.4 0.4 copy-done
  2.9 0.5 collective-permute-start.1
  3.4 1.1 %collective-permute-done.1.refs_1_.refs_6_ = bf16[128,1024]{1,0:T(8,128)(2,1)S(1)} collective-permute-done((bf16[128,1024]{1,0:T(8,128)(2,1)S(1)}, bf16[128,1024]{1,0:T(8,128)(2,1)S(1)}, u32[]{:S(2)}, u32[]{:S(2)}) %collective-permute-start.1) | collective-permute-done | bytes 262176 | tf_op jit(solution)/shard_map/ppermute | solution.py:421
  4.5 0.8 att_grad.1.refs_2_.refs_3_
  5.3 0.2 pack_fields.1
  5.5 2.9 %collective-permute-start.2 = (bf16[1024,128]{1,0:T(8,128)(2,1)S(1)}, bf16[1024,128]{1,0:T(8,128)(2,1)S(1)}, u32[]{:S(2)}, u32[]{:S(2)}) collective-permute-start(bf16[1024,128]{1,0:T(8,128)(2,1)S(1)} %get-tuple-element.41), channel_id=1, source_target_pairs={{0,1},{1,0},{2,3},{3,2},{4,5},{5,4},{6,7},{7,6},{8,9},{9,8},{10,11... | collective-permute-start | bytes 786440 | tf_op jit(solution)/shard_map/ppermute | solution.py:418
  8.4 1.5 %collective-permute-start.3 = (bf16[1024,128]{1,0:T(8,128)(2,1)S(1)}, bf16[1024,128]{1,0:T(8,128)(2,1)S(1)}, u32[]{:S(2)}, u32[]{:S(2)}) collective-permute-start(bf16[1024,128]{1,0:T(8,128)(2,1)S(1)} %get-tuple-element.42), channel_id=1, source_target_pairs={{0,2},{1,3},{2,0},{3,1},{4,6},{5,7},{6,4},{7,5},{8,10},{9,11},{10,... | collective-permute-start | bytes 786440 | tf_op jit(solution)/shard_map/ppermute | solution.py:418
  9.9 0.0 collective-permute-start.4
  10.0 1.9 %collective-permute-start.12 = (bf16[128,1024]{1,0:T(8,128)(2,1)S(1)}, bf16[128,1024]{1,0:T(8,128)(2,1)S(1)}, u32[]{:S(2)}, u32[]{:S(2)}) collective-permute-start(bf16[128,1024]{1,0:T(8,128)(2,1)S(1)} %bitcast.6), channel_id=1, source_target_pairs={{0,1},{1,0},{2,3},{3,2},{4,5},{5,4},{6,7},{7,6},{8,9},{9,8},{10,11... | collective-permute-start | bytes 786440 | tf_op jit(solution)/shard_map/ppermute | solution.py:418
  11.9 1.5 %collective-permute-start.13 = (bf16[128,1024]{1,0:T(8,128)(2,1)S(1)}, bf16[128,1024]{1,0:T(8,128)(2,1)S(1)}, u32[]{:S(2)}, u32[]{:S(2)}) collective-permute-start(bf16[128,1024]{1,0:T(8,128)(2,1)S(1)} %bitcast.7), channel_id=1, source_target_pairs={{0,2},{1,3},{2,0},{3,1},{4,6},{5,7},{6,4},{7,5},{8,10},{9,11},{10,... | collective-permute-start | bytes 786440 | tf_op jit(solution)/shard_map/ppermute | solution.py:418
  13.4 0.0 collective-permute-done.2.refs_4_
  13.4 2.3 %collective-permute-start.14 = (bf16[128,1024]{1,0:T(8,128)(2,1)S(1)}, bf16[128,1024]{1,0:T(8,128)(2,1)S(1)}, u32[]{:S(2)}, u32[]{:S(2)}) collective-permute-start(bf16[128,1024]{1,0:T(8,128)(2,1)S(1)} %bitcast.8), channel_id=1, source_target_pairs={{0,3},{1,2},{2,1},{3,0},{4,7},{5,6},{6,5},{7,4},{8,11},{9,10},{10,... | collective-permute-start | bytes 786440 | tf_op jit(solution)/shard_map/ppermute | solution.py:418
  15.8 0.6 collective-permute-done.3.refs_5_
  16.3 3.8 %collective-permute-done.4.refs_6_ = bf16[1024,128]{1,0:T(8,128)(2,1)S(1)} collective-permute-done((bf16[1024,128]{1,0:T(8,128)(2,1)S(1)}, bf16[1024,128]{1,0:T(8,128)(2,1)S(1)}, u32[]{:S(2)}, u32[]{:S(2)}) %collective-permute-start.4) | collective-permute-done | bytes 262176 | tf_op jit(solution)/shard_map/ppermute | solution.py:418
  20.1 0.7 forward.1
  20.8 4.3 %collective-permute-start.5 = (bf16[2048,128]{1,0:T(8,128)(2,1)S(1)}, bf16[2048,128]{1,0:T(8,128)(2,1)S(1)}, u32[]{:S(2)}, u32[]{:S(2)}) collective-permute-start(bf16[2048,128]{1,0:T(8,128)(2,1)S(1)} %get-tuple-element.45.refs_2_.refs_1_), channel_id=1, source_target_pairs={{0,4},{1,5},{2,6},{3,7},{4,8},{5,9},{6,10},{7,11},{8,12},{9,13},{1... | collective-permute-start | bytes 1572872 | tf_op jit(solution)/shard_map/ppermute | solution.py:418
  25.1 1.3 %collective-permute-start.21 = (bf16[2048,128]{1,0:T(8,128)(2,1)S(1)}, bf16[2048,128]{1,0:T(8,128)(2,1)S(1)}, u32[]{:S(2)}, u32[]{:S(2)}) collective-permute-start(bf16[2048,128]{1,0:T(8,128)(2,1)S(1)} %copy.12), channel_id=1, source_target_pairs={{4,0},{5,1},{6,2},{7,3},{8,4},{9,5},{10,6},{11,7},{12,8},{13,9},{1... | collective-permute-start | bytes 1572872 | tf_op jit(solution)/shard_map/ppermute | solution.py:418
  26.4 0.0 collective-permute-done.12.refs_7_
  26.4 1.6 %collective-permute-start.6 = (bf16[256,128]{1,0:T(8,128)(2,1)S(1)}, bf16[256,128]{1,0:T(8,128)(2,1)S(1)}, u32[]{:S(2)}, u32[]{:S(2)}) collective-permute-start(bf16[256,128]{1,0:T(8,128)(2,1)S(1)} %get-tuple-element.48), channel_id=1, source_target_pairs={{0,1},{1,0},{2,3},{3,2},{4,5},{5,4},{6,7},{7,6},{8,9},{9,8},{10,11... | collective-permute-start | bytes 196616 | tf_op jit(solution)/shard_map/ppermute | solution.py:418
  28.0 0.8 collective-permute-done.13.refs_8_
  28.8 1.5 %collective-permute-start.7 = (bf16[256,128]{1,0:T(8,128)(2,1)S(1)}, bf16[256,128]{1,0:T(8,128)(2,1)S(1)}, u32[]{:S(2)}, u32[]{:S(2)}) collective-permute-start(bf16[256,128]{1,0:T(8,128)(2,1)S(1)} %get-tuple-element.49), channel_id=1, source_target_pairs={{0,2},{1,3},{2,0},{3,1},{4,6},{5,7},{6,4},{7,5},{8,10},{9,11},{10,... | collective-permute-start | bytes 196616 | tf_op jit(solution)/shard_map/ppermute | solution.py:418
  30.4 0.0 collective-permute-done.14.refs_9_
  30.4 0.0 collective-permute-start.8
  30.4 0.4 collective-permute-done.6.refs_1_
  30.8 1.2 %collective-permute-start.15 = (bf16[128,1024]{1,0:T(8,128)(2,1)S(1)}, bf16[128,1024]{1,0:T(8,128)(2,1)S(1)}, u32[]{:S(2)}, u32[]{:S(2)}) collective-permute-start(bf16[128,1024]{1,0:T(8,128)(2,1)S(1)} %collective-permute-done.12.refs_7_), channel_id=1, source_target_pairs={{0,16},{16,0},{1,17},{17,1},{2,18},{18,2},{3,19},{19,3},{4,20},{20... | collective-permute-start | bytes 786440 | tf_op jit(solution)/shard_map/ppermute | solution.py:421
  32.0 1.1 %collective-permute-done.7.refs_2_ = bf16[256,128]{1,0:T(8,128)(2,1)S(1)} collective-permute-done((bf16[256,128]{1,0:T(8,128)(2,1)S(1)}, bf16[256,128]{1,0:T(8,128)(2,1)S(1)}, u32[]{:S(2)}, u32[]{:S(2)}) %collective-permute-start.7) | collective-permute-done | bytes 65568 | tf_op jit(solution)/shard_map/ppermute | solution.py:418
  33.1 0.6 collective-permute-start.16
  33.7 1.8 %collective-permute-done.8.refs_3_ = bf16[256,128]{1,0:T(8,128)(2,1)S(1)} collective-permute-done((bf16[256,128]{1,0:T(8,128)(2,1)S(1)}, bf16[256,128]{1,0:T(8,128)(2,1)S(1)}, u32[]{:S(2)}, u32[]{:S(2)}) %collective-permute-start.8) | collective-permute-done | bytes 65568 | tf_op jit(solution)/shard_map/ppermute | solution.py:418
  35.5 0.2 collective-permute-start.17
  35.8 0.0 collective-permute-done.15.refs_10_
  35.8 1.5 %collective-permute-start.10 = (bf16[256,128]{1,0:T(8,128)(2,1)S(1)}, bf16[256,128]{1,0:T(8,128)(2,1)S(1)}, u32[]{:S(2)}, u32[]{:S(2)}) collective-permute-start(bf16[256,128]{1,0:T(8,128)(2,1)S(1)} %get-tuple-element.53), channel_id=1, source_target_pairs={{0,2},{1,3},{2,0},{3,1},{4,6},{5,7},{6,4},{7,5},{8,10},{9,11},{10,... | collective-permute-start | bytes 196616 | tf_op jit(solution)/shard_map/ppermute | solution.py:418
  37.3 0.3 collective-permute-start.11
  37.6 1.7 %collective-permute-start.9 = (bf16[256,128]{1,0:T(8,128)(2,1)S(1)}, bf16[256,128]{1,0:T(8,128)(2,1)S(1)}, u32[]{:S(2)}, u32[]{:S(2)}) collective-permute-start(bf16[256,128]{1,0:T(8,128)(2,1)S(1)} %get-tuple-element.52), channel_id=1, source_target_pairs={{0,1},{1,0},{2,3},{3,2},{4,5},{5,4},{6,7},{7,6},{8,9},{9,8},{10,11... | collective-permute-start | bytes 196616 | tf_op jit(solution)/shard_map/ppermute | solution.py:418
  39.3 5.1 %attention.1 = (bf16[2,128,512]{2,1,0:T(8,128)(2,1)S(1)}, bf16[2,512,128]{2,1,0:T(8,128)(2,1)S(1)}, f32[2,2,512,128]{3,2,1,0:T(8,128)S(1)}, f32[48,512]{1,0:T(8,128)S(1)}) custom-call(s32[4]{0:T(128)S(1)} %copy-done.2, bf16[2048,128]{1,0:T(8,128)(2,1)S(1)} %get-tuple-element.44.refs_1_.refs_0_, bf16[2048,128]{1,0:T(8,128)(2,1)S(1)} %get-tuple-element.45.refs_2_.refs_1_, ...), custom_call_target="tpu_custom_call" | custom-call | tf_op jit(solution)/shard_map/attention/pallas_call | solution.py:52
  44.4 0.0 collective-permute-start.22
  44.4 0.8 weight.1
  45.2 3.9 %collective-permute-start.20 = (bf16[32,1024]{1,0:T(8,128)(2,1)S(1)}, bf16[32,1024]{1,0:T(8,128)(2,1)S(1)}, u32[]{:S(2)}, u32[]{:S(2)}) collective-permute-start(bf16[32,1024]{1,0:T(8,128)(2,1)S(1)} %get-tuple-element.58), channel_id=1, source_target_pairs={{0,12},{1,13},{2,14},{3,15},{4,8},{5,9},{6,10},{7,11},{8,4},{9,5},... | collective-permute-start | bytes 196616 | tf_op jit(solution)/shard_map/ppermute | solution.py:418
  49.1 0.6 collective-permute-start.19
  49.7 3.4 %collective-permute-done.20.refs_5_.refs_3_ = bf16[32,1024]{1,0:T(8,128)(2,1)S(1)} collective-permute-done((bf16[32,1024]{1,0:T(8,128)(2,1)S(1)}, bf16[32,1024]{1,0:T(8,128)(2,1)S(1)}, u32[]{:S(2)}, u32[]{:S(2)}) %collective-permute-start.20) | collective-permute-done | bytes 65568 | tf_op jit(solution)/shard_map/ppermute | solution.py:418
  53.2 2.3 %tail.1.refs_4_.refs_1_ = f32[2,2,512,128]{3,2,1,0:T(8,128)S(1)} custom-call(s32[4]{0:T(128)S(1)} %copy-done.2, bf16[2048,128]{1,0:T(8,128)(2,1)S(1)} %get-tuple-element.45.refs_2_.refs_1_, bf16[2048,128]{1,0:T(8,128)(2,1)S(1)} %collective-permute-done.21.refs_2_, f32[48,512]{1,0:T(8,128)S(1)} %collective-permute-done.22.refs_3_, ...), custom_call_target="tpu_custom_call" | custom-call | tf_op jit(solution)/shard_map/tail/pallas_call | solution.py:52
  55.5 0.1 exchange.1
  55.7 0.1 collective-permute-start.26
  55.7 0.5 collective-permute-start.27
  56.2 0.8 collective-permute-start.23
  57.0 1.4 %collective-permute-start.24 = (bf16[32,1024]{1,0:T(8,128)(2,1)S(1)}, bf16[32,1024]{1,0:T(8,128)(2,1)S(1)}, u32[]{:S(2)}, u32[]{:S(2)}) collective-permute-start(bf16[32,1024]{1,0:T(8,128)(2,1)S(1)} %sum.1.refs_3_.refs_0_), channel_id=1, source_target_pairs={{0,8},{1,9},{2,10},{3,11},{4,12},{5,13},{6,14},{7,15},{8,0},{9,1},... | collective-permute-start | bytes 196616 | tf_op jit(solution)/shard_map/ppermute | solution.py:418
  58.4 2.2 %collective-permute-start.25 = (bf16[32,1024]{1,0:T(8,128)(2,1)S(1)}, bf16[32,1024]{1,0:T(8,128)(2,1)S(1)}, u32[]{:S(2)}, u32[]{:S(2)}) collective-permute-start(bf16[32,1024]{1,0:T(8,128)(2,1)S(1)} %sum.1.refs_3_.refs_0_), channel_id=1, source_target_pairs={{0,12},{1,13},{2,14},{3,15},{4,8},{5,9},{6,10},{7,11},{8,4},{9,5},... | collective-permute-start | bytes 196616 | tf_op jit(solution)/shard_map/ppermute | solution.py:418
  60.6 0.6 collective-permute-done.23.refs_1_
  61.2 4.1 %collective-permute-done.24.refs_2_ = bf16[32,1024]{1,0:T(8,128)(2,1)S(1)} collective-permute-done((bf16[32,1024]{1,0:T(8,128)(2,1)S(1)}, bf16[32,1024]{1,0:T(8,128)(2,1)S(1)}, u32[]{:S(2)}, u32[]{:S(2)}) %collective-permute-start.24) | collective-permute-done | bytes 65568 | tf_op jit(solution)/shard_map/ppermute | solution.py:418
  65.3 0.3 gather_line.1
  65.6 0.6 collective-permute-start.28
  66.2 1.4 %collective-permute-start.29 = (bf16[1408,128]{1,0:T(8,128)(2,1)S(1)}, bf16[1408,128]{1,0:T(8,128)(2,1)S(1)}, u32[]{:S(2)}, u32[]{:S(2)}) collective-permute-start(bf16[1408,128]{1,0:T(8,128)(2,1)S(1)} %get-tuple-element.68), channel_id=1, source_target_pairs={{0,2},{1,3},{2,0},{3,1},{4,6},{5,7},{6,4},{7,5},{8,10},{9,11},{10,... | collective-permute-start | bytes 1081352 | tf_op jit(solution)/shard_map/ppermute | solution.py:418
  67.6 1.6 %collective-permute-start.30 = (bf16[1408,128]{1,0:T(8,128)(2,1)S(1)}, bf16[1408,128]{1,0:T(8,128)(2,1)S(1)}, u32[]{:S(2)}, u32[]{:S(2)}) collective-permute-start(bf16[1408,128]{1,0:T(8,128)(2,1)S(1)} %get-tuple-element.69), channel_id=1, source_target_pairs={{0,3},{1,2},{2,1},{3,0},{4,7},{5,6},{6,5},{7,4},{8,11},{9,10},{10,... | collective-permute-start | bytes 1081352 | tf_op jit(solution)/shard_map/ppermute | solution.py:418
  69.1 1.3 %collective-permute-start.31 = (bf16[384,128]{1,0:T(8,128)(2,1)S(1)}, bf16[384,128]{1,0:T(8,128)(2,1)S(1)}, u32[]{:S(2)}, u32[]{:S(2)}) collective-permute-start(bf16[384,128]{1,0:T(8,128)(2,1)S(1)} %get-tuple-element.71), channel_id=1, source_target_pairs={{0,4},{1,5},{2,6},{3,7},{4,0},{5,1},{6,2},{7,3},{8,12},{9,13},{10,... | collective-permute-start | bytes 294920 | tf_op jit(solution)/shard_map/ppermute | solution.py:418
  70.4 1.3 %collective-permute-start.32 = (bf16[384,128]{1,0:T(8,128)(2,1)S(1)}, bf16[384,128]{1,0:T(8,128)(2,1)S(1)}, u32[]{:S(2)}, u32[]{:S(2)}) collective-permute-start(bf16[384,128]{1,0:T(8,128)(2,1)S(1)} %get-tuple-element.72), channel_id=1, source_target_pairs={{0,8},{1,9},{2,10},{3,11},{4,12},{5,13},{6,14},{7,15},{8,0},{9,1},... | collective-permute-start | bytes 294920 | tf_op jit(solution)/shard_map/ppermute | solution.py:418
  71.7 2.4 %collective-permute-done.31.refs_5_ = bf16[384,128]{1,0:T(8,128)(2,1)S(1)} collective-permute-done((bf16[384,128]{1,0:T(8,128)(2,1)S(1)}, bf16[384,128]{1,0:T(8,128)(2,1)S(1)}, u32[]{:S(2)}, u32[]{:S(2)}) %collective-permute-start.31) | collective-permute-done | bytes 98336 | tf_op jit(solution)/shard_map/ppermute | solution.py:418
  74.1 2.5 %collective-permute-start.33 = (bf16[384,128]{1,0:T(8,128)(2,1)S(1)}, bf16[384,128]{1,0:T(8,128)(2,1)S(1)}, u32[]{:S(2)}, u32[]{:S(2)}) collective-permute-start(bf16[384,128]{1,0:T(8,128)(2,1)S(1)} %get-tuple-element.73), channel_id=1, source_target_pairs={{0,12},{1,13},{2,14},{3,15},{4,8},{5,9},{6,10},{7,11},{8,4},{9,5},... | collective-permute-start | bytes 294920 | tf_op jit(solution)/shard_map/ppermute | solution.py:418
  76.6 1.9 %collective-permute-done.32.refs_6_ = bf16[384,128]{1,0:T(8,128)(2,1)S(1)} collective-permute-done((bf16[384,128]{1,0:T(8,128)(2,1)S(1)}, bf16[384,128]{1,0:T(8,128)(2,1)S(1)}, u32[]{:S(2)}, u32[]{:S(2)}) %collective-permute-start.32) | collective-permute-done | bytes 98336 | tf_op jit(solution)/shard_map/ppermute | solution.py:418
  78.5 2.1 %collective-permute-done.33.refs_7_ = bf16[384,128]{1,0:T(8,128)(2,1)S(1)} collective-permute-done((bf16[384,128]{1,0:T(8,128)(2,1)S(1)}, bf16[384,128]{1,0:T(8,128)(2,1)S(1)}, u32[]{:S(2)}, u32[]{:S(2)}) %collective-permute-start.33) | collective-permute-done | bytes 98336 | tf_op jit(solution)/shard_map/ppermute | solution.py:418
  80.6 1.6 %collective-permute-done.30.refs_3_ = bf16[1408,128]{1,0:T(8,128)(2,1)S(1)} collective-permute-done((bf16[1408,128]{1,0:T(8,128)(2,1)S(1)}, bf16[1408,128]{1,0:T(8,128)(2,1)S(1)}, u32[]{:S(2)}, u32[]{:S(2)}) %collective-permute-start.30) | collective-permute-done | bytes 360480 | tf_op jit(solution)/shard_map/ppermute | solution.py:418
  82.3 1.3 %finish.1 = (bf16[128,1024]{1,0:T(8,128)(2,1)}, bf16[128,1024]{1,0:T(8,128)(2,1)}, bf16[128,1024]{1,0:T(8,128)(2,1)}, bf16[512,1024]{1,0:T(8,128)(2,1)}) custom-call(bf16[1408,128]{1,0:T(8,128)(2,1)S(1)} %get-tuple-element.66.refs_0_, bf16[1408,128]{1,0:T(8,128)(2,1)S(1)} %collective-permute-done.28.refs_1_, ...), custom_call_target="tpu_custom_call" | custom-call | tf_op jit(solution)/shard_map/finish/pallas_call | solution.py:52
  (32 shorter events, 0.3 us)
Async XLA Ops:
  0.6 1.1 %copy-start.4 = (bf16[1,128,1024]{2,1,0:T(8,128)(2,1)S(1)}, bf16[1,128,1024]{2,1,0:T(8,128)(2,1)}, u32[]{:S(2)}) copy-start(bf16[1,128,1024]{2,1,0:T(8,128)(2,1)} %param.9) | copy-start | bytes 786436
  0.6 1.1 %copy-start.5 = (bf16[1,128,1024]{2,1,0:T(8,128)(2,1)S(1)}, bf16[1,128,1024]{2,1,0:T(8,128)(2,1)}, u32[]{:S(2)}) copy-start(bf16[1,128,1024]{2,1,0:T(8,128)(2,1)} %param.8) | copy-start | bytes 786436
  1.8 2.7 %copy-start.1 = (bf16[512,1024]{1,0:T(8,128)(2,1)S(1)}, bf16[512,1024]{1,0:T(8,128)(2,1)}, u32[]{:S(2)}) copy-start(bf16[512,1024]{1,0:T(8,128)(2,1)} %refs_2_.1) | copy-start | bytes 3145732
  1.8 1.0 %copy-start = (bf16[1,128,1024]{2,1,0:T(8,128)(2,1)S(1)}, bf16[1,128,1024]{2,1,0:T(8,128)(2,1)}, u32[]{:S(2)}) copy-start(bf16[1,128,1024]{2,1,0:T(8,128)(2,1)} %param.10) | copy-start | bytes 786436
  1.9 3.4 %collective-permute-start = (bf16[3,128,512]{2,1,0:T(8,128)(2,1)S(1)}, bf16[3,128,512]{2,1,0:T(8,128)(2,1)S(1)}, u32[]{:S(2)}, u32[]{:S(2)}) collective-permute-start(bf16[3,128,512]{2,1,0:T(8,128)(2,1)S(1)} %pad_maximum_fusion.1), channel_id=1, source_target_pairs={{0,16},{16,0},{1,17},{17,1},{2,18},{18,2},{3,19},{19,3},{4,20},{20... | collective-permute-start | bytes 1179656 | tf_op jit(solution)/shard_map/ppermute | solution.py:421
  2.9 1.6 %collective-permute-start.1 = (bf16[128,1024]{1,0:T(8,128)(2,1)S(1)}, bf16[128,1024]{1,0:T(8,128)(2,1)S(1)}, u32[]{:S(2)}, u32[]{:S(2)}) collective-permute-start(bf16[128,1024]{1,0:T(8,128)(2,1)S(1)} %bitcast.4), channel_id=1, source_target_pairs={{0,16},{16,0},{1,17},{17,1},{2,18},{18,2},{3,19},{19,3},{4,20},{20... | collective-permute-start | bytes 786440 | tf_op jit(solution)/shard_map/ppermute | solution.py:421
  5.5 7.9 %collective-permute-start.2 = (bf16[1024,128]{1,0:T(8,128)(2,1)S(1)}, bf16[1024,128]{1,0:T(8,128)(2,1)S(1)}, u32[]{:S(2)}, u32[]{:S(2)}) collective-permute-start(bf16[1024,128]{1,0:T(8,128)(2,1)S(1)} %get-tuple-element.41), channel_id=1, source_target_pairs={{0,1},{1,0},{2,3},{3,2},{4,5},{5,4},{6,7},{7,6},{8,9},{9,8},{10,11... | collective-permute-start | bytes 786440 | tf_op jit(solution)/shard_map/ppermute | solution.py:418
  8.4 11.7 %copy-start.3 = (s32[4]{0:T(128)S(1)}, s32[4]{0:T(128)}, u32[]{:S(2)}) copy-start(s32[4]{0:T(128)} %refs_0_.3) | copy-start | bytes 52
  8.4 7.9 %collective-permute-start.3 = (bf16[1024,128]{1,0:T(8,128)(2,1)S(1)}, bf16[1024,128]{1,0:T(8,128)(2,1)S(1)}, u32[]{:S(2)}, u32[]{:S(2)}) collective-permute-start(bf16[1024,128]{1,0:T(8,128)(2,1)S(1)} %get-tuple-element.42), channel_id=1, source_target_pairs={{0,2},{1,3},{2,0},{3,1},{4,6},{5,7},{6,4},{7,5},{8,10},{9,11},{10,... | collective-permute-start | bytes 786440 | tf_op jit(solution)/shard_map/ppermute | solution.py:418
  9.9 10.2 %collective-permute-start.4 = (bf16[1024,128]{1,0:T(8,128)(2,1)S(1)}, bf16[1024,128]{1,0:T(8,128)(2,1)S(1)}, u32[]{:S(2)}, u32[]{:S(2)}) collective-permute-start(bf16[1024,128]{1,0:T(8,128)(2,1)S(1)} %get-tuple-element.43), channel_id=1, source_target_pairs={{0,3},{1,2},{2,1},{3,0},{4,7},{5,6},{6,5},{7,4},{8,11},{9,10},{10,... | collective-permute-start | bytes 786440 | tf_op jit(solution)/shard_map/ppermute | solution.py:418
  10.0 16.5 %collective-permute-start.12 = (bf16[128,1024]{1,0:T(8,128)(2,1)S(1)}, bf16[128,1024]{1,0:T(8,128)(2,1)S(1)}, u32[]{:S(2)}, u32[]{:S(2)}) collective-permute-start(bf16[128,1024]{1,0:T(8,128)(2,1)S(1)} %bitcast.6), channel_id=1, source_target_pairs={{0,1},{1,0},{2,3},{3,2},{4,5},{5,4},{6,7},{7,6},{8,9},{9,8},{10,11... | collective-permute-start | bytes 786440 | tf_op jit(solution)/shard_map/ppermute | solution.py:418
  11.9 16.9 %collective-permute-start.13 = (bf16[128,1024]{1,0:T(8,128)(2,1)S(1)}, bf16[128,1024]{1,0:T(8,128)(2,1)S(1)}, u32[]{:S(2)}, u32[]{:S(2)}) collective-permute-start(bf16[128,1024]{1,0:T(8,128)(2,1)S(1)} %bitcast.7), channel_id=1, source_target_pairs={{0,2},{1,3},{2,0},{3,1},{4,6},{5,7},{6,4},{7,5},{8,10},{9,11},{10,... | collective-permute-start | bytes 786440 | tf_op jit(solution)/shard_map/ppermute | solution.py:418
  13.4 16.9 %collective-permute-start.14 = (bf16[128,1024]{1,0:T(8,128)(2,1)S(1)}, bf16[128,1024]{1,0:T(8,128)(2,1)S(1)}, u32[]{:S(2)}, u32[]{:S(2)}) collective-permute-start(bf16[128,1024]{1,0:T(8,128)(2,1)S(1)} %bitcast.8), channel_id=1, source_target_pairs={{0,3},{1,2},{2,1},{3,0},{4,7},{5,6},{6,5},{7,4},{8,11},{9,10},{10,... | collective-permute-start | bytes 786440 | tf_op jit(solution)/shard_map/ppermute | solution.py:418
  20.8 16.8 %collective-permute-start.5 = (bf16[2048,128]{1,0:T(8,128)(2,1)S(1)}, bf16[2048,128]{1,0:T(8,128)(2,1)S(1)}, u32[]{:S(2)}, u32[]{:S(2)}) collective-permute-start(bf16[2048,128]{1,0:T(8,128)(2,1)S(1)} %get-tuple-element.45.refs_2_.refs_1_), channel_id=1, source_target_pairs={{0,4},{1,5},{2,6},{3,7},{4,8},{5,9},{6,10},{7,11},{8,12},{9,13},{1... | collective-permute-start | bytes 1572872 | tf_op jit(solution)/shard_map/ppermute | solution.py:418
  25.1 24.6 %collective-permute-start.21 = (bf16[2048,128]{1,0:T(8,128)(2,1)S(1)}, bf16[2048,128]{1,0:T(8,128)(2,1)S(1)}, u32[]{:S(2)}, u32[]{:S(2)}) collective-permute-start(bf16[2048,128]{1,0:T(8,128)(2,1)S(1)} %copy.12), channel_id=1, source_target_pairs={{4,0},{5,1},{6,2},{7,3},{8,4},{9,5},{10,6},{11,7},{12,8},{13,9},{1... | collective-permute-start | bytes 1572872 | tf_op jit(solution)/shard_map/ppermute | solution.py:418
  26.4 4.3 %collective-permute-start.6 = (bf16[256,128]{1,0:T(8,128)(2,1)S(1)}, bf16[256,128]{1,0:T(8,128)(2,1)S(1)}, u32[]{:S(2)}, u32[]{:S(2)}) collective-permute-start(bf16[256,128]{1,0:T(8,128)(2,1)S(1)} %get-tuple-element.48), channel_id=1, source_target_pairs={{0,1},{1,0},{2,3},{3,2},{4,5},{5,4},{6,7},{7,6},{8,9},{9,8},{10,11... | collective-permute-start | bytes 196616 | tf_op jit(solution)/shard_map/ppermute | solution.py:418
  28.8 4.3 %collective-permute-start.7 = (bf16[256,128]{1,0:T(8,128)(2,1)S(1)}, bf16[256,128]{1,0:T(8,128)(2,1)S(1)}, u32[]{:S(2)}, u32[]{:S(2)}) collective-permute-start(bf16[256,128]{1,0:T(8,128)(2,1)S(1)} %get-tuple-element.49), channel_id=1, source_target_pairs={{0,2},{1,3},{2,0},{3,1},{4,6},{5,7},{6,4},{7,5},{8,10},{9,11},{10,... | collective-permute-start | bytes 196616 | tf_op jit(solution)/shard_map/ppermute | solution.py:418
  30.4 5.2 %collective-permute-start.8 = (bf16[256,128]{1,0:T(8,128)(2,1)S(1)}, bf16[256,128]{1,0:T(8,128)(2,1)S(1)}, u32[]{:S(2)}, u32[]{:S(2)}) collective-permute-start(bf16[256,128]{1,0:T(8,128)(2,1)S(1)} %get-tuple-element.50), channel_id=1, source_target_pairs={{0,3},{1,2},{2,1},{3,0},{4,7},{5,6},{6,5},{7,4},{8,11},{9,10},{10,... | collective-permute-start | bytes 196616 | tf_op jit(solution)/shard_map/ppermute | solution.py:418
  30.8 5.0 %collective-permute-start.15 = (bf16[128,1024]{1,0:T(8,128)(2,1)S(1)}, bf16[128,1024]{1,0:T(8,128)(2,1)S(1)}, u32[]{:S(2)}, u32[]{:S(2)}) collective-permute-start(bf16[128,1024]{1,0:T(8,128)(2,1)S(1)} %collective-permute-done.12.refs_7_), channel_id=1, source_target_pairs={{0,16},{16,0},{1,17},{17,1},{2,18},{18,2},{3,19},{19,3},{4,20},{20... | collective-permute-start | bytes 786440 | tf_op jit(solution)/shard_map/ppermute | solution.py:421
  33.1 4.2 %collective-permute-start.16 = (bf16[128,1024]{1,0:T(8,128)(2,1)S(1)}, bf16[128,1024]{1,0:T(8,128)(2,1)S(1)}, u32[]{:S(2)}, u32[]{:S(2)}) collective-permute-start(bf16[128,1024]{1,0:T(8,128)(2,1)S(1)} %collective-permute-done.13.refs_8_), channel_id=1, source_target_pairs={{0,16},{16,0},{1,17},{17,1},{2,18},{18,2},{3,19},{19,3},{4,20},{20... | collective-permute-start | bytes 786440 | tf_op jit(solution)/shard_map/ppermute | solution.py:421
  35.5 8.8 %collective-permute-start.17 = (bf16[128,1024]{1,0:T(8,128)(2,1)S(1)}, bf16[128,1024]{1,0:T(8,128)(2,1)S(1)}, u32[]{:S(2)}, u32[]{:S(2)}) collective-permute-start(bf16[128,1024]{1,0:T(8,128)(2,1)S(1)} %collective-permute-done.14.refs_9_), channel_id=1, source_target_pairs={{0,16},{16,0},{1,17},{17,1},{2,18},{18,2},{3,19},{19,3},{4,20},{20... | collective-permute-start | bytes 786440 | tf_op jit(solution)/shard_map/ppermute | solution.py:421
  35.8 8.6 %collective-permute-start.10 = (bf16[256,128]{1,0:T(8,128)(2,1)S(1)}, bf16[256,128]{1,0:T(8,128)(2,1)S(1)}, u32[]{:S(2)}, u32[]{:S(2)}) collective-permute-start(bf16[256,128]{1,0:T(8,128)(2,1)S(1)} %get-tuple-element.53), channel_id=1, source_target_pairs={{0,2},{1,3},{2,0},{3,1},{4,6},{5,7},{6,4},{7,5},{8,10},{9,11},{10,... | collective-permute-start | bytes 196616 | tf_op jit(solution)/shard_map/ppermute | solution.py:418
  37.3 2.0 %copy-start.2 = (s32[4]{0:T(128)S(1)}, s32[4]{0:T(128)}, u32[]{:S(2)}) copy-start(s32[4]{0:T(128)} %refs_0_.5) | copy-start | bytes 52
  37.3 7.1 %collective-permute-start.11 = (bf16[256,128]{1,0:T(8,128)(2,1)S(1)}, bf16[256,128]{1,0:T(8,128)(2,1)S(1)}, u32[]{:S(2)}, u32[]{:S(2)}) collective-permute-start(bf16[256,128]{1,0:T(8,128)(2,1)S(1)} %get-tuple-element.54), channel_id=1, source_target_pairs={{0,3},{1,2},{2,1},{3,0},{4,7},{5,6},{6,5},{7,4},{8,11},{9,10},{10,... | collective-permute-start | bytes 196616 | tf_op jit(solution)/shard_map/ppermute | solution.py:418
  37.6 6.8 %collective-permute-start.9 = (bf16[256,128]{1,0:T(8,128)(2,1)S(1)}, bf16[256,128]{1,0:T(8,128)(2,1)S(1)}, u32[]{:S(2)}, u32[]{:S(2)}) collective-permute-start(bf16[256,128]{1,0:T(8,128)(2,1)S(1)} %get-tuple-element.52), channel_id=1, source_target_pairs={{0,1},{1,0},{2,3},{3,2},{4,5},{5,4},{6,7},{7,6},{8,9},{9,8},{10,11... | collective-permute-start | bytes 196616 | tf_op jit(solution)/shard_map/ppermute | solution.py:418
  44.4 8.8 %collective-permute-start.22 = (f32[48,512]{1,0:T(8,128)S(1)}, f32[48,512]{1,0:T(8,128)S(1)}, u32[]{:S(2)}, u32[]{:S(2)}) collective-permute-start(f32[48,512]{1,0:T(8,128)S(1)} %get-tuple-element.59), channel_id=1, source_target_pairs={{0,16},{1,17},{2,18},{3,19},{4,0},{5,1},{6,2},{7,3},{8,4},{9,5},{1... | collective-permute-start | bytes 294920 | tf_op jit(solution)/shard_map/ppermute | solution.py:418
  45.2 8.0 %collective-permute-start.20 = (bf16[32,1024]{1,0:T(8,128)(2,1)S(1)}, bf16[32,1024]{1,0:T(8,128)(2,1)S(1)}, u32[]{:S(2)}, u32[]{:S(2)}) collective-permute-start(bf16[32,1024]{1,0:T(8,128)(2,1)S(1)} %get-tuple-element.58), channel_id=1, source_target_pairs={{0,12},{1,13},{2,14},{3,15},{4,8},{5,9},{6,10},{7,11},{8,4},{9,5},... | collective-permute-start | bytes 196616 | tf_op jit(solution)/shard_map/ppermute | solution.py:418
  49.1 6.4 %collective-permute-start.18 = (bf16[32,1024]{1,0:T(8,128)(2,1)S(1)}, bf16[32,1024]{1,0:T(8,128)(2,1)S(1)}, u32[]{:S(2)}, u32[]{:S(2)}) collective-permute-start(bf16[32,1024]{1,0:T(8,128)(2,1)S(1)} %get-tuple-element.56), channel_id=1, source_target_pairs={{0,4},{1,5},{2,6},{3,7},{4,0},{5,1},{6,2},{7,3},{8,12},{9,13},{10,... | collective-permute-start | bytes 196616 | tf_op jit(solution)/shard_map/ppermute | solution.py:418
  49.1 6.4 %collective-permute-start.19 = (bf16[32,1024]{1,0:T(8,128)(2,1)S(1)}, bf16[32,1024]{1,0:T(8,128)(2,1)S(1)}, u32[]{:S(2)}, u32[]{:S(2)}) collective-permute-start(bf16[32,1024]{1,0:T(8,128)(2,1)S(1)} %get-tuple-element.57), channel_id=1, source_target_pairs={{0,8},{1,9},{2,10},{3,11},{4,12},{5,13},{6,14},{7,15},{8,0},{9,1},... | collective-permute-start | bytes 196616 | tf_op jit(solution)/shard_map/ppermute | solution.py:418
  55.7 9.6 %collective-permute-start.26 = (bf16[3,256,128]{2,1,0:T(8,128)(2,1)S(1)}, bf16[3,256,128]{2,1,0:T(8,128)(2,1)S(1)}, u32[]{:S(2)}, u32[]{:S(2)}) collective-permute-start(bf16[3,256,128]{2,1,0:T(8,128)(2,1)S(1)} %get-tuple-element.64), channel_id=1, source_target_pairs={{0,16},{16,0},{1,17},{17,1},{2,18},{18,2},{3,19},{19,3},{4,20},{20... | collective-permute-start | bytes 589832 | tf_op jit(solution)/shard_map/ppermute | solution.py:421
  55.7 9.5 %collective-permute-start.27 = (bf16[3,256,128]{2,1,0:T(8,128)(2,1)S(1)}, bf16[3,256,128]{2,1,0:T(8,128)(2,1)S(1)}, u32[]{:S(2)}, u32[]{:S(2)}) collective-permute-start(bf16[3,256,128]{2,1,0:T(8,128)(2,1)S(1)} %get-tuple-element.65), channel_id=1, source_target_pairs={{0,16},{16,0},{1,17},{17,1},{2,18},{18,2},{3,19},{19,3},{4,20},{20... | collective-permute-start | bytes 589832 | tf_op jit(solution)/shard_map/ppermute | solution.py:421
  56.2 5.0 %collective-permute-start.23 = (bf16[32,1024]{1,0:T(8,128)(2,1)S(1)}, bf16[32,1024]{1,0:T(8,128)(2,1)S(1)}, u32[]{:S(2)}, u32[]{:S(2)}) collective-permute-start(bf16[32,1024]{1,0:T(8,128)(2,1)S(1)} %sum.1.refs_3_.refs_0_), channel_id=1, source_target_pairs={{0,4},{1,5},{2,6},{3,7},{4,0},{5,1},{6,2},{7,3},{8,12},{9,13},{10,... | collective-permute-start | bytes 196616 | tf_op jit(solution)/shard_map/ppermute | solution.py:418
  57.0 8.2 %collective-permute-start.24 = (bf16[32,1024]{1,0:T(8,128)(2,1)S(1)}, bf16[32,1024]{1,0:T(8,128)(2,1)S(1)}, u32[]{:S(2)}, u32[]{:S(2)}) collective-permute-start(bf16[32,1024]{1,0:T(8,128)(2,1)S(1)} %sum.1.refs_3_.refs_0_), channel_id=1, source_target_pairs={{0,8},{1,9},{2,10},{3,11},{4,12},{5,13},{6,14},{7,15},{8,0},{9,1},... | collective-permute-start | bytes 196616 | tf_op jit(solution)/shard_map/ppermute | solution.py:418
  58.4 6.9 %collective-permute-start.25 = (bf16[32,1024]{1,0:T(8,128)(2,1)S(1)}, bf16[32,1024]{1,0:T(8,128)(2,1)S(1)}, u32[]{:S(2)}, u32[]{:S(2)}) collective-permute-start(bf16[32,1024]{1,0:T(8,128)(2,1)S(1)} %sum.1.refs_3_.refs_0_), channel_id=1, source_target_pairs={{0,12},{1,13},{2,14},{3,15},{4,8},{5,9},{6,10},{7,11},{8,4},{9,5},... | collective-permute-start | bytes 196616 | tf_op jit(solution)/shard_map/ppermute | solution.py:418
  65.6 15.1 %collective-permute-start.28 = (bf16[1408,128]{1,0:T(8,128)(2,1)S(1)}, bf16[1408,128]{1,0:T(8,128)(2,1)S(1)}, u32[]{:S(2)}, u32[]{:S(2)}) collective-permute-start(bf16[1408,128]{1,0:T(8,128)(2,1)S(1)} %get-tuple-element.67), channel_id=1, source_target_pairs={{0,1},{1,0},{2,3},{3,2},{4,5},{5,4},{6,7},{7,6},{8,9},{9,8},{10,11... | collective-permute-start | bytes 1081352 | tf_op jit(solution)/shard_map/ppermute | solution.py:418
  66.2 14.5 %collective-permute-start.29 = (bf16[1408,128]{1,0:T(8,128)(2,1)S(1)}, bf16[1408,128]{1,0:T(8,128)(2,1)S(1)}, u32[]{:S(2)}, u32[]{:S(2)}) collective-permute-start(bf16[1408,128]{1,0:T(8,128)(2,1)S(1)} %get-tuple-element.68), channel_id=1, source_target_pairs={{0,2},{1,3},{2,0},{3,1},{4,6},{5,7},{6,4},{7,5},{8,10},{9,11},{10,... | collective-permute-start | bytes 1081352 | tf_op jit(solution)/shard_map/ppermute | solution.py:418
  67.6 14.7 %collective-permute-start.30 = (bf16[1408,128]{1,0:T(8,128)(2,1)S(1)}, bf16[1408,128]{1,0:T(8,128)(2,1)S(1)}, u32[]{:S(2)}, u32[]{:S(2)}) collective-permute-start(bf16[1408,128]{1,0:T(8,128)(2,1)S(1)} %get-tuple-element.69), channel_id=1, source_target_pairs={{0,3},{1,2},{2,1},{3,0},{4,7},{5,6},{6,5},{7,4},{8,11},{9,10},{10,... | collective-permute-start | bytes 1081352 | tf_op jit(solution)/shard_map/ppermute | solution.py:418
  69.1 5.0 %collective-permute-start.31 = (bf16[384,128]{1,0:T(8,128)(2,1)S(1)}, bf16[384,128]{1,0:T(8,128)(2,1)S(1)}, u32[]{:S(2)}, u32[]{:S(2)}) collective-permute-start(bf16[384,128]{1,0:T(8,128)(2,1)S(1)} %get-tuple-element.71), channel_id=1, source_target_pairs={{0,4},{1,5},{2,6},{3,7},{4,0},{5,1},{6,2},{7,3},{8,12},{9,13},{10,... | collective-permute-start | bytes 294920 | tf_op jit(solution)/shard_map/ppermute | solution.py:418
  70.4 8.1 %collective-permute-start.32 = (bf16[384,128]{1,0:T(8,128)(2,1)S(1)}, bf16[384,128]{1,0:T(8,128)(2,1)S(1)}, u32[]{:S(2)}, u32[]{:S(2)}) collective-permute-start(bf16[384,128]{1,0:T(8,128)(2,1)S(1)} %get-tuple-element.72), channel_id=1, source_target_pairs={{0,8},{1,9},{2,10},{3,11},{4,12},{5,13},{6,14},{7,15},{8,0},{9,1},... | collective-permute-start | bytes 294920 | tf_op jit(solution)/shard_map/ppermute | solution.py:418
  74.1 6.5 %collective-permute-start.33 = (bf16[384,128]{1,0:T(8,128)(2,1)S(1)}, bf16[384,128]{1,0:T(8,128)(2,1)S(1)}, u32[]{:S(2)}, u32[]{:S(2)}) collective-permute-start(bf16[384,128]{1,0:T(8,128)(2,1)S(1)} %get-tuple-element.73), channel_id=1, source_target_pairs={{0,12},{1,13},{2,14},{3,15},{4,8},{5,9},{6,10},{7,11},{8,4},{9,5},... | collective-permute-start | bytes 294920 | tf_op jit(solution)/shard_map/ppermute | solution.py:418

commit v4 on v3

--- a/solution.py
+++ b/solution.py
@@ -234,24 +234,29 @@
             window = slice(b * rows, b * rows + span + rows)
             mine = slice(b * rows, (b + 1) * rows)
             own = slice(span - b * rows, span + rows)
-            for i in range(2):
-                query = fqg_ref[i * span + b * rows : i * span + (b + 1) * rows]
-                grad = fqg_ref[(2 + i) * span + b * rows : (2 + i) * span + (b + 1) * rows]
-                probs, total = softmax(nt(key_s[i, window], query), bias)
-                probs_low = probs.astype(BF)
-                out_ref[i, :, mine] = nn(value_t[i, :, window], probs_low).astype(BF)
-                dscores, delta = score_grads(probs, probs_low, nt(value_s[i, window], grad))
-                stats_ref[i * 8 : i * 8 + 1, mine] = total
-                stats_ref[i * 8 + 1 : i * 8 + 2, mine] = delta
-                dquery_ref[i, mine] = (nn(key_t[i, :, window], dscores) * SCALE).astype(BF).T
-                dkey = nn(dscores[own], query) * SCALE
-                dvalue = nn(probs_low[own], grad)
+            both = range(2)
+            query = [fqg_ref[i * span + b * rows : i * span + (b + 1) * rows] for i in both]
+            grad = [fqg_ref[(2 + i) * span + b * rows : (2 + i) * span + (b + 1) * rows] for i in both]
+            scores = [nt(key_s[i, window], query[i]) for i in both]
+            dprobs = [nt(value_s[i, window], grad[i]) for i in both]
+            probs, total = zip(*[softmax(scores[i], bias) for i in both])
+            probs_low = [probs[i].astype(BF) for i in both]
+            outputs = [nn(value_t[i, :, window], probs_low[i]) for i in both]
+            dvalue = [nn(probs_low[i][own], grad[i]) for i in both]
+            dscores, delta = zip(*[score_grads(probs[i], probs_low[i], dprobs[i]) for i in both])
+            dquery = [nn(key_t[i, :, window], dscores[i]) for i in both]
+            dkey = [nn(dscores[i][own], query[i]) * SCALE for i in both]
+            for i in both:
+                out_ref[i, :, mine] = outputs[i].astype(BF)
+                stats_ref[i * 8 : i * 8 + 1, mine] = total[i]
+                stats_ref[i * 8 + 1 : i * 8 + 2, mine] = delta[i]
+                dquery_ref[i, mine] = (dquery[i] * SCALE).astype(BF).T
                 if b == g - 1:
-                    dkv_ref[i, 0] = dkey
-                    dkv_ref[i, 1] = dvalue
+                    dkv_ref[i, 0] = dkey[i]
+                    dkv_ref[i, 1] = dvalue[i]
                 else:
-                    dkv_ref[i, 0, : (b + 1) * rows] += dkey
-                    dkv_ref[i, 1, : (b + 1) * rows] += dvalue
+                    dkv_ref[i, 0, : (b + 1) * rows] += dkey[i]
+                    dkv_ref[i, 1, : (b + 1) * rows] += dvalue[i]
 
     roles(band, lambda: None)
 
@@ -271,18 +276,22 @@
                 block = lax.div(lax.broadcasted_iota(jnp.int32, (span - b * rows, rows), 0), BLK)
                 bias = jnp.where(block >= WMAX - width, 0.0, -1e30)
                 mine = slice(b * rows, (b + 1) * rows)
-                for i in range(2):
-                    query = next_ref[i * span + b * rows : i * span + (b + 1) * rows]
-                    at = (2 + i) * span + b * rows
-                    grad = next_ref[at : at + rows]
-                    key = fkv_ref[i * span + b * rows : (i + 1) * span]
-                    value = fkv_ref[(2 + i) * span + b * rows : (3 + i) * span]
-                    total = stats_ref[i * 8 : i * 8 + 1, mine]
-                    delta = stats_ref[i * 8 + 1 : i * 8 + 2, mine]
-                    probs = jnp.exp2(nt(key, query) * SCALE_2 + bias - total)
-                    dscores = (probs * (nt(value, grad) - delta)).astype(BF)
-                    out_ref[i, 0, b * rows :] += nn(dscores, query) * SCALE
-                    out_ref[i, 1, b * rows :] += nn(probs.astype(BF), grad)
+                both = range(2)
+                query = [next_ref[i * span + b * rows : i * span + (b + 1) * rows] for i in both]
+                grad = [next_ref[(2 + i) * span + b * rows : (2 + i) * span + (b + 1) * rows] for i in both]
+                scores = [nt(fkv_ref[i * span + b * rows : (i + 1) * span], query[i]) for i in both]
+                dprobs = [nt(fkv_ref[(2 + i) * span + b * rows : (3 + i) * span], grad[i]) for i in both]
+                probs = [
+                    jnp.exp2(scores[i] * SCALE_2 + bias - stats_ref[i * 8 : i * 8 + 1, mine]) for i in both
+                ]
+                dvalue = [nn(probs[i].astype(BF), grad[i]) for i in both]
+                dscores = [
+                    (probs[i] * (dprobs[i] - stats_ref[i * 8 + 1 : i * 8 + 2, mine])).astype(BF) for i in both
+                ]
+                dkey = [nn(dscores[i], query[i]) * SCALE for i in both]
+                for i in both:
+                    out_ref[i, 0, b * rows :] += dkey[i]
+                    out_ref[i, 1, b * rows :] += dvalue[i]
 
     roles(band, lambda: None)
 

time: 83.8 us -> 82.6 us (0.986)
  Pallas kernels: 11.6 us -> 9.75 us
  waiting for transfers between devices: 25.8 us -> 27.2 us
    pallas_call x12, Pallas kernels: 11.6 us -> 9.75 us  [call(): pl.pallas_call(body, out_shape=outs, in_specs=[scalars] * smem + [vmem] *...]
    ppermute x27, waiting for transfers between devices: 24.7 us -> 26.1 us  [send(): return lax.ppermute(value, both, pairs)]
  transfers between devices with their start and end apart: 34 -> 34, of which waited for: 14 -> 14; matrix products, arithmetic and copies ran while one was open for 0% -> 0% of each run, Pallas kernels for 12% -> 9%
where the time goes in v4:
time: 82.6 us; the launch traced here: 82.4 us
  starting transfers between devices  42.9 us (52%)
  waiting for transfers between devices  27.2 us (33%)
  Pallas kernels  9.75 us (12%)
  local copies, waits for them, and re-layouts  1.63 us (2%)
  between operations  0.87 us (1%)
    ppermute x27, starting transfers between devices, send(): return lax.ppermute(value, both, pairs)  39.3 us
    ppermute x27, waiting for transfers between devices, send(): return lax.ppermute(value, both, pairs)  26.1 us
    pallas_call x12, Pallas kernels, call(): pl.pallas_call(body, out_shape=outs, in_specs=[scalars] * smem + [vmem] *...  9.75 us
    ppermute x7, starting transfers between devices, swap(): return lax.ppermute(value, 'dp', [(0, 1), (1, 0)])  3.55 us
  transfers between devices with their start and end apart: 34, of which 14 were waited for; matrix products, arithmetic and copies ran while one was open for 0% of the time, Pallas kernels for 9%

profile of v4, /device:TPU:0, one launch (start us, length us, event | category | flops | bytes accessed | tf_op | source)
XLA Modules:
  0.0 82.4 jit_solution(8489854414246243752)
XLA Ops:
  0.7 1.0 %constant_dynamic-slice_fusion.2 = (bf16[1,128,512]{2,1,0:T(8,128)(2,1)S(1)}, bf16[1,128,512]{2,1,0:T(8,128)(2,1)S(1)}) fusion(bf16[1,128,1024]{2,1,0:T(8,128)(2,1)} %param.7, s32[]{:T(128)S(6)} %select_n.5, s32[]{:T(128)S(6)} %select_n.4), kind=kLoop, calls=%fused_computation.4 | loop fusion | bytes 524296 | tf_op jit(solution)/shard_map/dynamic_slice | solution.py:454
  1.7 0.1 copy-done.5
  1.8 0.0 copy-start
  1.9 0.5 collective-permute-start
  2.4 0.4 copy-done
  2.9 0.5 collective-permute-start.1
  3.4 1.1 %collective-permute-done.1.refs_1_.refs_6_ = bf16[128,1024]{1,0:T(8,128)(2,1)S(1)} collective-permute-done((bf16[128,1024]{1,0:T(8,128)(2,1)S(1)}, bf16[128,1024]{1,0:T(8,128)(2,1)S(1)}, u32[]{:S(2)}, u32[]{:S(2)}) %collective-permute-start.1) | collective-permute-done | bytes 262176 | tf_op jit(solution)/shard_map/ppermute | solution.py:430
  4.5 0.8 att_grad.1.refs_2_.refs_3_
  5.3 0.0 collective-permute-done.refs_1_.refs_2_
  5.3 0.2 pack_fields.1
  5.5 2.9 %collective-permute-start.2 = (bf16[1024,128]{1,0:T(8,128)(2,1)S(1)}, bf16[1024,128]{1,0:T(8,128)(2,1)S(1)}, u32[]{:S(2)}, u32[]{:S(2)}) collective-permute-start(bf16[1024,128]{1,0:T(8,128)(2,1)S(1)} %get-tuple-element.41), channel_id=1, source_target_pairs={{0,1},{1,0},{2,3},{3,2},{4,5},{5,4},{6,7},{7,6},{8,9},{9,8},{10,11... | collective-permute-start | bytes 786440 | tf_op jit(solution)/shard_map/ppermute | solution.py:427
  8.4 1.5 %collective-permute-start.3 = (bf16[1024,128]{1,0:T(8,128)(2,1)S(1)}, bf16[1024,128]{1,0:T(8,128)(2,1)S(1)}, u32[]{:S(2)}, u32[]{:S(2)}) collective-permute-start(bf16[1024,128]{1,0:T(8,128)(2,1)S(1)} %get-tuple-element.42), channel_id=1, source_target_pairs={{0,2},{1,3},{2,0},{3,1},{4,6},{5,7},{6,4},{7,5},{8,10},{9,11},{10,... | collective-permute-start | bytes 786440 | tf_op jit(solution)/shard_map/ppermute | solution.py:427
  9.9 0.0 collective-permute-start.4
  10.0 1.9 %collective-permute-start.12 = (bf16[128,1024]{1,0:T(8,128)(2,1)S(1)}, bf16[128,1024]{1,0:T(8,128)(2,1)S(1)}, u32[]{:S(2)}, u32[]{:S(2)}) collective-permute-start(bf16[128,1024]{1,0:T(8,128)(2,1)S(1)} %bitcast.6), channel_id=1, source_target_pairs={{0,1},{1,0},{2,3},{3,2},{4,5},{5,4},{6,7},{7,6},{8,9},{9,8},{10,11... | collective-permute-start | bytes 786440 | tf_op jit(solution)/shard_map/ppermute | solution.py:427
  11.9 1.5 %collective-permute-start.13 = (bf16[128,1024]{1,0:T(8,128)(2,1)S(1)}, bf16[128,1024]{1,0:T(8,128)(2,1)S(1)}, u32[]{:S(2)}, u32[]{:S(2)}) collective-permute-start(bf16[128,1024]{1,0:T(8,128)(2,1)S(1)} %bitcast.7), channel_id=1, source_target_pairs={{0,2},{1,3},{2,0},{3,1},{4,6},{5,7},{6,4},{7,5},{8,10},{9,11},{10,... | collective-permute-start | bytes 786440 | tf_op jit(solution)/shard_map/ppermute | solution.py:427
  13.4 2.3 %collective-permute-start.14 = (bf16[128,1024]{1,0:T(8,128)(2,1)S(1)}, bf16[128,1024]{1,0:T(8,128)(2,1)S(1)}, u32[]{:S(2)}, u32[]{:S(2)}) collective-permute-start(bf16[128,1024]{1,0:T(8,128)(2,1)S(1)} %bitcast.8), channel_id=1, source_target_pairs={{0,3},{1,2},{2,1},{3,0},{4,7},{5,6},{6,5},{7,4},{8,11},{9,10},{10,... | collective-permute-start | bytes 786440 | tf_op jit(solution)/shard_map/ppermute | solution.py:427
  15.8 0.6 collective-permute-done.3.refs_5_
  16.3 3.8 %collective-permute-done.4.refs_6_ = bf16[1024,128]{1,0:T(8,128)(2,1)S(1)} collective-permute-done((bf16[1024,128]{1,0:T(8,128)(2,1)S(1)}, bf16[1024,128]{1,0:T(8,128)(2,1)S(1)}, u32[]{:S(2)}, u32[]{:S(2)}) %collective-permute-start.4) | collective-permute-done | bytes 262176 | tf_op jit(solution)/shard_map/ppermute | solution.py:427
  20.1 0.7 forward.1
  20.8 4.3 %collective-permute-start.5 = (bf16[2048,128]{1,0:T(8,128)(2,1)S(1)}, bf16[2048,128]{1,0:T(8,128)(2,1)S(1)}, u32[]{:S(2)}, u32[]{:S(2)}) collective-permute-start(bf16[2048,128]{1,0:T(8,128)(2,1)S(1)} %get-tuple-element.45.refs_2_.refs_1_), channel_id=1, source_target_pairs={{0,4},{1,5},{2,6},{3,7},{4,8},{5,9},{6,10},{7,11},{8,12},{9,13},{1... | collective-permute-start | bytes 1572872 | tf_op jit(solution)/shard_map/ppermute | solution.py:427
  25.1 1.3 %collective-permute-start.21 = (bf16[2048,128]{1,0:T(8,128)(2,1)S(1)}, bf16[2048,128]{1,0:T(8,128)(2,1)S(1)}, u32[]{:S(2)}, u32[]{:S(2)}) collective-permute-start(bf16[2048,128]{1,0:T(8,128)(2,1)S(1)} %copy.12), channel_id=1, source_target_pairs={{4,0},{5,1},{6,2},{7,3},{8,4},{9,5},{10,6},{11,7},{12,8},{13,9},{1... | collective-permute-start | bytes 1572872 | tf_op jit(solution)/shard_map/ppermute | solution.py:427
  26.4 1.6 %collective-permute-start.6 = (bf16[256,128]{1,0:T(8,128)(2,1)S(1)}, bf16[256,128]{1,0:T(8,128)(2,1)S(1)}, u32[]{:S(2)}, u32[]{:S(2)}) collective-permute-start(bf16[256,128]{1,0:T(8,128)(2,1)S(1)} %get-tuple-element.48), channel_id=1, source_target_pairs={{0,1},{1,0},{2,3},{3,2},{4,5},{5,4},{6,7},{7,6},{8,9},{9,8},{10,11... | collective-permute-start | bytes 196616 | tf_op jit(solution)/shard_map/ppermute | solution.py:427
  28.0 0.8 %collective-permute-done.13.refs_8_ = bf16[128,1024]{1,0:T(8,128)(2,1)S(1)} collective-permute-done((bf16[128,1024]{1,0:T(8,128)(2,1)S(1)}, bf16[128,1024]{1,0:T(8,128)(2,1)S(1)}, u32[]{:S(2)}, u32[]{:S(2)}) %collective-permute-start.13) | collective-permute-done | bytes 262176 | tf_op jit(solution)/shard_map/ppermute | solution.py:427
  28.8 1.5 %collective-permute-start.7 = (bf16[256,128]{1,0:T(8,128)(2,1)S(1)}, bf16[256,128]{1,0:T(8,128)(2,1)S(1)}, u32[]{:S(2)}, u32[]{:S(2)}) collective-permute-start(bf16[256,128]{1,0:T(8,128)(2,1)S(1)} %get-tuple-element.49), channel_id=1, source_target_pairs={{0,2},{1,3},{2,0},{3,1},{4,6},{5,7},{6,4},{7,5},{8,10},{9,11},{10,... | collective-permute-start | bytes 196616 | tf_op jit(solution)/shard_map/ppermute | solution.py:427
  30.4 0.4 collective-permute-done.6.refs_1_
  30.8 1.2 %collective-permute-start.15 = (bf16[128,1024]{1,0:T(8,128)(2,1)S(1)}, bf16[128,1024]{1,0:T(8,128)(2,1)S(1)}, u32[]{:S(2)}, u32[]{:S(2)}) collective-permute-start(bf16[128,1024]{1,0:T(8,128)(2,1)S(1)} %collective-permute-done.12.refs_7_), channel_id=1, source_target_pairs={{0,16},{16,0},{1,17},{17,1},{2,18},{18,2},{3,19},{19,3},{4,20},{20... | collective-permute-start | bytes 786440 | tf_op jit(solution)/shard_map/ppermute | solution.py:430
  32.0 1.1 %collective-permute-done.7.refs_2_ = bf16[256,128]{1,0:T(8,128)(2,1)S(1)} collective-permute-done((bf16[256,128]{1,0:T(8,128)(2,1)S(1)}, bf16[256,128]{1,0:T(8,128)(2,1)S(1)}, u32[]{:S(2)}, u32[]{:S(2)}) %collective-permute-start.7) | collective-permute-done | bytes 65568 | tf_op jit(solution)/shard_map/ppermute | solution.py:427
  33.1 0.6 collective-permute-start.16
  33.7 1.8 %collective-permute-done.8.refs_3_ = bf16[256,128]{1,0:T(8,128)(2,1)S(1)} collective-permute-done((bf16[256,128]{1,0:T(8,128)(2,1)S(1)}, bf16[256,128]{1,0:T(8,128)(2,1)S(1)}, u32[]{:S(2)}, u32[]{:S(2)}) %collective-permute-start.8) | collective-permute-done | bytes 65568 | tf_op jit(solution)/shard_map/ppermute | solution.py:427
  35.5 0.2 collective-permute-start.17
  35.8 1.5 %collective-permute-start.10 = (bf16[256,128]{1,0:T(8,128)(2,1)S(1)}, bf16[256,128]{1,0:T(8,128)(2,1)S(1)}, u32[]{:S(2)}, u32[]{:S(2)}) collective-permute-start(bf16[256,128]{1,0:T(8,128)(2,1)S(1)} %get-tuple-element.53), channel_id=1, source_target_pairs={{0,2},{1,3},{2,0},{3,1},{4,6},{5,7},{6,4},{7,5},{8,10},{9,11},{10,... | collective-permute-start | bytes 196616 | tf_op jit(solution)/shard_map/ppermute | solution.py:427
  37.3 0.0 collective-permute-done.16.refs_11_
  37.3 0.3 collective-permute-start.11
  37.6 0.0 collective-permute-done.5.refs_3_
  37.6 1.7 %collective-permute-start.9 = (bf16[256,128]{1,0:T(8,128)(2,1)S(1)}, bf16[256,128]{1,0:T(8,128)(2,1)S(1)}, u32[]{:S(2)}, u32[]{:S(2)}) collective-permute-start(bf16[256,128]{1,0:T(8,128)(2,1)S(1)} %get-tuple-element.52), channel_id=1, source_target_pairs={{0,1},{1,0},{2,3},{3,2},{4,5},{5,4},{6,7},{7,6},{8,9},{9,8},{10,11... | collective-permute-start | bytes 196616 | tf_op jit(solution)/shard_map/ppermute | solution.py:427
  39.3 3.8 %attention.1 = (bf16[2,128,512]{2,1,0:T(8,128)(2,1)S(1)}, bf16[2,512,128]{2,1,0:T(8,128)(2,1)S(1)}, f32[2,2,512,128]{3,2,1,0:T(8,128)S(1)}, f32[48,512]{1,0:T(8,128)S(1)}) custom-call(s32[4]{0:T(128)S(1)} %copy-done.2, bf16[2048,128]{1,0:T(8,128)(2,1)S(1)} %get-tuple-element.44.refs_1_.refs_0_, bf16[2048,128]{1,0:T(8,128)(2,1)S(1)} %get-tuple-element.45.refs_2_.refs_1_, ...), custom_call_target="tpu_custom_call" | custom-call | tf_op jit(solution)/shard_map/attention/pallas_call | solution.py:52
  43.1 0.0 collective-permute-done.17.refs_12_
  43.1 0.0 collective-permute-start.22
  43.1 0.0 collective-permute-done.10.refs_3_
  43.2 0.8 weight.1
  43.9 3.9 %collective-permute-start.20 = (bf16[32,1024]{1,0:T(8,128)(2,1)S(1)}, bf16[32,1024]{1,0:T(8,128)(2,1)S(1)}, u32[]{:S(2)}, u32[]{:S(2)}) collective-permute-start(bf16[32,1024]{1,0:T(8,128)(2,1)S(1)} %get-tuple-element.58), channel_id=1, source_target_pairs={{0,12},{1,13},{2,14},{3,15},{4,8},{5,9},{6,10},{7,11},{8,4},{9,5},... | collective-permute-start | bytes 196616 | tf_op jit(solution)/shard_map/ppermute | solution.py:427
  47.8 0.6 collective-permute-start.19
  48.5 3.4 %collective-permute-done.20.refs_5_.refs_3_ = bf16[32,1024]{1,0:T(8,128)(2,1)S(1)} collective-permute-done((bf16[32,1024]{1,0:T(8,128)(2,1)S(1)}, bf16[32,1024]{1,0:T(8,128)(2,1)S(1)}, u32[]{:S(2)}, u32[]{:S(2)}) %collective-permute-start.20) | collective-permute-done | bytes 65568 | tf_op jit(solution)/shard_map/ppermute | solution.py:427
  51.9 1.7 %tail.1.refs_4_.refs_1_ = f32[2,2,512,128]{3,2,1,0:T(8,128)S(1)} custom-call(s32[4]{0:T(128)S(1)} %copy-done.2, bf16[2048,128]{1,0:T(8,128)(2,1)S(1)} %get-tuple-element.45.refs_2_.refs_1_, bf16[2048,128]{1,0:T(8,128)(2,1)S(1)} %collective-permute-done.21.refs_2_, f32[48,512]{1,0:T(8,128)S(1)} %collective-permute-done.22.refs_3_, ...), custom_call_target="tpu_custom_call" | custom-call | tf_op jit(solution)/shard_map/tail/pallas_call | solution.py:52
  53.6 0.1 collective-permute-done.19.refs_2_
  53.8 0.1 exchange.1
  53.9 0.1 collective-permute-start.26
  54.0 0.5 collective-permute-start.27
  54.5 1.3 %collective-permute-start.23 = (bf16[32,1024]{1,0:T(8,128)(2,1)S(1)}, bf16[32,1024]{1,0:T(8,128)(2,1)S(1)}, u32[]{:S(2)}, u32[]{:S(2)}) collective-permute-start(bf16[32,1024]{1,0:T(8,128)(2,1)S(1)} %sum.1.refs_3_.refs_0_), channel_id=1, source_target_pairs={{0,4},{1,5},{2,6},{3,7},{4,0},{5,1},{6,2},{7,3},{8,12},{9,13},{10,... | collective-permute-start | bytes 196616 | tf_op jit(solution)/shard_map/ppermute | solution.py:427
  55.8 1.4 %collective-permute-start.24 = (bf16[32,1024]{1,0:T(8,128)(2,1)S(1)}, bf16[32,1024]{1,0:T(8,128)(2,1)S(1)}, u32[]{:S(2)}, u32[]{:S(2)}) collective-permute-start(bf16[32,1024]{1,0:T(8,128)(2,1)S(1)} %sum.1.refs_3_.refs_0_), channel_id=1, source_target_pairs={{0,8},{1,9},{2,10},{3,11},{4,12},{5,13},{6,14},{7,15},{8,0},{9,1},... | collective-permute-start | bytes 196616 | tf_op jit(solution)/shard_map/ppermute | solution.py:427
  57.1 1.7 %collective-permute-start.25 = (bf16[32,1024]{1,0:T(8,128)(2,1)S(1)}, bf16[32,1024]{1,0:T(8,128)(2,1)S(1)}, u32[]{:S(2)}, u32[]{:S(2)}) collective-permute-start(bf16[32,1024]{1,0:T(8,128)(2,1)S(1)} %sum.1.refs_3_.refs_0_), channel_id=1, source_target_pairs={{0,12},{1,13},{2,14},{3,15},{4,8},{5,9},{6,10},{7,11},{8,4},{9,5},... | collective-permute-start | bytes 196616 | tf_op jit(solution)/shard_map/ppermute | solution.py:427
  58.9 5.0 %collective-permute-done.24.refs_2_ = bf16[32,1024]{1,0:T(8,128)(2,1)S(1)} collective-permute-done((bf16[32,1024]{1,0:T(8,128)(2,1)S(1)}, bf16[32,1024]{1,0:T(8,128)(2,1)S(1)}, u32[]{:S(2)}, u32[]{:S(2)}) %collective-permute-start.24) | collective-permute-done | bytes 65568 | tf_op jit(solution)/shard_map/ppermute | solution.py:427
  63.9 0.3 gather_line.1
  64.2 0.6 collective-permute-start.28
  64.8 1.3 %collective-permute-start.29 = (bf16[1408,128]{1,0:T(8,128)(2,1)S(1)}, bf16[1408,128]{1,0:T(8,128)(2,1)S(1)}, u32[]{:S(2)}, u32[]{:S(2)}) collective-permute-start(bf16[1408,128]{1,0:T(8,128)(2,1)S(1)} %get-tuple-element.68), channel_id=1, source_target_pairs={{0,2},{1,3},{2,0},{3,1},{4,6},{5,7},{6,4},{7,5},{8,10},{9,11},{10,... | collective-permute-start | bytes 1081352 | tf_op jit(solution)/shard_map/ppermute | solution.py:427
  66.1 1.7 %collective-permute-start.30 = (bf16[1408,128]{1,0:T(8,128)(2,1)S(1)}, bf16[1408,128]{1,0:T(8,128)(2,1)S(1)}, u32[]{:S(2)}, u32[]{:S(2)}) collective-permute-start(bf16[1408,128]{1,0:T(8,128)(2,1)S(1)} %get-tuple-element.69), channel_id=1, source_target_pairs={{0,3},{1,2},{2,1},{3,0},{4,7},{5,6},{6,5},{7,4},{8,11},{9,10},{10,... | collective-permute-start | bytes 1081352 | tf_op jit(solution)/shard_map/ppermute | solution.py:427
  67.7 1.3 %collective-permute-start.31 = (bf16[384,128]{1,0:T(8,128)(2,1)S(1)}, bf16[384,128]{1,0:T(8,128)(2,1)S(1)}, u32[]{:S(2)}, u32[]{:S(2)}) collective-permute-start(bf16[384,128]{1,0:T(8,128)(2,1)S(1)} %get-tuple-element.71), channel_id=1, source_target_pairs={{0,4},{1,5},{2,6},{3,7},{4,0},{5,1},{6,2},{7,3},{8,12},{9,13},{10,... | collective-permute-start | bytes 294920 | tf_op jit(solution)/shard_map/ppermute | solution.py:427
  69.1 1.4 %collective-permute-start.32 = (bf16[384,128]{1,0:T(8,128)(2,1)S(1)}, bf16[384,128]{1,0:T(8,128)(2,1)S(1)}, u32[]{:S(2)}, u32[]{:S(2)}) collective-permute-start(bf16[384,128]{1,0:T(8,128)(2,1)S(1)} %get-tuple-element.72), channel_id=1, source_target_pairs={{0,8},{1,9},{2,10},{3,11},{4,12},{5,13},{6,14},{7,15},{8,0},{9,1},... | collective-permute-start | bytes 294920 | tf_op jit(solution)/shard_map/ppermute | solution.py:427
  70.4 2.8 %collective-permute-done.31.refs_5_ = bf16[384,128]{1,0:T(8,128)(2,1)S(1)} collective-permute-done((bf16[384,128]{1,0:T(8,128)(2,1)S(1)}, bf16[384,128]{1,0:T(8,128)(2,1)S(1)}, u32[]{:S(2)}, u32[]{:S(2)}) %collective-permute-start.31) | collective-permute-done | bytes 98336 | tf_op jit(solution)/shard_map/ppermute | solution.py:427
  73.2 1.7 %collective-permute-start.33 = (bf16[384,128]{1,0:T(8,128)(2,1)S(1)}, bf16[384,128]{1,0:T(8,128)(2,1)S(1)}, u32[]{:S(2)}, u32[]{:S(2)}) collective-permute-start(bf16[384,128]{1,0:T(8,128)(2,1)S(1)} %get-tuple-element.73), channel_id=1, source_target_pairs={{0,12},{1,13},{2,14},{3,15},{4,8},{5,9},{6,10},{7,11},{8,4},{9,5},... | collective-permute-start | bytes 294920 | tf_op jit(solution)/shard_map/ppermute | solution.py:427
  74.9 2.8 %collective-permute-done.32.refs_6_ = bf16[384,128]{1,0:T(8,128)(2,1)S(1)} collective-permute-done((bf16[384,128]{1,0:T(8,128)(2,1)S(1)}, bf16[384,128]{1,0:T(8,128)(2,1)S(1)}, u32[]{:S(2)}, u32[]{:S(2)}) %collective-permute-start.32) | collective-permute-done | bytes 98336 | tf_op jit(solution)/shard_map/ppermute | solution.py:427
  77.7 2.0 %collective-permute-done.33.refs_7_ = bf16[384,128]{1,0:T(8,128)(2,1)S(1)} collective-permute-done((bf16[384,128]{1,0:T(8,128)(2,1)S(1)}, bf16[384,128]{1,0:T(8,128)(2,1)S(1)}, u32[]{:S(2)}, u32[]{:S(2)}) %collective-permute-start.33) | collective-permute-done | bytes 98336 | tf_op jit(solution)/shard_map/ppermute | solution.py:427
  79.7 1.4 %collective-permute-done.30.refs_3_ = bf16[1408,128]{1,0:T(8,128)(2,1)S(1)} collective-permute-done((bf16[1408,128]{1,0:T(8,128)(2,1)S(1)}, bf16[1408,128]{1,0:T(8,128)(2,1)S(1)}, u32[]{:S(2)}, u32[]{:S(2)}) %collective-permute-start.30) | collective-permute-done | bytes 360480 | tf_op jit(solution)/shard_map/ppermute | solution.py:427
  81.1 1.3 %finish.1 = (bf16[128,1024]{1,0:T(8,128)(2,1)}, bf16[128,1024]{1,0:T(8,128)(2,1)}, bf16[128,1024]{1,0:T(8,128)(2,1)}, bf16[512,1024]{1,0:T(8,128)(2,1)}) custom-call(bf16[1408,128]{1,0:T(8,128)(2,1)S(1)} %get-tuple-element.66.refs_0_, bf16[1408,128]{1,0:T(8,128)(2,1)S(1)} %collective-permute-done.28.refs_1_, ...), custom_call_target="tpu_custom_call" | custom-call | tf_op jit(solution)/shard_map/finish/pallas_call | solution.py:52
  (32 shorter events, 0.3 us)
Async XLA Ops:
  0.6 1.1 %copy-start.4 = (bf16[1,128,1024]{2,1,0:T(8,128)(2,1)S(1)}, bf16[1,128,1024]{2,1,0:T(8,128)(2,1)}, u32[]{:S(2)}) copy-start(bf16[1,128,1024]{2,1,0:T(8,128)(2,1)} %param.9) | copy-start | bytes 786436
  0.6 1.1 %copy-start.5 = (bf16[1,128,1024]{2,1,0:T(8,128)(2,1)S(1)}, bf16[1,128,1024]{2,1,0:T(8,128)(2,1)}, u32[]{:S(2)}) copy-start(bf16[1,128,1024]{2,1,0:T(8,128)(2,1)} %param.8) | copy-start | bytes 786436
  1.8 2.7 %copy-start.1 = (bf16[512,1024]{1,0:T(8,128)(2,1)S(1)}, bf16[512,1024]{1,0:T(8,128)(2,1)}, u32[]{:S(2)}) copy-start(bf16[512,1024]{1,0:T(8,128)(2,1)} %refs_2_.1) | copy-start | bytes 3145732
  1.8 1.0 %copy-start = (bf16[1,128,1024]{2,1,0:T(8,128)(2,1)S(1)}, bf16[1,128,1024]{2,1,0:T(8,128)(2,1)}, u32[]{:S(2)}) copy-start(bf16[1,128,1024]{2,1,0:T(8,128)(2,1)} %param.10) | copy-start | bytes 786436
  1.9 3.4 %collective-permute-start = (bf16[3,128,512]{2,1,0:T(8,128)(2,1)S(1)}, bf16[3,128,512]{2,1,0:T(8,128)(2,1)S(1)}, u32[]{:S(2)}, u32[]{:S(2)}) collective-permute-start(bf16[3,128,512]{2,1,0:T(8,128)(2,1)S(1)} %pad_maximum_fusion.1), channel_id=1, source_target_pairs={{0,16},{16,0},{1,17},{17,1},{2,18},{18,2},{3,19},{19,3},{4,20},{20... | collective-permute-start | bytes 1179656 | tf_op jit(solution)/shard_map/ppermute | solution.py:430
  2.9 1.6 %collective-permute-start.1 = (bf16[128,1024]{1,0:T(8,128)(2,1)S(1)}, bf16[128,1024]{1,0:T(8,128)(2,1)S(1)}, u32[]{:S(2)}, u32[]{:S(2)}) collective-permute-start(bf16[128,1024]{1,0:T(8,128)(2,1)S(1)} %bitcast.4), channel_id=1, source_target_pairs={{0,16},{16,0},{1,17},{17,1},{2,18},{18,2},{3,19},{19,3},{4,20},{20... | collective-permute-start | bytes 786440 | tf_op jit(solution)/shard_map/ppermute | solution.py:430
  5.5 7.9 %collective-permute-start.2 = (bf16[1024,128]{1,0:T(8,128)(2,1)S(1)}, bf16[1024,128]{1,0:T(8,128)(2,1)S(1)}, u32[]{:S(2)}, u32[]{:S(2)}) collective-permute-start(bf16[1024,128]{1,0:T(8,128)(2,1)S(1)} %get-tuple-element.41), channel_id=1, source_target_pairs={{0,1},{1,0},{2,3},{3,2},{4,5},{5,4},{6,7},{7,6},{8,9},{9,8},{10,11... | collective-permute-start | bytes 786440 | tf_op jit(solution)/shard_map/ppermute | solution.py:427
  8.4 11.7 %copy-start.3 = (s32[4]{0:T(128)S(1)}, s32[4]{0:T(128)}, u32[]{:S(2)}) copy-start(s32[4]{0:T(128)} %refs_0_.3) | copy-start | bytes 52
  8.4 7.9 %collective-permute-start.3 = (bf16[1024,128]{1,0:T(8,128)(2,1)S(1)}, bf16[1024,128]{1,0:T(8,128)(2,1)S(1)}, u32[]{:S(2)}, u32[]{:S(2)}) collective-permute-start(bf16[1024,128]{1,0:T(8,128)(2,1)S(1)} %get-tuple-element.42), channel_id=1, source_target_pairs={{0,2},{1,3},{2,0},{3,1},{4,6},{5,7},{6,4},{7,5},{8,10},{9,11},{10,... | collective-permute-start | bytes 786440 | tf_op jit(solution)/shard_map/ppermute | solution.py:427
  9.9 10.2 %collective-permute-start.4 = (bf16[1024,128]{1,0:T(8,128)(2,1)S(1)}, bf16[1024,128]{1,0:T(8,128)(2,1)S(1)}, u32[]{:S(2)}, u32[]{:S(2)}) collective-permute-start(bf16[1024,128]{1,0:T(8,128)(2,1)S(1)} %get-tuple-element.43), channel_id=1, source_target_pairs={{0,3},{1,2},{2,1},{3,0},{4,7},{5,6},{6,5},{7,4},{8,11},{9,10},{10,... | collective-permute-start | bytes 786440 | tf_op jit(solution)/shard_map/ppermute | solution.py:427
  10.0 16.5 %collective-permute-start.12 = (bf16[128,1024]{1,0:T(8,128)(2,1)S(1)}, bf16[128,1024]{1,0:T(8,128)(2,1)S(1)}, u32[]{:S(2)}, u32[]{:S(2)}) collective-permute-start(bf16[128,1024]{1,0:T(8,128)(2,1)S(1)} %bitcast.6), channel_id=1, source_target_pairs={{0,1},{1,0},{2,3},{3,2},{4,5},{5,4},{6,7},{7,6},{8,9},{9,8},{10,11... | collective-permute-start | bytes 786440 | tf_op jit(solution)/shard_map/ppermute | solution.py:427
  11.9 16.9 %collective-permute-start.13 = (bf16[128,1024]{1,0:T(8,128)(2,1)S(1)}, bf16[128,1024]{1,0:T(8,128)(2,1)S(1)}, u32[]{:S(2)}, u32[]{:S(2)}) collective-permute-start(bf16[128,1024]{1,0:T(8,128)(2,1)S(1)} %bitcast.7), channel_id=1, source_target_pairs={{0,2},{1,3},{2,0},{3,1},{4,6},{5,7},{6,4},{7,5},{8,10},{9,11},{10,... | collective-permute-start | bytes 786440 | tf_op jit(solution)/shard_map/ppermute | solution.py:427
  13.4 16.9 %collective-permute-start.14 = (bf16[128,1024]{1,0:T(8,128)(2,1)S(1)}, bf16[128,1024]{1,0:T(8,128)(2,1)S(1)}, u32[]{:S(2)}, u32[]{:S(2)}) collective-permute-start(bf16[128,1024]{1,0:T(8,128)(2,1)S(1)} %bitcast.8), channel_id=1, source_target_pairs={{0,3},{1,2},{2,1},{3,0},{4,7},{5,6},{6,5},{7,4},{8,11},{9,10},{10,... | collective-permute-start | bytes 786440 | tf_op jit(solution)/shard_map/ppermute | solution.py:427
  20.8 16.8 %collective-permute-start.5 = (bf16[2048,128]{1,0:T(8,128)(2,1)S(1)}, bf16[2048,128]{1,0:T(8,128)(2,1)S(1)}, u32[]{:S(2)}, u32[]{:S(2)}) collective-permute-start(bf16[2048,128]{1,0:T(8,128)(2,1)S(1)} %get-tuple-element.45.refs_2_.refs_1_), channel_id=1, source_target_pairs={{0,4},{1,5},{2,6},{3,7},{4,8},{5,9},{6,10},{7,11},{8,12},{9,13},{1... | collective-permute-start | bytes 1572872 | tf_op jit(solution)/shard_map/ppermute | solution.py:427
  25.1 23.3 %collective-permute-start.21 = (bf16[2048,128]{1,0:T(8,128)(2,1)S(1)}, bf16[2048,128]{1,0:T(8,128)(2,1)S(1)}, u32[]{:S(2)}, u32[]{:S(2)}) collective-permute-start(bf16[2048,128]{1,0:T(8,128)(2,1)S(1)} %copy.12), channel_id=1, source_target_pairs={{4,0},{5,1},{6,2},{7,3},{8,4},{9,5},{10,6},{11,7},{12,8},{13,9},{1... | collective-permute-start | bytes 1572872 | tf_op jit(solution)/shard_map/ppermute | solution.py:427
  26.4 4.3 %collective-permute-start.6 = (bf16[256,128]{1,0:T(8,128)(2,1)S(1)}, bf16[256,128]{1,0:T(8,128)(2,1)S(1)}, u32[]{:S(2)}, u32[]{:S(2)}) collective-permute-start(bf16[256,128]{1,0:T(8,128)(2,1)S(1)} %get-tuple-element.48), channel_id=1, source_target_pairs={{0,1},{1,0},{2,3},{3,2},{4,5},{5,4},{6,7},{7,6},{8,9},{9,8},{10,11... | collective-permute-start | bytes 196616 | tf_op jit(solution)/shard_map/ppermute | solution.py:427
  28.8 4.3 %collective-permute-start.7 = (bf16[256,128]{1,0:T(8,128)(2,1)S(1)}, bf16[256,128]{1,0:T(8,128)(2,1)S(1)}, u32[]{:S(2)}, u32[]{:S(2)}) collective-permute-start(bf16[256,128]{1,0:T(8,128)(2,1)S(1)} %get-tuple-element.49), channel_id=1, source_target_pairs={{0,2},{1,3},{2,0},{3,1},{4,6},{5,7},{6,4},{7,5},{8,10},{9,11},{10,... | collective-permute-start | bytes 196616 | tf_op jit(solution)/shard_map/ppermute | solution.py:427
  30.4 5.2 %collective-permute-start.8 = (bf16[256,128]{1,0:T(8,128)(2,1)S(1)}, bf16[256,128]{1,0:T(8,128)(2,1)S(1)}, u32[]{:S(2)}, u32[]{:S(2)}) collective-permute-start(bf16[256,128]{1,0:T(8,128)(2,1)S(1)} %get-tuple-element.50), channel_id=1, source_target_pairs={{0,3},{1,2},{2,1},{3,0},{4,7},{5,6},{6,5},{7,4},{8,11},{9,10},{10,... | collective-permute-start | bytes 196616 | tf_op jit(solution)/shard_map/ppermute | solution.py:427
  30.8 5.0 %collective-permute-start.15 = (bf16[128,1024]{1,0:T(8,128)(2,1)S(1)}, bf16[128,1024]{1,0:T(8,128)(2,1)S(1)}, u32[]{:S(2)}, u32[]{:S(2)}) collective-permute-start(bf16[128,1024]{1,0:T(8,128)(2,1)S(1)} %collective-permute-done.12.refs_7_), channel_id=1, source_target_pairs={{0,16},{16,0},{1,17},{17,1},{2,18},{18,2},{3,19},{19,3},{4,20},{20... | collective-permute-start | bytes 786440 | tf_op jit(solution)/shard_map/ppermute | solution.py:430
  33.1 4.2 %collective-permute-start.16 = (bf16[128,1024]{1,0:T(8,128)(2,1)S(1)}, bf16[128,1024]{1,0:T(8,128)(2,1)S(1)}, u32[]{:S(2)}, u32[]{:S(2)}) collective-permute-start(bf16[128,1024]{1,0:T(8,128)(2,1)S(1)} %collective-permute-done.13.refs_8_), channel_id=1, source_target_pairs={{0,16},{16,0},{1,17},{17,1},{2,18},{18,2},{3,19},{19,3},{4,20},{20... | collective-permute-start | bytes 786440 | tf_op jit(solution)/shard_map/ppermute | solution.py:430
  35.5 7.6 %collective-permute-start.17 = (bf16[128,1024]{1,0:T(8,128)(2,1)S(1)}, bf16[128,1024]{1,0:T(8,128)(2,1)S(1)}, u32[]{:S(2)}, u32[]{:S(2)}) collective-permute-start(bf16[128,1024]{1,0:T(8,128)(2,1)S(1)} %collective-permute-done.14.refs_9_), channel_id=1, source_target_pairs={{0,16},{16,0},{1,17},{17,1},{2,18},{18,2},{3,19},{19,3},{4,20},{20... | collective-permute-start | bytes 786440 | tf_op jit(solution)/shard_map/ppermute | solution.py:430
  35.8 7.4 %collective-permute-start.10 = (bf16[256,128]{1,0:T(8,128)(2,1)S(1)}, bf16[256,128]{1,0:T(8,128)(2,1)S(1)}, u32[]{:S(2)}, u32[]{:S(2)}) collective-permute-start(bf16[256,128]{1,0:T(8,128)(2,1)S(1)} %get-tuple-element.53), channel_id=1, source_target_pairs={{0,2},{1,3},{2,0},{3,1},{4,6},{5,7},{6,4},{7,5},{8,10},{9,11},{10,... | collective-permute-start | bytes 196616 | tf_op jit(solution)/shard_map/ppermute | solution.py:427
  37.3 2.0 %copy-start.2 = (s32[4]{0:T(128)S(1)}, s32[4]{0:T(128)}, u32[]{:S(2)}) copy-start(s32[4]{0:T(128)} %refs_0_.5) | copy-start | bytes 52
  37.3 5.9 %collective-permute-start.11 = (bf16[256,128]{1,0:T(8,128)(2,1)S(1)}, bf16[256,128]{1,0:T(8,128)(2,1)S(1)}, u32[]{:S(2)}, u32[]{:S(2)}) collective-permute-start(bf16[256,128]{1,0:T(8,128)(2,1)S(1)} %get-tuple-element.54), channel_id=1, source_target_pairs={{0,3},{1,2},{2,1},{3,0},{4,7},{5,6},{6,5},{7,4},{8,11},{9,10},{10,... | collective-permute-start | bytes 196616 | tf_op jit(solution)/shard_map/ppermute | solution.py:427
  37.6 5.5 %collective-permute-start.9 = (bf16[256,128]{1,0:T(8,128)(2,1)S(1)}, bf16[256,128]{1,0:T(8,128)(2,1)S(1)}, u32[]{:S(2)}, u32[]{:S(2)}) collective-permute-start(bf16[256,128]{1,0:T(8,128)(2,1)S(1)} %get-tuple-element.52), channel_id=1, source_target_pairs={{0,1},{1,0},{2,3},{3,2},{4,5},{5,4},{6,7},{7,6},{8,9},{9,8},{10,11... | collective-permute-start | bytes 196616 | tf_op jit(solution)/shard_map/ppermute | solution.py:427
  43.1 8.8 %collective-permute-start.22 = (f32[48,512]{1,0:T(8,128)S(1)}, f32[48,512]{1,0:T(8,128)S(1)}, u32[]{:S(2)}, u32[]{:S(2)}) collective-permute-start(f32[48,512]{1,0:T(8,128)S(1)} %get-tuple-element.59), channel_id=1, source_target_pairs={{0,16},{1,17},{2,18},{3,19},{4,0},{5,1},{6,2},{7,3},{8,4},{9,5},{1... | collective-permute-start | bytes 294920 | tf_op jit(solution)/shard_map/ppermute | solution.py:427
  43.9 8.0 %collective-permute-start.20 = (bf16[32,1024]{1,0:T(8,128)(2,1)S(1)}, bf16[32,1024]{1,0:T(8,128)(2,1)S(1)}, u32[]{:S(2)}, u32[]{:S(2)}) collective-permute-start(bf16[32,1024]{1,0:T(8,128)(2,1)S(1)} %get-tuple-element.58), channel_id=1, source_target_pairs={{0,12},{1,13},{2,14},{3,15},{4,8},{5,9},{6,10},{7,11},{8,4},{9,5},... | collective-permute-start | bytes 196616 | tf_op jit(solution)/shard_map/ppermute | solution.py:427
  47.8 5.8 %collective-permute-start.18 = (bf16[32,1024]{1,0:T(8,128)(2,1)S(1)}, bf16[32,1024]{1,0:T(8,128)(2,1)S(1)}, u32[]{:S(2)}, u32[]{:S(2)}) collective-permute-start(bf16[32,1024]{1,0:T(8,128)(2,1)S(1)} %get-tuple-element.56), channel_id=1, source_target_pairs={{0,4},{1,5},{2,6},{3,7},{4,0},{5,1},{6,2},{7,3},{8,12},{9,13},{10,... | collective-permute-start | bytes 196616 | tf_op jit(solution)/shard_map/ppermute | solution.py:427
  47.8 5.9 %collective-permute-start.19 = (bf16[32,1024]{1,0:T(8,128)(2,1)S(1)}, bf16[32,1024]{1,0:T(8,128)(2,1)S(1)}, u32[]{:S(2)}, u32[]{:S(2)}) collective-permute-start(bf16[32,1024]{1,0:T(8,128)(2,1)S(1)} %get-tuple-element.57), channel_id=1, source_target_pairs={{0,8},{1,9},{2,10},{3,11},{4,12},{5,13},{6,14},{7,15},{8,0},{9,1},... | collective-permute-start | bytes 196616 | tf_op jit(solution)/shard_map/ppermute | solution.py:427
  53.9 10.0 %collective-permute-start.26 = (bf16[3,256,128]{2,1,0:T(8,128)(2,1)S(1)}, bf16[3,256,128]{2,1,0:T(8,128)(2,1)S(1)}, u32[]{:S(2)}, u32[]{:S(2)}) collective-permute-start(bf16[3,256,128]{2,1,0:T(8,128)(2,1)S(1)} %get-tuple-element.64), channel_id=1, source_target_pairs={{0,16},{16,0},{1,17},{17,1},{2,18},{18,2},{3,19},{19,3},{4,20},{20... | collective-permute-start | bytes 589832 | tf_op jit(solution)/shard_map/ppermute | solution.py:430
  54.0 9.9 %collective-permute-start.27 = (bf16[3,256,128]{2,1,0:T(8,128)(2,1)S(1)}, bf16[3,256,128]{2,1,0:T(8,128)(2,1)S(1)}, u32[]{:S(2)}, u32[]{:S(2)}) collective-permute-start(bf16[3,256,128]{2,1,0:T(8,128)(2,1)S(1)} %get-tuple-element.65), channel_id=1, source_target_pairs={{0,16},{16,0},{1,17},{17,1},{2,18},{18,2},{3,19},{19,3},{4,20},{20... | collective-permute-start | bytes 589832 | tf_op jit(solution)/shard_map/ppermute | solution.py:430
  54.5 4.4 %collective-permute-start.23 = (bf16[32,1024]{1,0:T(8,128)(2,1)S(1)}, bf16[32,1024]{1,0:T(8,128)(2,1)S(1)}, u32[]{:S(2)}, u32[]{:S(2)}) collective-permute-start(bf16[32,1024]{1,0:T(8,128)(2,1)S(1)} %sum.1.refs_3_.refs_0_), channel_id=1, source_target_pairs={{0,4},{1,5},{2,6},{3,7},{4,0},{5,1},{6,2},{7,3},{8,12},{9,13},{10,... | collective-permute-start | bytes 196616 | tf_op jit(solution)/shard_map/ppermute | solution.py:427
  55.8 8.1 %collective-permute-start.24 = (bf16[32,1024]{1,0:T(8,128)(2,1)S(1)}, bf16[32,1024]{1,0:T(8,128)(2,1)S(1)}, u32[]{:S(2)}, u32[]{:S(2)}) collective-permute-start(bf16[32,1024]{1,0:T(8,128)(2,1)S(1)} %sum.1.refs_3_.refs_0_), channel_id=1, source_target_pairs={{0,8},{1,9},{2,10},{3,11},{4,12},{5,13},{6,14},{7,15},{8,0},{9,1},... | collective-permute-start | bytes 196616 | tf_op jit(solution)/shard_map/ppermute | solution.py:427
  57.1 6.8 %collective-permute-start.25 = (bf16[32,1024]{1,0:T(8,128)(2,1)S(1)}, bf16[32,1024]{1,0:T(8,128)(2,1)S(1)}, u32[]{:S(2)}, u32[]{:S(2)}) collective-permute-start(bf16[32,1024]{1,0:T(8,128)(2,1)S(1)} %sum.1.refs_3_.refs_0_), channel_id=1, source_target_pairs={{0,12},{1,13},{2,14},{3,15},{4,8},{5,9},{6,10},{7,11},{8,4},{9,5},... | collective-permute-start | bytes 196616 | tf_op jit(solution)/shard_map/ppermute | solution.py:427
  64.2 15.5 %collective-permute-start.28 = (bf16[1408,128]{1,0:T(8,128)(2,1)S(1)}, bf16[1408,128]{1,0:T(8,128)(2,1)S(1)}, u32[]{:S(2)}, u32[]{:S(2)}) collective-permute-start(bf16[1408,128]{1,0:T(8,128)(2,1)S(1)} %get-tuple-element.67), channel_id=1, source_target_pairs={{0,1},{1,0},{2,3},{3,2},{4,5},{5,4},{6,7},{7,6},{8,9},{9,8},{10,11... | collective-permute-start | bytes 1081352 | tf_op jit(solution)/shard_map/ppermute | solution.py:427
  64.8 15.0 %collective-permute-start.29 = (bf16[1408,128]{1,0:T(8,128)(2,1)S(1)}, bf16[1408,128]{1,0:T(8,128)(2,1)S(1)}, u32[]{:S(2)}, u32[]{:S(2)}) collective-permute-start(bf16[1408,128]{1,0:T(8,128)(2,1)S(1)} %get-tuple-element.68), channel_id=1, source_target_pairs={{0,2},{1,3},{2,0},{3,1},{4,6},{5,7},{6,4},{7,5},{8,10},{9,11},{10,... | collective-permute-start | bytes 1081352 | tf_op jit(solution)/shard_map/ppermute | solution.py:427
  66.1 15.0 %collective-permute-start.30 = (bf16[1408,128]{1,0:T(8,128)(2,1)S(1)}, bf16[1408,128]{1,0:T(8,128)(2,1)S(1)}, u32[]{:S(2)}, u32[]{:S(2)}) collective-permute-start(bf16[1408,128]{1,0:T(8,128)(2,1)S(1)} %get-tuple-element.69), channel_id=1, source_target_pairs={{0,3},{1,2},{2,1},{3,0},{4,7},{5,6},{6,5},{7,4},{8,11},{9,10},{10,... | collective-permute-start | bytes 1081352 | tf_op jit(solution)/shard_map/ppermute | solution.py:427
  67.7 5.5 %collective-permute-start.31 = (bf16[384,128]{1,0:T(8,128)(2,1)S(1)}, bf16[384,128]{1,0:T(8,128)(2,1)S(1)}, u32[]{:S(2)}, u32[]{:S(2)}) collective-permute-start(bf16[384,128]{1,0:T(8,128)(2,1)S(1)} %get-tuple-element.71), channel_id=1, source_target_pairs={{0,4},{1,5},{2,6},{3,7},{4,0},{5,1},{6,2},{7,3},{8,12},{9,13},{10,... | collective-permute-start | bytes 294920 | tf_op jit(solution)/shard_map/ppermute | solution.py:427
  69.1 8.6 %collective-permute-start.32 = (bf16[384,128]{1,0:T(8,128)(2,1)S(1)}, bf16[384,128]{1,0:T(8,128)(2,1)S(1)}, u32[]{:S(2)}, u32[]{:S(2)}) collective-permute-start(bf16[384,128]{1,0:T(8,128)(2,1)S(1)} %get-tuple-element.72), channel_id=1, source_target_pairs={{0,8},{1,9},{2,10},{3,11},{4,12},{5,13},{6,14},{7,15},{8,0},{9,1},... | collective-permute-start | bytes 294920 | tf_op jit(solution)/shard_map/ppermute | solution.py:427
  73.2 6.5 %collective-permute-start.33 = (bf16[384,128]{1,0:T(8,128)(2,1)S(1)}, bf16[384,128]{1,0:T(8,128)(2,1)S(1)}, u32[]{:S(2)}, u32[]{:S(2)}) collective-permute-start(bf16[384,128]{1,0:T(8,128)(2,1)S(1)} %get-tuple-element.73), channel_id=1, source_target_pairs={{0,12},{1,13},{2,14},{3,15},{4,8},{5,9},{6,10},{7,11},{8,4},{9,5},... | collective-permute-start | bytes 294920 | tf_op jit(solution)/shard_map/ppermute | solution.py:427

commit v5 on v3

--- a/solution.py
+++ b/solution.py
@@ -229,29 +229,35 @@
                 ref[i, :span] = halo_ref[at : at + span]
             key_t[i] = key_s[i].T
             value_t[i] = value_s[i].T
-        for b in reversed(range(g)):
-            bias = jnp.where(near & ((block + b >= g) | (line > 0)), 0.0, -1e30)
-            window = slice(b * rows, b * rows + span + rows)
-            mine = slice(b * rows, (b + 1) * rows)
-            own = slice(span - b * rows, span + rows)
-            for i in range(2):
-                query = fqg_ref[i * span + b * rows : i * span + (b + 1) * rows]
-                grad = fqg_ref[(2 + i) * span + b * rows : (2 + i) * span + (b + 1) * rows]
-                probs, total = softmax(nt(key_s[i, window], query), bias)
-                probs_low = probs.astype(BF)
-                out_ref[i, :, mine] = nn(value_t[i, :, window], probs_low).astype(BF)
-                dscores, delta = score_grads(probs, probs_low, nt(value_s[i, window], grad))
-                stats_ref[i * 8 : i * 8 + 1, mine] = total
-                stats_ref[i * 8 + 1 : i * 8 + 2, mine] = delta
-                dquery_ref[i, mine] = (nn(key_t[i, :, window], dscores) * SCALE).astype(BF).T
-                dkey = nn(dscores[own], query) * SCALE
-                dvalue = nn(probs_low[own], grad)
+        for last in range(g - 1, 0, -2):
+            chains = [(b, i) for b in (last, last - 1) for i in range(2)]
+            each = range(len(chains))
+            bias = [jnp.where(near & ((block + b >= g) | (line > 0)), 0.0, -1e30) for b in (last, last - 1)]
+            window = [slice(b * rows, b * rows + span + rows) for b, _ in chains]
+            mine = [slice(b * rows, (b + 1) * rows) for b, _ in chains]
+            own = [slice(span - b * rows, span + rows) for b, _ in chains]
+            query = [fqg_ref[i * span + b * rows : i * span + (b + 1) * rows] for b, i in chains]
+            grad = [fqg_ref[(2 + i) * span + b * rows : (2 + i) * span + (b + 1) * rows] for b, i in chains]
+            scores = [nt(key_s[chains[n][1], window[n]], query[n]) for n in each]
+            dprobs = [nt(value_s[chains[n][1], window[n]], grad[n]) for n in each]
+            probs, total = zip(*[softmax(scores[n], bias[n // 2]) for n in each])
+            probs_low = [probs[n].astype(BF) for n in each]
+            outputs = [nn(value_t[chains[n][1], :, window[n]], probs_low[n]) for n in each]
+            dvalue = [nn(probs_low[n][own[n]], grad[n]) for n in each]
+            dscores, delta = zip(*[score_grads(probs[n], probs_low[n], dprobs[n]) for n in each])
+            dquery = [nn(key_t[chains[n][1], :, window[n]], dscores[n]) for n in each]
+            dkey = [nn(dscores[n][own[n]], query[n]) * SCALE for n in each]
+            for n, (b, i) in enumerate(chains):
+                out_ref[i, :, mine[n]] = outputs[n].astype(BF)
+                stats_ref[i * 8 : i * 8 + 1, mine[n]] = total[n]
+                stats_ref[i * 8 + 1 : i * 8 + 2, mine[n]] = delta[n]
+                dquery_ref[i, mine[n]] = (dquery[n] * SCALE).astype(BF).T
                 if b == g - 1:
-                    dkv_ref[i, 0] = dkey
-                    dkv_ref[i, 1] = dvalue
+                    dkv_ref[i, 0] = dkey[n]
+                    dkv_ref[i, 1] = dvalue[n]
                 else:
-                    dkv_ref[i, 0, : (b + 1) * rows] += dkey
-                    dkv_ref[i, 1, : (b + 1) * rows] += dvalue
+                    dkv_ref[i, 0, : (b + 1) * rows] += dkey[n]
+                    dkv_ref[i, 1, : (b + 1) * rows] += dvalue[n]
 
     roles(band, lambda: None)
 
@@ -267,22 +273,33 @@
         @pl.when(line < g - 1)
         def _():
             width = width_ref[spot_]
-            for b in range(g):
-                block = lax.div(lax.broadcasted_iota(jnp.int32, (span - b * rows, rows), 0), BLK)
-                bias = jnp.where(block >= WMAX - width, 0.0, -1e30)
-                mine = slice(b * rows, (b + 1) * rows)
-                for i in range(2):
-                    query = next_ref[i * span + b * rows : i * span + (b + 1) * rows]
-                    at = (2 + i) * span + b * rows
-                    grad = next_ref[at : at + rows]
-                    key = fkv_ref[i * span + b * rows : (i + 1) * span]
-                    value = fkv_ref[(2 + i) * span + b * rows : (3 + i) * span]
-                    total = stats_ref[i * 8 : i * 8 + 1, mine]
-                    delta = stats_ref[i * 8 + 1 : i * 8 + 2, mine]
-                    probs = jnp.exp2(nt(key, query) * SCALE_2 + bias - total)
-                    dscores = (probs * (nt(value, grad) - delta)).astype(BF)
-                    out_ref[i, 0, b * rows :] += nn(dscores, query) * SCALE
-                    out_ref[i, 1, b * rows :] += nn(probs.astype(BF), grad)
+            for first in range(0, g, 2):
+                chains = [(b, i) for b in (first, first + 1) for i in range(2)]
+                each = range(len(chains))
+                bias = []
+                for b in (first, first + 1):
+                    block = lax.div(lax.broadcasted_iota(jnp.int32, (span - b * rows, rows), 0), BLK)
+                    bias.append(jnp.where(block >= WMAX - width, 0.0, -1e30))
+                mine = [slice(b * rows, (b + 1) * rows) for b, _ in chains]
+                query = [next_ref[i * span + b * rows : i * span + (b + 1) * rows] for b, i in chains]
+                grad = [next_ref[(2 + i) * span + b * rows : (2 + i) * span + (b + 1) * rows] for b, i in chains]
+                scores = [nt(fkv_ref[i * span + b * rows : (i + 1) * span], query[n]) for n, (b, i) in enumerate(chains)]
+                dprobs = [
+                    nt(fkv_ref[(2 + i) * span + b * rows : (3 + i) * span], grad[n]) for n, (b, i) in enumerate(chains)
+                ]
+                probs = [
+                    jnp.exp2(scores[n] * SCALE_2 + bias[n // 2] - stats_ref[i * 8 : i * 8 + 1, mine[n]])
+                    for n, (_, i) in enumerate(chains)
+                ]
+                dvalue = [nn(probs[n].astype(BF), grad[n]) for n in each]
+                dscores = [
+                    (probs[n] * (dprobs[n] - stats_ref[i * 8 + 1 : i * 8 + 2, mine[n]])).astype(BF)
+                    for n, (_, i) in enumerate(chains)
+                ]
+                dkey = [nn(dscores[n], query[n]) * SCALE for n in each]
+                for n, (b, i) in enumerate(chains):
+                    out_ref[i, 0, b * rows :] += dkey[n]
+                    out_ref[i, 1, b * rows :] += dvalue[n]
 
     roles(band, lambda: None)
 

time: 83.8 us -> 82.4 us (0.983)
  Pallas kernels: 11.6 us -> 9.27 us
  waiting for transfers between devices: 25.8 us -> 27.4 us
    pallas_call x12, Pallas kernels: 11.6 us -> 9.27 us  [call(): pl.pallas_call(body, out_shape=outs, in_specs=[scalars] * smem + [vmem] *...]
    ppermute x27, waiting for transfers between devices: 24.7 us -> 26.3 us  [send(): return lax.ppermute(value, both, pairs)]
  transfers between devices with their start and end apart: 34 -> 34, of which waited for: 14 -> 14; matrix products, arithmetic and copies ran while one was open for 0% -> 0% of each run, Pallas kernels for 12% -> 9%
where the time goes in v5:
time: 82.4 us; the launch traced here: 82.2 us
  starting transfers between devices  42.9 us (52%)
  waiting for transfers between devices  27.4 us (33%)
  Pallas kernels  9.27 us (11%)
  local copies, waits for them, and re-layouts  1.63 us (2%)
  between operations  0.88 us (1%)
    ppermute x27, starting transfers between devices, send(): return lax.ppermute(value, both, pairs)  39.3 us
    ppermute x27, waiting for transfers between devices, send(): return lax.ppermute(value, both, pairs)  26.3 us
    pallas_call x12, Pallas kernels, call(): pl.pallas_call(body, out_shape=outs, in_specs=[scalars] * smem + [vmem] *...  9.27 us
    ppermute x7, starting transfers between devices, swap(): return lax.ppermute(value, 'dp', [(0, 1), (1, 0)])  3.55 us
  transfers between devices with their start and end apart: 34, of which 14 were waited for; matrix products, arithmetic and copies ran while one was open for 0% of the time, Pallas kernels for 9%

profile of v5, /device:TPU:0, one launch (start us, length us, event | category | flops | bytes accessed | tf_op | source)
XLA Modules:
  0.0 82.2 jit_solution(15151961894002940227)
XLA Ops:
  0.7 1.0 %constant_dynamic-slice_fusion.2 = (bf16[1,128,512]{2,1,0:T(8,128)(2,1)S(1)}, bf16[1,128,512]{2,1,0:T(8,128)(2,1)S(1)}) fusion(bf16[1,128,1024]{2,1,0:T(8,128)(2,1)} %param.7, s32[]{:T(128)S(6)} %select_n.5, s32[]{:T(128)S(6)} %select_n.4), kind=kLoop, calls=%fused_computation.4 | loop fusion | bytes 524296 | tf_op jit(solution)/shard_map/dynamic_slice | solution.py:462
  1.7 0.1 copy-done.5
  1.8 0.0 copy-start
  1.9 0.5 collective-permute-start
  2.4 0.4 copy-done
  2.9 0.5 collective-permute-start.1
  3.4 1.1 %collective-permute-done.1.refs_1_.refs_6_ = bf16[128,1024]{1,0:T(8,128)(2,1)S(1)} collective-permute-done((bf16[128,1024]{1,0:T(8,128)(2,1)S(1)}, bf16[128,1024]{1,0:T(8,128)(2,1)S(1)}, u32[]{:S(2)}, u32[]{:S(2)}) %collective-permute-start.1) | collective-permute-done | bytes 262176 | tf_op jit(solution)/shard_map/ppermute | solution.py:438
  4.5 0.8 %att_grad.1.refs_2_.refs_3_ = bf16[2,128,512]{2,1,0:T(8,128)(2,1)S(1)} custom-call(bf16[128,1024]{1,0:T(8,128)(2,1)S(1)} %bitcast.5, bf16[128,1024]{1,0:T(8,128)(2,1)S(1)} %collective-permute-done.1.refs_1_.refs_6_, bf16[512,1024]{1,0:T(8,128)(2,1)S(1)} %copy-done.1), custom_call_target="tpu_custom_call" | custom-call | tf_op jit(solution)/shard_map/att_grad/pallas_call | solution.py:52
  5.3 0.2 pack_fields.1
  5.5 2.9 %collective-permute-start.2 = (bf16[1024,128]{1,0:T(8,128)(2,1)S(1)}, bf16[1024,128]{1,0:T(8,128)(2,1)S(1)}, u32[]{:S(2)}, u32[]{:S(2)}) collective-permute-start(bf16[1024,128]{1,0:T(8,128)(2,1)S(1)} %get-tuple-element.41), channel_id=1, source_target_pairs={{0,1},{1,0},{2,3},{3,2},{4,5},{5,4},{6,7},{7,6},{8,9},{9,8},{10,11... | collective-permute-start | bytes 786440 | tf_op jit(solution)/shard_map/ppermute | solution.py:435
  8.4 1.5 %collective-permute-start.3 = (bf16[1024,128]{1,0:T(8,128)(2,1)S(1)}, bf16[1024,128]{1,0:T(8,128)(2,1)S(1)}, u32[]{:S(2)}, u32[]{:S(2)}) collective-permute-start(bf16[1024,128]{1,0:T(8,128)(2,1)S(1)} %get-tuple-element.42), channel_id=1, source_target_pairs={{0,2},{1,3},{2,0},{3,1},{4,6},{5,7},{6,4},{7,5},{8,10},{9,11},{10,... | collective-permute-start | bytes 786440 | tf_op jit(solution)/shard_map/ppermute | solution.py:435
  9.9 0.0 collective-permute-start.4
  10.0 1.9 %collective-permute-start.12 = (bf16[128,1024]{1,0:T(8,128)(2,1)S(1)}, bf16[128,1024]{1,0:T(8,128)(2,1)S(1)}, u32[]{:S(2)}, u32[]{:S(2)}) collective-permute-start(bf16[128,1024]{1,0:T(8,128)(2,1)S(1)} %bitcast.6), channel_id=1, source_target_pairs={{0,1},{1,0},{2,3},{3,2},{4,5},{5,4},{6,7},{7,6},{8,9},{9,8},{10,11... | collective-permute-start | bytes 786440 | tf_op jit(solution)/shard_map/ppermute | solution.py:435
  11.9 1.5 %collective-permute-start.13 = (bf16[128,1024]{1,0:T(8,128)(2,1)S(1)}, bf16[128,1024]{1,0:T(8,128)(2,1)S(1)}, u32[]{:S(2)}, u32[]{:S(2)}) collective-permute-start(bf16[128,1024]{1,0:T(8,128)(2,1)S(1)} %bitcast.7), channel_id=1, source_target_pairs={{0,2},{1,3},{2,0},{3,1},{4,6},{5,7},{6,4},{7,5},{8,10},{9,11},{10,... | collective-permute-start | bytes 786440 | tf_op jit(solution)/shard_map/ppermute | solution.py:435
  13.4 2.3 %collective-permute-start.14 = (bf16[128,1024]{1,0:T(8,128)(2,1)S(1)}, bf16[128,1024]{1,0:T(8,128)(2,1)S(1)}, u32[]{:S(2)}, u32[]{:S(2)}) collective-permute-start(bf16[128,1024]{1,0:T(8,128)(2,1)S(1)} %bitcast.8), channel_id=1, source_target_pairs={{0,3},{1,2},{2,1},{3,0},{4,7},{5,6},{6,5},{7,4},{8,11},{9,10},{10,... | collective-permute-start | bytes 786440 | tf_op jit(solution)/shard_map/ppermute | solution.py:435
  15.8 0.6 collective-permute-done.3.refs_5_
  16.3 3.8 %collective-permute-done.4.refs_6_ = bf16[1024,128]{1,0:T(8,128)(2,1)S(1)} collective-permute-done((bf16[1024,128]{1,0:T(8,128)(2,1)S(1)}, bf16[1024,128]{1,0:T(8,128)(2,1)S(1)}, u32[]{:S(2)}, u32[]{:S(2)}) %collective-permute-start.4) | collective-permute-done | bytes 262176 | tf_op jit(solution)/shard_map/ppermute | solution.py:435
  20.1 0.7 forward.1
  20.8 4.3 %collective-permute-start.5 = (bf16[2048,128]{1,0:T(8,128)(2,1)S(1)}, bf16[2048,128]{1,0:T(8,128)(2,1)S(1)}, u32[]{:S(2)}, u32[]{:S(2)}) collective-permute-start(bf16[2048,128]{1,0:T(8,128)(2,1)S(1)} %get-tuple-element.45.refs_2_.refs_1_), channel_id=1, source_target_pairs={{0,4},{1,5},{2,6},{3,7},{4,8},{5,9},{6,10},{7,11},{8,12},{9,13},{1... | collective-permute-start | bytes 1572872 | tf_op jit(solution)/shard_map/ppermute | solution.py:435
  25.1 1.3 %collective-permute-start.21 = (bf16[2048,128]{1,0:T(8,128)(2,1)S(1)}, bf16[2048,128]{1,0:T(8,128)(2,1)S(1)}, u32[]{:S(2)}, u32[]{:S(2)}) collective-permute-start(bf16[2048,128]{1,0:T(8,128)(2,1)S(1)} %copy.12), channel_id=1, source_target_pairs={{4,0},{5,1},{6,2},{7,3},{8,4},{9,5},{10,6},{11,7},{12,8},{13,9},{1... | collective-permute-start | bytes 1572872 | tf_op jit(solution)/shard_map/ppermute | solution.py:435
  26.4 1.6 %collective-permute-start.6 = (bf16[256,128]{1,0:T(8,128)(2,1)S(1)}, bf16[256,128]{1,0:T(8,128)(2,1)S(1)}, u32[]{:S(2)}, u32[]{:S(2)}) collective-permute-start(bf16[256,128]{1,0:T(8,128)(2,1)S(1)} %get-tuple-element.48), channel_id=1, source_target_pairs={{0,1},{1,0},{2,3},{3,2},{4,5},{5,4},{6,7},{7,6},{8,9},{9,8},{10,11... | collective-permute-start | bytes 196616 | tf_op jit(solution)/shard_map/ppermute | solution.py:435
  28.0 0.8 %collective-permute-done.13.refs_8_ = bf16[128,1024]{1,0:T(8,128)(2,1)S(1)} collective-permute-done((bf16[128,1024]{1,0:T(8,128)(2,1)S(1)}, bf16[128,1024]{1,0:T(8,128)(2,1)S(1)}, u32[]{:S(2)}, u32[]{:S(2)}) %collective-permute-start.13) | collective-permute-done | bytes 262176 | tf_op jit(solution)/shard_map/ppermute | solution.py:435
  28.8 1.5 %collective-permute-start.7 = (bf16[256,128]{1,0:T(8,128)(2,1)S(1)}, bf16[256,128]{1,0:T(8,128)(2,1)S(1)}, u32[]{:S(2)}, u32[]{:S(2)}) collective-permute-start(bf16[256,128]{1,0:T(8,128)(2,1)S(1)} %get-tuple-element.49), channel_id=1, source_target_pairs={{0,2},{1,3},{2,0},{3,1},{4,6},{5,7},{6,4},{7,5},{8,10},{9,11},{10,... | collective-permute-start | bytes 196616 | tf_op jit(solution)/shard_map/ppermute | solution.py:435
  30.4 0.4 collective-permute-done.6.refs_1_
  30.8 1.2 %collective-permute-start.15 = (bf16[128,1024]{1,0:T(8,128)(2,1)S(1)}, bf16[128,1024]{1,0:T(8,128)(2,1)S(1)}, u32[]{:S(2)}, u32[]{:S(2)}) collective-permute-start(bf16[128,1024]{1,0:T(8,128)(2,1)S(1)} %collective-permute-done.12.refs_7_), channel_id=1, source_target_pairs={{0,16},{16,0},{1,17},{17,1},{2,18},{18,2},{3,19},{19,3},{4,20},{20... | collective-permute-start | bytes 786440 | tf_op jit(solution)/shard_map/ppermute | solution.py:438
  32.0 1.1 %collective-permute-done.7.refs_2_ = bf16[256,128]{1,0:T(8,128)(2,1)S(1)} collective-permute-done((bf16[256,128]{1,0:T(8,128)(2,1)S(1)}, bf16[256,128]{1,0:T(8,128)(2,1)S(1)}, u32[]{:S(2)}, u32[]{:S(2)}) %collective-permute-start.7) | collective-permute-done | bytes 65568 | tf_op jit(solution)/shard_map/ppermute | solution.py:435
  33.1 0.6 collective-permute-start.16
  33.7 1.8 %collective-permute-done.8.refs_3_ = bf16[256,128]{1,0:T(8,128)(2,1)S(1)} collective-permute-done((bf16[256,128]{1,0:T(8,128)(2,1)S(1)}, bf16[256,128]{1,0:T(8,128)(2,1)S(1)}, u32[]{:S(2)}, u32[]{:S(2)}) %collective-permute-start.8) | collective-permute-done | bytes 65568 | tf_op jit(solution)/shard_map/ppermute | solution.py:435
  35.5 0.2 collective-permute-start.17
  35.8 1.5 %collective-permute-start.10 = (bf16[256,128]{1,0:T(8,128)(2,1)S(1)}, bf16[256,128]{1,0:T(8,128)(2,1)S(1)}, u32[]{:S(2)}, u32[]{:S(2)}) collective-permute-start(bf16[256,128]{1,0:T(8,128)(2,1)S(1)} %get-tuple-element.53), channel_id=1, source_target_pairs={{0,2},{1,3},{2,0},{3,1},{4,6},{5,7},{6,4},{7,5},{8,10},{9,11},{10,... | collective-permute-start | bytes 196616 | tf_op jit(solution)/shard_map/ppermute | solution.py:435
  37.3 0.0 collective-permute-done.16.refs_11_
  37.3 0.3 collective-permute-start.11
  37.6 1.7 %collective-permute-start.9 = (bf16[256,128]{1,0:T(8,128)(2,1)S(1)}, bf16[256,128]{1,0:T(8,128)(2,1)S(1)}, u32[]{:S(2)}, u32[]{:S(2)}) collective-permute-start(bf16[256,128]{1,0:T(8,128)(2,1)S(1)} %get-tuple-element.52), channel_id=1, source_target_pairs={{0,1},{1,0},{2,3},{3,2},{4,5},{5,4},{6,7},{7,6},{8,9},{9,8},{10,11... | collective-permute-start | bytes 196616 | tf_op jit(solution)/shard_map/ppermute | solution.py:435
  39.3 3.5 %attention.1 = (bf16[2,128,512]{2,1,0:T(8,128)(2,1)S(1)}, bf16[2,512,128]{2,1,0:T(8,128)(2,1)S(1)}, f32[2,2,512,128]{3,2,1,0:T(8,128)S(1)}, f32[48,512]{1,0:T(8,128)S(1)}) custom-call(s32[4]{0:T(128)S(1)} %copy-done.2, bf16[2048,128]{1,0:T(8,128)(2,1)S(1)} %get-tuple-element.44.refs_1_.refs_0_, bf16[2048,128]{1,0:T(8,128)(2,1)S(1)} %get-tuple-element.45.refs_2_.refs_1_, ...), custom_call_target="tpu_custom_call" | custom-call | tf_op jit(solution)/shard_map/attention/pallas_call | solution.py:52
  42.8 0.0 collective-permute-start.22
  42.8 0.0 collective-permute-done.10.refs_3_
  42.8 0.0 collective-permute-done.11.refs_4_
  42.9 0.8 weight.1
  43.6 3.9 %collective-permute-start.20 = (bf16[32,1024]{1,0:T(8,128)(2,1)S(1)}, bf16[32,1024]{1,0:T(8,128)(2,1)S(1)}, u32[]{:S(2)}, u32[]{:S(2)}) collective-permute-start(bf16[32,1024]{1,0:T(8,128)(2,1)S(1)} %get-tuple-element.58), channel_id=1, source_target_pairs={{0,12},{1,13},{2,14},{3,15},{4,8},{5,9},{6,10},{7,11},{8,4},{9,5},... | collective-permute-start | bytes 196616 | tf_op jit(solution)/shard_map/ppermute | solution.py:435
  47.5 0.0 collective-permute-start.18
  47.5 0.6 collective-permute-start.19
  48.2 0.0 collective-permute-done.21.refs_2_
  48.2 3.4 %collective-permute-done.20.refs_5_.refs_3_ = bf16[32,1024]{1,0:T(8,128)(2,1)S(1)} collective-permute-done((bf16[32,1024]{1,0:T(8,128)(2,1)S(1)}, bf16[32,1024]{1,0:T(8,128)(2,1)S(1)}, u32[]{:S(2)}, u32[]{:S(2)}) %collective-permute-start.20) | collective-permute-done | bytes 65568 | tf_op jit(solution)/shard_map/ppermute | solution.py:435
  51.6 1.6 %tail.1.refs_4_.refs_1_ = f32[2,2,512,128]{3,2,1,0:T(8,128)S(1)} custom-call(s32[4]{0:T(128)S(1)} %copy-done.2, bf16[2048,128]{1,0:T(8,128)(2,1)S(1)} %get-tuple-element.45.refs_2_.refs_1_, bf16[2048,128]{1,0:T(8,128)(2,1)S(1)} %collective-permute-done.21.refs_2_, f32[48,512]{1,0:T(8,128)S(1)} %collective-permute-done.22.refs_3_, ...), custom_call_target="tpu_custom_call" | custom-call | tf_op jit(solution)/shard_map/tail/pallas_call | solution.py:52
  53.2 0.3 collective-permute-done.19.refs_2_
  53.5 0.1 exchange.1
  53.6 0.1 collective-permute-start.26
  53.7 0.5 collective-permute-start.27
  54.2 1.3 %collective-permute-start.23 = (bf16[32,1024]{1,0:T(8,128)(2,1)S(1)}, bf16[32,1024]{1,0:T(8,128)(2,1)S(1)}, u32[]{:S(2)}, u32[]{:S(2)}) collective-permute-start(bf16[32,1024]{1,0:T(8,128)(2,1)S(1)} %sum.1.refs_3_.refs_0_), channel_id=1, source_target_pairs={{0,4},{1,5},{2,6},{3,7},{4,0},{5,1},{6,2},{7,3},{8,12},{9,13},{10,... | collective-permute-start | bytes 196616 | tf_op jit(solution)/shard_map/ppermute | solution.py:435
  55.5 1.4 %collective-permute-start.24 = (bf16[32,1024]{1,0:T(8,128)(2,1)S(1)}, bf16[32,1024]{1,0:T(8,128)(2,1)S(1)}, u32[]{:S(2)}, u32[]{:S(2)}) collective-permute-start(bf16[32,1024]{1,0:T(8,128)(2,1)S(1)} %sum.1.refs_3_.refs_0_), channel_id=1, source_target_pairs={{0,8},{1,9},{2,10},{3,11},{4,12},{5,13},{6,14},{7,15},{8,0},{9,1},... | collective-permute-start | bytes 196616 | tf_op jit(solution)/shard_map/ppermute | solution.py:435
  56.8 1.7 %collective-permute-start.25 = (bf16[32,1024]{1,0:T(8,128)(2,1)S(1)}, bf16[32,1024]{1,0:T(8,128)(2,1)S(1)}, u32[]{:S(2)}, u32[]{:S(2)}) collective-permute-start(bf16[32,1024]{1,0:T(8,128)(2,1)S(1)} %sum.1.refs_3_.refs_0_), channel_id=1, source_target_pairs={{0,12},{1,13},{2,14},{3,15},{4,8},{5,9},{6,10},{7,11},{8,4},{9,5},... | collective-permute-start | bytes 196616 | tf_op jit(solution)/shard_map/ppermute | solution.py:435
  58.6 5.0 %collective-permute-done.24.refs_2_ = bf16[32,1024]{1,0:T(8,128)(2,1)S(1)} collective-permute-done((bf16[32,1024]{1,0:T(8,128)(2,1)S(1)}, bf16[32,1024]{1,0:T(8,128)(2,1)S(1)}, u32[]{:S(2)}, u32[]{:S(2)}) %collective-permute-start.24) | collective-permute-done | bytes 65568 | tf_op jit(solution)/shard_map/ppermute | solution.py:435
  63.6 0.3 gather_line.1
  63.9 0.6 collective-permute-start.28
  64.5 1.3 %collective-permute-start.29 = (bf16[1408,128]{1,0:T(8,128)(2,1)S(1)}, bf16[1408,128]{1,0:T(8,128)(2,1)S(1)}, u32[]{:S(2)}, u32[]{:S(2)}) collective-permute-start(bf16[1408,128]{1,0:T(8,128)(2,1)S(1)} %get-tuple-element.68), channel_id=1, source_target_pairs={{0,2},{1,3},{2,0},{3,1},{4,6},{5,7},{6,4},{7,5},{8,10},{9,11},{10,... | collective-permute-start | bytes 1081352 | tf_op jit(solution)/shard_map/ppermute | solution.py:435
  65.8 1.7 %collective-permute-start.30 = (bf16[1408,128]{1,0:T(8,128)(2,1)S(1)}, bf16[1408,128]{1,0:T(8,128)(2,1)S(1)}, u32[]{:S(2)}, u32[]{:S(2)}) collective-permute-start(bf16[1408,128]{1,0:T(8,128)(2,1)S(1)} %get-tuple-element.69), channel_id=1, source_target_pairs={{0,3},{1,2},{2,1},{3,0},{4,7},{5,6},{6,5},{7,4},{8,11},{9,10},{10,... | collective-permute-start | bytes 1081352 | tf_op jit(solution)/shard_map/ppermute | solution.py:435
  67.4 1.3 %collective-permute-start.31 = (bf16[384,128]{1,0:T(8,128)(2,1)S(1)}, bf16[384,128]{1,0:T(8,128)(2,1)S(1)}, u32[]{:S(2)}, u32[]{:S(2)}) collective-permute-start(bf16[384,128]{1,0:T(8,128)(2,1)S(1)} %get-tuple-element.71), channel_id=1, source_target_pairs={{0,4},{1,5},{2,6},{3,7},{4,0},{5,1},{6,2},{7,3},{8,12},{9,13},{10,... | collective-permute-start | bytes 294920 | tf_op jit(solution)/shard_map/ppermute | solution.py:435
  68.8 1.4 %collective-permute-start.32 = (bf16[384,128]{1,0:T(8,128)(2,1)S(1)}, bf16[384,128]{1,0:T(8,128)(2,1)S(1)}, u32[]{:S(2)}, u32[]{:S(2)}) collective-permute-start(bf16[384,128]{1,0:T(8,128)(2,1)S(1)} %get-tuple-element.72), channel_id=1, source_target_pairs={{0,8},{1,9},{2,10},{3,11},{4,12},{5,13},{6,14},{7,15},{8,0},{9,1},... | collective-permute-start | bytes 294920 | tf_op jit(solution)/shard_map/ppermute | solution.py:435
  70.1 2.8 %collective-permute-done.31.refs_5_ = bf16[384,128]{1,0:T(8,128)(2,1)S(1)} collective-permute-done((bf16[384,128]{1,0:T(8,128)(2,1)S(1)}, bf16[384,128]{1,0:T(8,128)(2,1)S(1)}, u32[]{:S(2)}, u32[]{:S(2)}) %collective-permute-start.31) | collective-permute-done | bytes 98336 | tf_op jit(solution)/shard_map/ppermute | solution.py:435
  72.9 1.7 %collective-permute-start.33 = (bf16[384,128]{1,0:T(8,128)(2,1)S(1)}, bf16[384,128]{1,0:T(8,128)(2,1)S(1)}, u32[]{:S(2)}, u32[]{:S(2)}) collective-permute-start(bf16[384,128]{1,0:T(8,128)(2,1)S(1)} %get-tuple-element.73), channel_id=1, source_target_pairs={{0,12},{1,13},{2,14},{3,15},{4,8},{5,9},{6,10},{7,11},{8,4},{9,5},... | collective-permute-start | bytes 294920 | tf_op jit(solution)/shard_map/ppermute | solution.py:435
  74.6 2.8 %collective-permute-done.32.refs_6_ = bf16[384,128]{1,0:T(8,128)(2,1)S(1)} collective-permute-done((bf16[384,128]{1,0:T(8,128)(2,1)S(1)}, bf16[384,128]{1,0:T(8,128)(2,1)S(1)}, u32[]{:S(2)}, u32[]{:S(2)}) %collective-permute-start.32) | collective-permute-done | bytes 98336 | tf_op jit(solution)/shard_map/ppermute | solution.py:435
  77.4 2.0 %collective-permute-done.33.refs_7_ = bf16[384,128]{1,0:T(8,128)(2,1)S(1)} collective-permute-done((bf16[384,128]{1,0:T(8,128)(2,1)S(1)}, bf16[384,128]{1,0:T(8,128)(2,1)S(1)}, u32[]{:S(2)}, u32[]{:S(2)}) %collective-permute-start.33) | collective-permute-done | bytes 98336 | tf_op jit(solution)/shard_map/ppermute | solution.py:435
  79.4 1.4 %collective-permute-done.30.refs_3_ = bf16[1408,128]{1,0:T(8,128)(2,1)S(1)} collective-permute-done((bf16[1408,128]{1,0:T(8,128)(2,1)S(1)}, bf16[1408,128]{1,0:T(8,128)(2,1)S(1)}, u32[]{:S(2)}, u32[]{:S(2)}) %collective-permute-start.30) | collective-permute-done | bytes 360480 | tf_op jit(solution)/shard_map/ppermute | solution.py:435
  80.8 1.3 %finish.1 = (bf16[128,1024]{1,0:T(8,128)(2,1)}, bf16[128,1024]{1,0:T(8,128)(2,1)}, bf16[128,1024]{1,0:T(8,128)(2,1)}, bf16[512,1024]{1,0:T(8,128)(2,1)}) custom-call(bf16[1408,128]{1,0:T(8,128)(2,1)S(1)} %get-tuple-element.66.refs_0_, bf16[1408,128]{1,0:T(8,128)(2,1)S(1)} %collective-permute-done.28.refs_1_, ...), custom_call_target="tpu_custom_call" | custom-call | tf_op jit(solution)/shard_map/finish/pallas_call | solution.py:52
  (32 shorter events, 0.3 us)
Async XLA Ops:
  0.6 1.1 %copy-start.4 = (bf16[1,128,1024]{2,1,0:T(8,128)(2,1)S(1)}, bf16[1,128,1024]{2,1,0:T(8,128)(2,1)}, u32[]{:S(2)}) copy-start(bf16[1,128,1024]{2,1,0:T(8,128)(2,1)} %param.9) | copy-start | bytes 786436
  0.6 1.1 %copy-start.5 = (bf16[1,128,1024]{2,1,0:T(8,128)(2,1)S(1)}, bf16[1,128,1024]{2,1,0:T(8,128)(2,1)}, u32[]{:S(2)}) copy-start(bf16[1,128,1024]{2,1,0:T(8,128)(2,1)} %param.8) | copy-start | bytes 786436
  1.8 2.7 %copy-start.1 = (bf16[512,1024]{1,0:T(8,128)(2,1)S(1)}, bf16[512,1024]{1,0:T(8,128)(2,1)}, u32[]{:S(2)}) copy-start(bf16[512,1024]{1,0:T(8,128)(2,1)} %refs_2_.1) | copy-start | bytes 3145732
  1.8 1.0 %copy-start = (bf16[1,128,1024]{2,1,0:T(8,128)(2,1)S(1)}, bf16[1,128,1024]{2,1,0:T(8,128)(2,1)}, u32[]{:S(2)}) copy-start(bf16[1,128,1024]{2,1,0:T(8,128)(2,1)} %param.10) | copy-start | bytes 786436
  1.9 3.4 %collective-permute-start = (bf16[3,128,512]{2,1,0:T(8,128)(2,1)S(1)}, bf16[3,128,512]{2,1,0:T(8,128)(2,1)S(1)}, u32[]{:S(2)}, u32[]{:S(2)}) collective-permute-start(bf16[3,128,512]{2,1,0:T(8,128)(2,1)S(1)} %pad_maximum_fusion.1), channel_id=1, source_target_pairs={{0,16},{16,0},{1,17},{17,1},{2,18},{18,2},{3,19},{19,3},{4,20},{20... | collective-permute-start | bytes 1179656 | tf_op jit(solution)/shard_map/ppermute | solution.py:438
  2.9 1.6 %collective-permute-start.1 = (bf16[128,1024]{1,0:T(8,128)(2,1)S(1)}, bf16[128,1024]{1,0:T(8,128)(2,1)S(1)}, u32[]{:S(2)}, u32[]{:S(2)}) collective-permute-start(bf16[128,1024]{1,0:T(8,128)(2,1)S(1)} %bitcast.4), channel_id=1, source_target_pairs={{0,16},{16,0},{1,17},{17,1},{2,18},{18,2},{3,19},{19,3},{4,20},{20... | collective-permute-start | bytes 786440 | tf_op jit(solution)/shard_map/ppermute | solution.py:438
  5.5 7.9 %collective-permute-start.2 = (bf16[1024,128]{1,0:T(8,128)(2,1)S(1)}, bf16[1024,128]{1,0:T(8,128)(2,1)S(1)}, u32[]{:S(2)}, u32[]{:S(2)}) collective-permute-start(bf16[1024,128]{1,0:T(8,128)(2,1)S(1)} %get-tuple-element.41), channel_id=1, source_target_pairs={{0,1},{1,0},{2,3},{3,2},{4,5},{5,4},{6,7},{7,6},{8,9},{9,8},{10,11... | collective-permute-start | bytes 786440 | tf_op jit(solution)/shard_map/ppermute | solution.py:435
  8.4 11.7 %copy-start.3 = (s32[4]{0:T(128)S(1)}, s32[4]{0:T(128)}, u32[]{:S(2)}) copy-start(s32[4]{0:T(128)} %refs_0_.3) | copy-start | bytes 52
  8.4 7.9 %collective-permute-start.3 = (bf16[1024,128]{1,0:T(8,128)(2,1)S(1)}, bf16[1024,128]{1,0:T(8,128)(2,1)S(1)}, u32[]{:S(2)}, u32[]{:S(2)}) collective-permute-start(bf16[1024,128]{1,0:T(8,128)(2,1)S(1)} %get-tuple-element.42), channel_id=1, source_target_pairs={{0,2},{1,3},{2,0},{3,1},{4,6},{5,7},{6,4},{7,5},{8,10},{9,11},{10,... | collective-permute-start | bytes 786440 | tf_op jit(solution)/shard_map/ppermute | solution.py:435
  9.9 10.2 %collective-permute-start.4 = (bf16[1024,128]{1,0:T(8,128)(2,1)S(1)}, bf16[1024,128]{1,0:T(8,128)(2,1)S(1)}, u32[]{:S(2)}, u32[]{:S(2)}) collective-permute-start(bf16[1024,128]{1,0:T(8,128)(2,1)S(1)} %get-tuple-element.43), channel_id=1, source_target_pairs={{0,3},{1,2},{2,1},{3,0},{4,7},{5,6},{6,5},{7,4},{8,11},{9,10},{10,... | collective-permute-start | bytes 786440 | tf_op jit(solution)/shard_map/ppermute | solution.py:435
  10.0 16.5 %collective-permute-start.12 = (bf16[128,1024]{1,0:T(8,128)(2,1)S(1)}, bf16[128,1024]{1,0:T(8,128)(2,1)S(1)}, u32[]{:S(2)}, u32[]{:S(2)}) collective-permute-start(bf16[128,1024]{1,0:T(8,128)(2,1)S(1)} %bitcast.6), channel_id=1, source_target_pairs={{0,1},{1,0},{2,3},{3,2},{4,5},{5,4},{6,7},{7,6},{8,9},{9,8},{10,11... | collective-permute-start | bytes 786440 | tf_op jit(solution)/shard_map/ppermute | solution.py:435
  11.9 16.9 %collective-permute-start.13 = (bf16[128,1024]{1,0:T(8,128)(2,1)S(1)}, bf16[128,1024]{1,0:T(8,128)(2,1)S(1)}, u32[]{:S(2)}, u32[]{:S(2)}) collective-permute-start(bf16[128,1024]{1,0:T(8,128)(2,1)S(1)} %bitcast.7), channel_id=1, source_target_pairs={{0,2},{1,3},{2,0},{3,1},{4,6},{5,7},{6,4},{7,5},{8,10},{9,11},{10,... | collective-permute-start | bytes 786440 | tf_op jit(solution)/shard_map/ppermute | solution.py:435
  13.4 16.9 %collective-permute-start.14 = (bf16[128,1024]{1,0:T(8,128)(2,1)S(1)}, bf16[128,1024]{1,0:T(8,128)(2,1)S(1)}, u32[]{:S(2)}, u32[]{:S(2)}) collective-permute-start(bf16[128,1024]{1,0:T(8,128)(2,1)S(1)} %bitcast.8), channel_id=1, source_target_pairs={{0,3},{1,2},{2,1},{3,0},{4,7},{5,6},{6,5},{7,4},{8,11},{9,10},{10,... | collective-permute-start | bytes 786440 | tf_op jit(solution)/shard_map/ppermute | solution.py:435
  20.8 16.8 %collective-permute-start.5 = (bf16[2048,128]{1,0:T(8,128)(2,1)S(1)}, bf16[2048,128]{1,0:T(8,128)(2,1)S(1)}, u32[]{:S(2)}, u32[]{:S(2)}) collective-permute-start(bf16[2048,128]{1,0:T(8,128)(2,1)S(1)} %get-tuple-element.45.refs_2_.refs_1_), channel_id=1, source_target_pairs={{0,4},{1,5},{2,6},{3,7},{4,8},{5,9},{6,10},{7,11},{8,12},{9,13},{1... | collective-permute-start | bytes 1572872 | tf_op jit(solution)/shard_map/ppermute | solution.py:435
  25.1 23.0 %collective-permute-start.21 = (bf16[2048,128]{1,0:T(8,128)(2,1)S(1)}, bf16[2048,128]{1,0:T(8,128)(2,1)S(1)}, u32[]{:S(2)}, u32[]{:S(2)}) collective-permute-start(bf16[2048,128]{1,0:T(8,128)(2,1)S(1)} %copy.12), channel_id=1, source_target_pairs={{4,0},{5,1},{6,2},{7,3},{8,4},{9,5},{10,6},{11,7},{12,8},{13,9},{1... | collective-permute-start | bytes 1572872 | tf_op jit(solution)/shard_map/ppermute | solution.py:435
  26.4 4.3 %collective-permute-start.6 = (bf16[256,128]{1,0:T(8,128)(2,1)S(1)}, bf16[256,128]{1,0:T(8,128)(2,1)S(1)}, u32[]{:S(2)}, u32[]{:S(2)}) collective-permute-start(bf16[256,128]{1,0:T(8,128)(2,1)S(1)} %get-tuple-element.48), channel_id=1, source_target_pairs={{0,1},{1,0},{2,3},{3,2},{4,5},{5,4},{6,7},{7,6},{8,9},{9,8},{10,11... | collective-permute-start | bytes 196616 | tf_op jit(solution)/shard_map/ppermute | solution.py:435
  28.8 4.3 %collective-permute-start.7 = (bf16[256,128]{1,0:T(8,128)(2,1)S(1)}, bf16[256,128]{1,0:T(8,128)(2,1)S(1)}, u32[]{:S(2)}, u32[]{:S(2)}) collective-permute-start(bf16[256,128]{1,0:T(8,128)(2,1)S(1)} %get-tuple-element.49), channel_id=1, source_target_pairs={{0,2},{1,3},{2,0},{3,1},{4,6},{5,7},{6,4},{7,5},{8,10},{9,11},{10,... | collective-permute-start | bytes 196616 | tf_op jit(solution)/shard_map/ppermute | solution.py:435
  30.4 5.2 %collective-permute-start.8 = (bf16[256,128]{1,0:T(8,128)(2,1)S(1)}, bf16[256,128]{1,0:T(8,128)(2,1)S(1)}, u32[]{:S(2)}, u32[]{:S(2)}) collective-permute-start(bf16[256,128]{1,0:T(8,128)(2,1)S(1)} %get-tuple-element.50), channel_id=1, source_target_pairs={{0,3},{1,2},{2,1},{3,0},{4,7},{5,6},{6,5},{7,4},{8,11},{9,10},{10,... | collective-permute-start | bytes 196616 | tf_op jit(solution)/shard_map/ppermute | solution.py:435
  30.8 5.0 %collective-permute-start.15 = (bf16[128,1024]{1,0:T(8,128)(2,1)S(1)}, bf16[128,1024]{1,0:T(8,128)(2,1)S(1)}, u32[]{:S(2)}, u32[]{:S(2)}) collective-permute-start(bf16[128,1024]{1,0:T(8,128)(2,1)S(1)} %collective-permute-done.12.refs_7_), channel_id=1, source_target_pairs={{0,16},{16,0},{1,17},{17,1},{2,18},{18,2},{3,19},{19,3},{4,20},{20... | collective-permute-start | bytes 786440 | tf_op jit(solution)/shard_map/ppermute | solution.py:438
  33.1 4.2 %collective-permute-start.16 = (bf16[128,1024]{1,0:T(8,128)(2,1)S(1)}, bf16[128,1024]{1,0:T(8,128)(2,1)S(1)}, u32[]{:S(2)}, u32[]{:S(2)}) collective-permute-start(bf16[128,1024]{1,0:T(8,128)(2,1)S(1)} %collective-permute-done.13.refs_8_), channel_id=1, source_target_pairs={{0,16},{16,0},{1,17},{17,1},{2,18},{18,2},{3,19},{19,3},{4,20},{20... | collective-permute-start | bytes 786440 | tf_op jit(solution)/shard_map/ppermute | solution.py:438
  35.5 7.3 %collective-permute-start.17 = (bf16[128,1024]{1,0:T(8,128)(2,1)S(1)}, bf16[128,1024]{1,0:T(8,128)(2,1)S(1)}, u32[]{:S(2)}, u32[]{:S(2)}) collective-permute-start(bf16[128,1024]{1,0:T(8,128)(2,1)S(1)} %collective-permute-done.14.refs_9_), channel_id=1, source_target_pairs={{0,16},{16,0},{1,17},{17,1},{2,18},{18,2},{3,19},{19,3},{4,20},{20... | collective-permute-start | bytes 786440 | tf_op jit(solution)/shard_map/ppermute | solution.py:438
  35.8 7.1 %collective-permute-start.10 = (bf16[256,128]{1,0:T(8,128)(2,1)S(1)}, bf16[256,128]{1,0:T(8,128)(2,1)S(1)}, u32[]{:S(2)}, u32[]{:S(2)}) collective-permute-start(bf16[256,128]{1,0:T(8,128)(2,1)S(1)} %get-tuple-element.53), channel_id=1, source_target_pairs={{0,2},{1,3},{2,0},{3,1},{4,6},{5,7},{6,4},{7,5},{8,10},{9,11},{10,... | collective-permute-start | bytes 196616 | tf_op jit(solution)/shard_map/ppermute | solution.py:435
  37.3 2.0 %copy-start.2 = (s32[4]{0:T(128)S(1)}, s32[4]{0:T(128)}, u32[]{:S(2)}) copy-start(s32[4]{0:T(128)} %refs_0_.5) | copy-start | bytes 52
  37.3 5.6 %collective-permute-start.11 = (bf16[256,128]{1,0:T(8,128)(2,1)S(1)}, bf16[256,128]{1,0:T(8,128)(2,1)S(1)}, u32[]{:S(2)}, u32[]{:S(2)}) collective-permute-start(bf16[256,128]{1,0:T(8,128)(2,1)S(1)} %get-tuple-element.54), channel_id=1, source_target_pairs={{0,3},{1,2},{2,1},{3,0},{4,7},{5,6},{6,5},{7,4},{8,11},{9,10},{10,... | collective-permute-start | bytes 196616 | tf_op jit(solution)/shard_map/ppermute | solution.py:435
  37.6 5.2 %collective-permute-start.9 = (bf16[256,128]{1,0:T(8,128)(2,1)S(1)}, bf16[256,128]{1,0:T(8,128)(2,1)S(1)}, u32[]{:S(2)}, u32[]{:S(2)}) collective-permute-start(bf16[256,128]{1,0:T(8,128)(2,1)S(1)} %get-tuple-element.52), channel_id=1, source_target_pairs={{0,1},{1,0},{2,3},{3,2},{4,5},{5,4},{6,7},{7,6},{8,9},{9,8},{10,11... | collective-permute-start | bytes 196616 | tf_op jit(solution)/shard_map/ppermute | solution.py:435
  42.8 8.8 %collective-permute-start.22 = (f32[48,512]{1,0:T(8,128)S(1)}, f32[48,512]{1,0:T(8,128)S(1)}, u32[]{:S(2)}, u32[]{:S(2)}) collective-permute-start(f32[48,512]{1,0:T(8,128)S(1)} %get-tuple-element.59), channel_id=1, source_target_pairs={{0,16},{1,17},{2,18},{3,19},{4,0},{5,1},{6,2},{7,3},{8,4},{9,5},{1... | collective-permute-start | bytes 294920 | tf_op jit(solution)/shard_map/ppermute | solution.py:435
  43.6 8.0 %collective-permute-start.20 = (bf16[32,1024]{1,0:T(8,128)(2,1)S(1)}, bf16[32,1024]{1,0:T(8,128)(2,1)S(1)}, u32[]{:S(2)}, u32[]{:S(2)}) collective-permute-start(bf16[32,1024]{1,0:T(8,128)(2,1)S(1)} %get-tuple-element.58), channel_id=1, source_target_pairs={{0,12},{1,13},{2,14},{3,15},{4,8},{5,9},{6,10},{7,11},{8,4},{9,5},... | collective-permute-start | bytes 196616 | tf_op jit(solution)/shard_map/ppermute | solution.py:435
  47.5 5.6 %collective-permute-start.18 = (bf16[32,1024]{1,0:T(8,128)(2,1)S(1)}, bf16[32,1024]{1,0:T(8,128)(2,1)S(1)}, u32[]{:S(2)}, u32[]{:S(2)}) collective-permute-start(bf16[32,1024]{1,0:T(8,128)(2,1)S(1)} %get-tuple-element.56), channel_id=1, source_target_pairs={{0,4},{1,5},{2,6},{3,7},{4,0},{5,1},{6,2},{7,3},{8,12},{9,13},{10,... | collective-permute-start | bytes 196616 | tf_op jit(solution)/shard_map/ppermute | solution.py:435
  47.5 5.9 %collective-permute-start.19 = (bf16[32,1024]{1,0:T(8,128)(2,1)S(1)}, bf16[32,1024]{1,0:T(8,128)(2,1)S(1)}, u32[]{:S(2)}, u32[]{:S(2)}) collective-permute-start(bf16[32,1024]{1,0:T(8,128)(2,1)S(1)} %get-tuple-element.57), channel_id=1, source_target_pairs={{0,8},{1,9},{2,10},{3,11},{4,12},{5,13},{6,14},{7,15},{8,0},{9,1},... | collective-permute-start | bytes 196616 | tf_op jit(solution)/shard_map/ppermute | solution.py:435
  53.6 10.0 %collective-permute-start.26 = (bf16[3,256,128]{2,1,0:T(8,128)(2,1)S(1)}, bf16[3,256,128]{2,1,0:T(8,128)(2,1)S(1)}, u32[]{:S(2)}, u32[]{:S(2)}) collective-permute-start(bf16[3,256,128]{2,1,0:T(8,128)(2,1)S(1)} %get-tuple-element.64), channel_id=1, source_target_pairs={{0,16},{16,0},{1,17},{17,1},{2,18},{18,2},{3,19},{19,3},{4,20},{20... | collective-permute-start | bytes 589832 | tf_op jit(solution)/shard_map/ppermute | solution.py:438
  53.7 9.9 %collective-permute-start.27 = (bf16[3,256,128]{2,1,0:T(8,128)(2,1)S(1)}, bf16[3,256,128]{2,1,0:T(8,128)(2,1)S(1)}, u32[]{:S(2)}, u32[]{:S(2)}) collective-permute-start(bf16[3,256,128]{2,1,0:T(8,128)(2,1)S(1)} %get-tuple-element.65), channel_id=1, source_target_pairs={{0,16},{16,0},{1,17},{17,1},{2,18},{18,2},{3,19},{19,3},{4,20},{20... | collective-permute-start | bytes 589832 | tf_op jit(solution)/shard_map/ppermute | solution.py:438
  54.2 4.4 %collective-permute-start.23 = (bf16[32,1024]{1,0:T(8,128)(2,1)S(1)}, bf16[32,1024]{1,0:T(8,128)(2,1)S(1)}, u32[]{:S(2)}, u32[]{:S(2)}) collective-permute-start(bf16[32,1024]{1,0:T(8,128)(2,1)S(1)} %sum.1.refs_3_.refs_0_), channel_id=1, source_target_pairs={{0,4},{1,5},{2,6},{3,7},{4,0},{5,1},{6,2},{7,3},{8,12},{9,13},{10,... | collective-permute-start | bytes 196616 | tf_op jit(solution)/shard_map/ppermute | solution.py:435
  55.5 8.1 %collective-permute-start.24 = (bf16[32,1024]{1,0:T(8,128)(2,1)S(1)}, bf16[32,1024]{1,0:T(8,128)(2,1)S(1)}, u32[]{:S(2)}, u32[]{:S(2)}) collective-permute-start(bf16[32,1024]{1,0:T(8,128)(2,1)S(1)} %sum.1.refs_3_.refs_0_), channel_id=1, source_target_pairs={{0,8},{1,9},{2,10},{3,11},{4,12},{5,13},{6,14},{7,15},{8,0},{9,1},... | collective-permute-start | bytes 196616 | tf_op jit(solution)/shard_map/ppermute | solution.py:435
  56.8 6.8 %collective-permute-start.25 = (bf16[32,1024]{1,0:T(8,128)(2,1)S(1)}, bf16[32,1024]{1,0:T(8,128)(2,1)S(1)}, u32[]{:S(2)}, u32[]{:S(2)}) collective-permute-start(bf16[32,1024]{1,0:T(8,128)(2,1)S(1)} %sum.1.refs_3_.refs_0_), channel_id=1, source_target_pairs={{0,12},{1,13},{2,14},{3,15},{4,8},{5,9},{6,10},{7,11},{8,4},{9,5},... | collective-permute-start | bytes 196616 | tf_op jit(solution)/shard_map/ppermute | solution.py:435
  63.9 15.5 %collective-permute-start.28 = (bf16[1408,128]{1,0:T(8,128)(2,1)S(1)}, bf16[1408,128]{1,0:T(8,128)(2,1)S(1)}, u32[]{:S(2)}, u32[]{:S(2)}) collective-permute-start(bf16[1408,128]{1,0:T(8,128)(2,1)S(1)} %get-tuple-element.67), channel_id=1, source_target_pairs={{0,1},{1,0},{2,3},{3,2},{4,5},{5,4},{6,7},{7,6},{8,9},{9,8},{10,11... | collective-permute-start | bytes 1081352 | tf_op jit(solution)/shard_map/ppermute | solution.py:435
  64.5 14.9 %collective-permute-start.29 = (bf16[1408,128]{1,0:T(8,128)(2,1)S(1)}, bf16[1408,128]{1,0:T(8,128)(2,1)S(1)}, u32[]{:S(2)}, u32[]{:S(2)}) collective-permute-start(bf16[1408,128]{1,0:T(8,128)(2,1)S(1)} %get-tuple-element.68), channel_id=1, source_target_pairs={{0,2},{1,3},{2,0},{3,1},{4,6},{5,7},{6,4},{7,5},{8,10},{9,11},{10,... | collective-permute-start | bytes 1081352 | tf_op jit(solution)/shard_map/ppermute | solution.py:435
  65.8 15.1 %collective-permute-start.30 = (bf16[1408,128]{1,0:T(8,128)(2,1)S(1)}, bf16[1408,128]{1,0:T(8,128)(2,1)S(1)}, u32[]{:S(2)}, u32[]{:S(2)}) collective-permute-start(bf16[1408,128]{1,0:T(8,128)(2,1)S(1)} %get-tuple-element.69), channel_id=1, source_target_pairs={{0,3},{1,2},{2,1},{3,0},{4,7},{5,6},{6,5},{7,4},{8,11},{9,10},{10,... | collective-permute-start | bytes 1081352 | tf_op jit(solution)/shard_map/ppermute | solution.py:435
  67.4 5.5 %collective-permute-start.31 = (bf16[384,128]{1,0:T(8,128)(2,1)S(1)}, bf16[384,128]{1,0:T(8,128)(2,1)S(1)}, u32[]{:S(2)}, u32[]{:S(2)}) collective-permute-start(bf16[384,128]{1,0:T(8,128)(2,1)S(1)} %get-tuple-element.71), channel_id=1, source_target_pairs={{0,4},{1,5},{2,6},{3,7},{4,0},{5,1},{6,2},{7,3},{8,12},{9,13},{10,... | collective-permute-start | bytes 294920 | tf_op jit(solution)/shard_map/ppermute | solution.py:435
  68.8 8.6 %collective-permute-start.32 = (bf16[384,128]{1,0:T(8,128)(2,1)S(1)}, bf16[384,128]{1,0:T(8,128)(2,1)S(1)}, u32[]{:S(2)}, u32[]{:S(2)}) collective-permute-start(bf16[384,128]{1,0:T(8,128)(2,1)S(1)} %get-tuple-element.72), channel_id=1, source_target_pairs={{0,8},{1,9},{2,10},{3,11},{4,12},{5,13},{6,14},{7,15},{8,0},{9,1},... | collective-permute-start | bytes 294920 | tf_op jit(solution)/shard_map/ppermute | solution.py:435
  72.9 6.5 %collective-permute-start.33 = (bf16[384,128]{1,0:T(8,128)(2,1)S(1)}, bf16[384,128]{1,0:T(8,128)(2,1)S(1)}, u32[]{:S(2)}, u32[]{:S(2)}) collective-permute-start(bf16[384,128]{1,0:T(8,128)(2,1)S(1)} %get-tuple-element.73), channel_id=1, source_target_pairs={{0,12},{1,13},{2,14},{3,15},{4,8},{5,9},{6,10},{7,11},{8,4},{9,5},... | collective-permute-start | bytes 294920 | tf_op jit(solution)/shard_map/ppermute | solution.py:435
